TPU v7x, 256 devices: a whole 4x4x8 slice. The times are simulated.
256 devices in a mesh: dp: 8 (over z_hi, core), mp: 32 (over x, y, z_lo).
Axes of the slice: x: 4, y: 4, z: 8 (z_hi: 4, z_lo: 2; z = z_hi * 2 + z_lo), core: 2. Of those that a mesh axis runs over, the one named last changes fastest.
Arguments:
- tokens: bfloat16 [1024, 8192], P(('dp', 'mp')), may hold values from -6 to 6
- gate_weight: bfloat16 [8192, 26624], P('dp', 'mp'), may hold values from -0.0625 to 0.0625
- up_weight: bfloat16 [8192, 26624], P('dp', 'mp'), may hold values from -0.0625 to 0.0625
- down_weight: bfloat16 [26624, 8192], P('mp', 'dp'), may hold values from -0.0390625 to 0.0390625
- grad_mixed: bfloat16 [1024, 8192], P(('dp', 'mp')), may hold values from -6 to 6
- amax_history: float32 [26624], P('mp'), may hold values from 1 to 4
Outputs:
- grad_tokens: bfloat16 [1024, 8192], P(('dp', 'mp'))
- grad_gate: bfloat16 [8192, 26624], P('dp', 'mp')
- grad_up: bfloat16 [8192, 26624], P('dp', 'mp')
- grad_down: bfloat16 [26624, 8192], P('mp', 'dp')
- amax: float32 [26624], P('mp')
All inputs are finite; a program needn't handle non-finite values.
Results may differ from a plain program's by a relative error of at most 0.0049.
Values may be sent and summed in bfloat16 or wider, within the bound.
No kernel may reach another device: no remote copies, remote signals or barrier semaphores. Data moves between devices by JAX's collectives and lax.ppermute only.
A program may use at most 128 MiB of HBM per device.

v0:
```python
import jax
import jax.numpy as jnp
from jax import lax
from jax.experimental import pallas as pl
from jax.experimental.pallas import tpu as pltpu
from jax.sharding import Mesh, PartitionSpec as P

NZ, NC, NX, NY, NL = 4, 2, 4, 4, 2
AXES = ("z", "c", "x", "y", "l")
MP = ("x", "y", "l")
BF = jnp.bfloat16
F32 = jnp.float32


def shift(value, axis, k):
    n = {"z": NZ, "c": NC, "l": NL}[axis]
    return lax.ppermute(value, axis, [(i, (i + k) % n) for i in range(n)])


def swap(value):
    return shift(value, "c", 1)


def dot(left, right):
    return jnp.dot(left, right, preferred_element_type=F32)


def exchange(value, axis):
    return lax.all_to_all(value, axis, split_axis=0, concat_axis=0, tiled=True)


VMEM_BYTES = 48 * 2**20


def params():
    return pltpu.CompilerParams(vmem_limit_bytes=VMEM_BYTES)


def dot_nt(left, right):
    return lax.dot_general(left, right, (((1,), (1,)), ((), ())), preferred_element_type=F32)


def project(zi, pairs, own, other, ties=()):
    n = len(own)
    peers, few, width = pairs.shape
    rows = peers * few // 2
    units = own[0].shape[0]
    steps, group = 4, rows // NZ
    tile = width // steps

    def kernel(z_ref, t_ref, g_ref, *refs):
        own_refs, other_refs = refs[:n], refs[n : 2 * n]
        refs = refs[2 * n + len(ties) :]
        out, sends, totals = refs[0], refs[1:NZ], refs[NZ:]
        step = pl.program_id(0)
        columns = [t_ref[...].reshape(rows, tile)] * 2 + [g_ref[...].reshape(rows, tile)]

        @pl.when(step == 0)
        def _():
            for total, c, w in zip(totals, columns, own_refs):
                total[...] = dot_nt(c, w[...])

        @pl.when((step > 0) & (step < steps // 2))
        def _():
            for total, c, w in zip(totals, columns, own_refs):
                total[...] += dot_nt(c, w[...])

        @pl.when(step >= steps // 2)
        def _():
            for total, c, w in zip(totals, columns, other_refs):
                total[...] += dot_nt(c, w[...])

        @pl.when(step == steps - 1)
        def _():
            for k in range(NZ):
                start = pl.multiple_of(lax.rem(z_ref[0] + k, NZ) * group, group)
                value = jnp.concatenate([total[pl.ds(start, group), :] for total in totals], axis=1)
                if k == 0:
                    out[...] = value
                else:
                    sends[k - 1][...] = value.astype(BF)

    half = steps // 2
    whole = pl.BlockSpec((group, n * units), lambda i, z: (0, 0))
    return pl.pallas_call(
        kernel,
        grid_spec=pltpu.PrefetchScalarGridSpec(
            num_scalar_prefetch=1,
            grid=(steps,),
            in_specs=[
                pl.BlockSpec((peers, few // 2, tile), lambda i, z: (0, 0, i)),
                pl.BlockSpec((peers, few // 2, tile), lambda i, z: (0, 1, i)),
            ]
            + [pl.BlockSpec((units, tile), lambda i, z: (0, jnp.minimum(i, half - 1)))] * n
            + [pl.BlockSpec((units, tile), lambda i, z: (0, jnp.maximum(i - half, 0)))] * n
            + [pl.BlockSpec(memory_space=pl.ANY)] * len(ties),
            out_specs=[whole] * NZ,
            scratch_shapes=[pltpu.VMEM((rows, units), F32)] * n,
        ),
        out_shape=[jax.ShapeDtypeStruct((group, n * units), F32)]
        + [jax.ShapeDtypeStruct((group, n * units), BF)] * (NZ - 1),
        compiler_params=params(),
        cost_estimate=pl.CostEstimate(
            flops=2 * rows * width * units * n,
            bytes_accessed=2 * (2 * rows * width + width * units * n) + 10 * group * n * units,
            transcendentals=0,
        ),
    )(zi, pairs, pairs, *own, *other, *ties)


def activations(parts, bound):
    rows, units = parts[0].shape[0], bound.shape[1]
    steps = 2
    tile = rows // steps

    def kernel(*refs):
        bound_ref, acts_ref, hidden_ref, amax_ref = refs[NZ:]
        total = refs[0][...]
        for ref in refs[1:NZ]:
            total = total + ref[...].astype(F32)
        gate, up, grad = (total[:, i * units : (i + 1) * units] for i in range(3))
        limit = bound_ref[...]
        sig = jax.nn.sigmoid(gate)
        act = gate * sig
        raw = act * up
        top = jnp.max(jnp.abs(raw), axis=0, keepdims=True)
        step = pl.program_id(0)

        @pl.when(step == 0)
        def _():
            amax_ref[...] = top

        @pl.when(step > 0)
        def _():
            amax_ref[...] = jnp.maximum(amax_ref[...], top)

        squash = jnp.tanh(raw / limit)
        masked = grad * (1.0 - squash * squash)
        hidden_ref[...] = (limit * squash).astype(BF)
        gate_act = masked * up * sig * (1.0 + gate * (1.0 - sig))
        acts_ref[...] = jnp.concatenate([gate_act, masked * act], axis=1).astype(BF)

    wide = pl.BlockSpec((tile, 2 * units), lambda i: (i, 0))
    narrow = pl.BlockSpec((tile, units), lambda i: (i, 0))
    line = pl.BlockSpec((1, units), lambda i: (0, 0))
    return pl.pallas_call(
        kernel,
        grid=(steps,),
        in_specs=[pl.BlockSpec((tile, 3 * units), lambda i: (i, 0))] * NZ + [line],
        out_specs=[wide, narrow, line],
        out_shape=[
            jax.ShapeDtypeStruct((rows, 2 * units), BF),
            jax.ShapeDtypeStruct((rows, units), BF),
            jax.ShapeDtypeStruct((1, units), F32),
        ],
        compiler_params=params(),
        cost_estimate=pl.CostEstimate(
            flops=40 * rows * units, bytes_accessed=34 * rows * units, transcendentals=2 * rows * units
        ),
    )(*parts, bound)


def input_terms(zi, pieces, own, other, ties=()):
    group, both = pieces[0].shape
    units, depth = own[0].shape
    steps = 4
    tile = 2 * depth // steps
    half = steps // 2
    rows = NZ * group

    def kernel(z_ref, *refs):
        p_refs, w_refs = refs[:NZ], refs[NZ : NZ + 4]
        out_ref, all_ref, stacked = refs[NZ + 4 + len(ties) :]
        step = pl.program_id(0)

        @pl.when(step == 0)
        def _():
            for j in range(NZ):
                start = pl.multiple_of(lax.rem(z_ref[0] + j, NZ) * group, group)
                all_ref[pl.ds(start, group), :] = p_refs[j][...]

        @pl.when(step < half)
        def _():
            stacked[:units, :] = w_refs[0][...]
            stacked[units:, :] = w_refs[1][...]

        @pl.when(step >= half)
        def _():
            stacked[:units, :] = w_refs[2][...]
            stacked[units:, :] = w_refs[3][...]

        out_ref[...] = dot(all_ref[...], stacked[...]).astype(BF)

    return pl.pallas_call(
        kernel,
        grid_spec=pltpu.PrefetchScalarGridSpec(
            num_scalar_prefetch=1,
            grid=(steps,),
            in_specs=[pl.BlockSpec((group, both), lambda i, z: (0, 0))] * NZ
            + [pl.BlockSpec((units, tile), lambda i, z: (0, jnp.minimum(i, half - 1)))] * 2
            + [pl.BlockSpec((units, tile), lambda i, z: (0, jnp.maximum(i - half, 0)))] * 2
            + [pl.BlockSpec(memory_space=pl.ANY)] * len(ties),
            out_specs=[
                pl.BlockSpec((rows, tile), lambda i, z: (0, i)),
                pl.BlockSpec((rows, both), lambda i, z: (0, 0)),
            ],
            scratch_shapes=[pltpu.VMEM((both, tile), BF)],
        ),
        out_shape=[
            jax.ShapeDtypeStruct((rows, 2 * depth), BF),
            jax.ShapeDtypeStruct((rows, both), BF),
        ],
        compiler_params=params(),
        cost_estimate=pl.CostEstimate(
            flops=4 * rows * both * depth,
            bytes_accessed=4 * rows * both + 4 * rows * depth + 4 * both * depth,
            transcendentals=0,
        ),
    )(zi, *pieces, *own, *other, *ties)


def repeated(shard, peers, ties=()):
    rows, width = shard.shape
    steps = 4

    def kernel(s_ref, *refs):
        refs[-1][...] = jnp.broadcast_to(s_ref[...][None], refs[-1].shape)

    return pl.pallas_call(
        kernel,
        grid=(steps,),
        in_specs=[pl.BlockSpec((rows, width), lambda i: (0, 0))]
        + [pl.BlockSpec(memory_space=pl.ANY)] * len(ties),
        out_specs=pl.BlockSpec((peers // steps, rows, width), lambda i: (i, 0, 0)),
        out_shape=jax.ShapeDtypeStruct((peers, rows, width), shard.dtype),
        cost_estimate=pl.CostEstimate(flops=0, bytes_accessed=2 * peers * rows * width, transcendentals=0),
    )(shard, *ties)


def summed(pieces, ties=()):
    peers, rows, width = pieces.shape
    steps = 4
    tile = width // steps

    def kernel(p_ref, *refs):
        refs[-1][...] = jnp.sum(p_ref[...].astype(F32), axis=0)

    return pl.pallas_call(
        kernel,
        grid=(steps,),
        in_specs=[pl.BlockSpec((peers, rows, tile), lambda i: (0, 0, i))]
        + [pl.BlockSpec(memory_space=pl.ANY)] * len(ties),
        out_specs=pl.BlockSpec((rows, tile), lambda i: (0, i)),
        out_shape=jax.ShapeDtypeStruct((rows, width), F32),
        cost_estimate=pl.CostEstimate(
            flops=peers * rows * width, bytes_accessed=2 * peers * rows * width, transcendentals=0
        ),
    )(pieces, *ties)


def hidden_message(first, second, tops, ties=()):
    rows, units = first.shape

    def kernel(a_ref, b_ref, s_ref, t_ref, *refs):
        out_ref = refs[-1]
        out_ref[:rows, :] = a_ref[...]
        out_ref[rows : 2 * rows, :] = b_ref[...]
        rest = jnp.maximum(s_ref[...], t_ref[...])
        addends = []
        for _ in range(3):
            addends.append(rest.astype(BF).astype(F32))
            rest = rest - addends[-1]
        line = lax.broadcasted_iota(jnp.int32, (16, units), 0)
        tail = jnp.zeros((16, units), F32)
        for i, addend in enumerate(addends):
            tail = jnp.where(line == i, addend, tail)
        out_ref[2 * rows :, :] = tail.astype(BF)

    whole = pl.BlockSpec((rows, units), lambda: (0, 0))
    one = pl.BlockSpec((1, units), lambda: (0, 0))
    return pl.pallas_call(
        kernel,
        in_specs=[whole, whole, one, one] + [pl.BlockSpec(memory_space=pl.ANY)] * len(ties),
        out_specs=pl.BlockSpec((2 * rows + 16, units), lambda: (0, 0)),
        out_shape=jax.ShapeDtypeStruct((2 * rows + 16, units), BF),
        cost_estimate=pl.CostEstimate(flops=0, bytes_accessed=8 * rows * units, transcendentals=0),
    )(first, second, *tops, *ties)


def hidden_by_z(zi, pieces, ties=()):
    units = pieces[0].shape[1]
    rows = (pieces[0].shape[0] - 16) // 2
    wide = -(-units // 128) * 128

    def kernel(z_ref, *refs):
        out_ref, top_ref = refs[-2:]
        if wide > units:
            out_ref[:, units:] = jnp.zeros((2 * NZ * rows, wide - units), BF)
        top = None
        for j in range(NZ):
            owner = lax.rem(z_ref[0] + j, NZ)
            for chunk in range(2):
                start = pl.multiple_of(chunk * NZ * rows + owner * rows, rows)
                out_ref[pl.ds(start, rows), :units] = refs[j][chunk * rows : (chunk + 1) * rows, :]
            tail = refs[j][2 * rows :, :].astype(F32)
            value = (tail[0:1] + tail[1:2]) + tail[2:3]
            top = value if top is None else jnp.maximum(top, value)
        top_ref[...] = top

    whole = pl.BlockSpec((2 * rows + 16, units), lambda i, z: (0, 0))
    return pl.pallas_call(
        kernel,
        grid_spec=pltpu.PrefetchScalarGridSpec(
            num_scalar_prefetch=1,
            grid=(1,),
            in_specs=[whole] * NZ + [pl.BlockSpec(memory_space=pl.ANY)] * len(ties),
            out_specs=[
                pl.BlockSpec((2 * NZ * rows, wide), lambda i, z: (0, 0)),
                pl.BlockSpec((1, units), lambda i, z: (0, 0)),
            ],
        ),
        out_shape=[
            jax.ShapeDtypeStruct((2 * NZ * rows, wide), BF),
            jax.ShapeDtypeStruct((1, units), F32),
        ],
        cost_estimate=pl.CostEstimate(flops=0, bytes_accessed=32 * rows * units, transcendentals=0),
    )(zi, *pieces, *ties)


def weight_gradients(terms, outs, units, depth):
    peers, few, _ = terms[0][2].shape
    rows = peers * few // 2
    wide = terms[0][0].shape[1]
    steps = 4
    tile = depth // steps
    n = len(terms)

    def kernel(*refs):
        lefts, rights, results, turned = refs[:n], refs[n : 2 * n], refs[2 * n : 2 * n + outs], refs[-1]

        @pl.when(pl.program_id(0) == 0)
        def _():
            for i in range(n):
                turned[:, i * rows : (i + 1) * rows] = lefts[i][...].T

        right = jnp.concatenate([r[...].reshape(rows, tile) for r in rights], axis=0)
        for o in range(outs):
            results[o][...] = dot(turned[o * units : (o + 1) * units, :], right).astype(BF)

    def left_spec(block):
        return pl.BlockSpec((rows, wide), lambda i: (block, 0))

    def right_spec(which, half):
        return pl.BlockSpec((peers, few // 2, tile), lambda i: (0, which, half * steps + i))

    return pl.pallas_call(
        kernel,
        grid=(steps,),
        in_specs=[left_spec(t[1]) for t in terms] + [right_spec(t[3], t[4]) for t in terms],
        out_specs=[pl.BlockSpec((units, tile), lambda i: (0, i))] * outs,
        out_shape=[jax.ShapeDtypeStruct((units, depth), BF)] * outs,
        scratch_shapes=[pltpu.VMEM((wide, n * rows), BF)],
        compiler_params=params(),
        cost_estimate=pl.CostEstimate(
            flops=2 * n * rows * wide * depth,
            bytes_accessed=2 * (n * rows * (wide + depth) + wide * depth),
            transcendentals=0,
        ),
    )(*[t[0] for t in terms], *[t[2] for t in terms])


def sum_parts(pieces):
    got = {k: shift(pieces[k], "z", k) for k in (2, 1, 3)}
    return [pieces[0]] + [got[k] for k in (1, 2, 3)]


def gather_parts(share):
    got = {j: shift(share, "z", -j) for j in (2, 1, 3)}
    return [share] + [got[j] for j in (1, 2, 3)]


def per_device(tokens, gate_weight, up_weight, down_weight, grad_mixed, amax_history):
    zi = lax.axis_index("z")
    ci = lax.axis_index("c")
    zs = zi.astype(jnp.int32).reshape((1,))
    own_rows, width = tokens.shape
    block = width // NZ
    half = block // NC
    few = NZ * NL * own_rows
    peers = NX * NY
    chunk = few // 2

    gate_t, up_t = gate_weight.T, up_weight.T
    gate_other = swap(gate_t)
    up_other = swap(up_t)
    down_other = swap(down_weight)

    def own_first(value):
        return jnp.where(ci == 0, value, jnp.concatenate([value[..., half:], value[..., :half]], axis=-1))

    both = jnp.concatenate([tokens, grad_mixed], axis=0).reshape(2 * own_rows, NZ, 1, block)
    both = jnp.broadcast_to(both.transpose(1, 2, 0, 3), (NZ, NL, 2 * own_rows, block))
    placed = own_first(exchange(both.reshape(NZ * NL, 2 * own_rows, block), ("z", "l")))
    parts = placed.reshape(2, few // 2 // own_rows, 2, own_rows, block).transpose(0, 2, 1, 3, 4)
    parts = parts.reshape(2, few, block)

    own, other = [gate_t, up_t, down_weight], [gate_other, up_other, down_other]
    bound = amax_history[None, :]

    pairs_a = exchange(repeated(parts[0], peers), ("x", "y"))
    pairs_b = exchange(repeated(parts[1], peers), ("x", "y"))
    part_a = project(zs, pairs_a, own, other)
    part_b = project(zs, pairs_b, own, other)
    acts_a, hidden_a, amax_a = activations(sum_parts(part_a), bound)
    acts_b, hidden_b, amax_b = activations(sum_parts(part_b), bound)
    terms_a, acts_all_a = input_terms(zs, gather_parts(acts_a), own[:2], other[:2], (acts_b,))
    terms_b, acts_all_b = input_terms(zs, gather_parts(acts_b), own[:2], other[:2])

    sums_a = exchange(terms_a.reshape(peers, chunk, block), ("x", "y"))
    sums_b = exchange(terms_b.reshape(peers, chunk, block), ("x", "y"))

    units = gate_t.shape[0]
    message = hidden_message(hidden_a, hidden_b, (amax_a, amax_b), (terms_b,))
    other_a, other_b = swap(pairs_a), swap(pairs_b)
    grad_gate, grad_up = weight_gradients(
        [
            (acts_all_a, 0, pairs_a, 0, 0),
            (acts_all_b, 0, pairs_b, 0, 0),
            (swap(acts_all_a), 0, other_a, 0, 1),
            (swap(acts_all_b), 0, other_b, 0, 1),
        ],
        2,
        units,
        half,
    )
    hidden_all, amax = hidden_by_z(zs, gather_parts(message), (grad_gate,))
    amax = jnp.maximum(amax, swap(amax))[0]
    hidden_other = swap(hidden_all)
    (grad_down,) = weight_gradients(
        [
            (hidden_all, 0, pairs_a, 1, 0),
            (hidden_all, 1, pairs_b, 1, 0),
            (hidden_other, 0, other_a, 1, 1),
            (hidden_other, 1, other_b, 1, 1),
        ],
        1,
        units,
        half,
    )

    mine = [summed(sums_a), summed(sums_b, (grad_gate, hidden_all))]
    back = exchange(jnp.concatenate(mine, axis=0).reshape(NZ * NL, own_rows, block), ("z", "l"))
    back = own_first(jnp.sum(back.reshape(NZ, NL, own_rows, block), axis=1).astype(BF))
    grad_tokens = back.transpose(1, 0, 2).reshape(own_rows, width)
    return (grad_tokens, grad_gate.T, grad_up.T, grad_down, amax)


def solution(mesh):
    split = Mesh(mesh.devices.reshape(NZ, NC, NX, NY, NL), AXES)
    rows, units = ("z", "c"), MP
    return jax.shard_map(
        per_device,
        mesh=split,
        in_specs=(
            P(AXES, None),
            P(rows, units),
            P(rows, units),
            P(units, rows),
            P(AXES, None),
            P(units),
        ),
        out_specs=(P(AXES, None), P(rows, units), P(rows, units), P(units, rows), P(units)),
        check_vma=False,
    )
```

profile of v0, /device:TPU:2, one launch (start us, length us, event | category | flops | bytes accessed | tf_op | source)
XLA Modules:
  0.0 275.5 jit_solution(4835181097139203455)
XLA Ops:
  2.3 8.5 %all-to-all-start = ((bf16[8,8,2048]{2,1,0:T(8,128)(2,1)}), bf16[8,8,2048]{2,1,0:T(8,128)(2,1)S(1)}, u32[]{:S(2)}, u32[]{:S(2)}) async-start(bf16[8,8,2048]{2,1,0:T(8,128)(2,1)} %bitcast.4), calls=%async_computation | async-start | bytes 524288 | tf_op jit(solution)/shard_map/all_to_all | solution.py:29
  10.8 11.9 %all-to-all-done = bf16[8,8,2048]{2,1,0:T(8,128)(2,1)S(1)} async-done(((bf16[8,8,2048]{2,1,0:T(8,128)(2,1)}), bf16[8,8,2048]{2,1,0:T(8,128)(2,1)S(1)}, u32[]{:S(2)}, u32[]{:S(2)}) %all-to-all-start) | async-done | bytes 262176 | tf_op jit(solution)/shard_map/all_to_all | solution.py:29
  23.7 2.8 %shard_map.101 = bf16[16,32,2048]{2,1,0:T(8,128)(2,1)} custom-call(bf16[32,2048]{1,0:T(8,128)(2,1)} %squeeze.9.s_ref), custom_call_target="tpu_custom_call" | custom-call | bytes 2097152 | tf_op jit(solution)/shard_map/pallas_call | solution.py:229
  26.5 7.5 %all-to-all-start.1 = ((bf16[16,32,2048]{2,1,0:T(8,128)(2,1)}), bf16[16,32,2048]{2,1,0:T(8,128)(2,1)S(1)}, u32[]{:S(2)}, u32[]{:S(2)}) async-start(bf16[16,32,2048]{2,1,0:T(8,128)(2,1)} %shard_map.101), calls=%async_computation.1 | async-start | bytes 4194304 | tf_op jit(solution)/shard_map/all_to_all | solution.py:29
  35.3 2.8 %shard_map.104 = bf16[16,32,2048]{2,1,0:T(8,128)(2,1)} custom-call(bf16[32,2048]{1,0:T(8,128)(2,1)} %squeeze.10.s_ref), custom_call_target="tpu_custom_call" | custom-call | bytes 2097152 | tf_op jit(solution)/shard_map/pallas_call | solution.py:229
  38.1 21.3 %all-to-all-done.1.t_ref.g_ref.refs_4_ = bf16[16,32,2048]{2,1,0:T(8,128)(2,1)S(1)} async-done(((bf16[16,32,2048]{2,1,0:T(8,128)(2,1)}), bf16[16,32,2048]{2,1,0:T(8,128)(2,1)S(1)}, u32[]{:S(2)}, u32[]{:S(2)}) %all-to-all-start.1) | async-done | bytes 2097184 | tf_op jit(solution)/shard_map/all_to_all | solution.py:29
  60.8 6.8 %all-to-all-start.2 = ((bf16[16,32,2048]{2,1,0:T(8,128)(2,1)}), bf16[16,32,2048]{2,1,0:T(8,128)(2,1)}, u32[]{:S(2)}, u32[]{:S(2)}) async-start(bf16[16,32,2048]{2,1,0:T(8,128)(2,1)} %shard_map.104), calls=%async_computation.2 | async-start | bytes 4194304 | tf_op jit(solution)/shard_map/all_to_all | solution.py:29
  70.5 8.5 %shard_map.102 = (f32[64,2496]{1,0:T(8,128)S(1)}, bf16[64,2496]{1,0:T(8,128)(2,1)}, bf16[64,2496]{1,0:T(8,128)(2,1)}, bf16[64,2496]{1,0:T(8,128)(2,1)}) custom-call(s32[1]{0:T(128)} %bitcast.z_ref, bf16[16,32,2048]{2,1,0:T(8,128)(2,1)} %copy-done, bf16[16,32,2048]{2,1,0:T(8,128)(2,1)} %copy-done, bf16[832,1024]{1,0:T(8,128)(2,1)S(1)} %bitcast.20, ...), custom_call_target="tpu_custom_call" | custom-call | flops 2617245696 | bytes 13918208 | tf_op jit(solution)/shard_map/pallas_call | solution.py:85
  79.0 4.2 %collective-permute-start.4 = (bf16[64,2496]{1,0:T(8,128)(2,1)}, bf16[64,2496]{1,0:T(8,128)(2,1)S(1)}, u32[]{:S(2)}, u32[]{:S(2)}) collective-permute-start(bf16[64,2496]{1,0:T(8,128)(2,1)} %get-tuple-element.29), channel_id=1, source_target_pairs={{0,128},{64,192},{128,0},{192,64},{1,129},{65,193},{129,1},{193,65... | collective-permute-start | bytes 958472 | tf_op jit(solution)/shard_map/ppermute | solution.py:17
  85.0 7.6 %all-to-all-done.2.t_ref.g_ref.refs_5_ = bf16[16,32,2048]{2,1,0:T(8,128)(2,1)} async-done(((bf16[16,32,2048]{2,1,0:T(8,128)(2,1)}), bf16[16,32,2048]{2,1,0:T(8,128)(2,1)}, u32[]{:S(2)}, u32[]{:S(2)}) %all-to-all-start.2) | async-done | bytes 2097184 | tf_op jit(solution)/shard_map/all_to_all | solution.py:29
  95.4 7.5 %shard_map.105 = (f32[64,2496]{1,0:T(8,128)S(1)}, bf16[64,2496]{1,0:T(8,128)(2,1)S(1)}, bf16[64,2496]{1,0:T(8,128)(2,1)S(1)}, bf16[64,2496]{1,0:T(8,128)(2,1)S(1)}) custom-call(s32[1]{0:T(128)} %bitcast.z_ref, bf16[16,32,2048]{2,1,0:T(8,128)(2,1)} %all-to-all-done.2.t_ref.g_ref.refs_5_, bf16[16,32,2048]{2,1,0:T(8,128)(2,1)} %all-to-all-done.2.t_ref.g_ref.refs_5_, ...), custom_call_target="tpu_custom_call" | custom-call | flops 2617245696 | bytes 13918208 | tf_op jit(solution)/shard_map/pallas_call | solution.py:85
  103.1 4.2 %collective-permute-start.10 = (bf16[64,2496]{1,0:T(8,128)(2,1)S(1)}, bf16[64,2496]{1,0:T(8,128)(2,1)S(1)}, u32[]{:S(2)}, u32[]{:S(2)}) collective-permute-start(bf16[64,2496]{1,0:T(8,128)(2,1)S(1)} %get-tuple-element.34), channel_id=1, source_target_pairs={{0,128},{64,192},{128,0},{192,64},{1,129},{65,193},{129,1},{193,65... | collective-permute-start | bytes 958472 | tf_op jit(solution)/shard_map/ppermute | solution.py:17
  110.4 5.1 %collective-permute-done.5.refs_3_ = bf16[64,2496]{1,0:T(8,128)(2,1)} collective-permute-done((bf16[64,2496]{1,0:T(8,128)(2,1)}, bf16[64,2496]{1,0:T(8,128)(2,1)}, u32[]{:S(2)}, u32[]{:S(2)}) %collective-permute-start.5) | collective-permute-done | bytes 319520 | tf_op jit(solution)/shard_map/ppermute | solution.py:17
  118.7 14.2 %collective-permute-done.10.refs_2_ = bf16[64,2496]{1,0:T(8,128)(2,1)S(1)} collective-permute-done((bf16[64,2496]{1,0:T(8,128)(2,1)S(1)}, bf16[64,2496]{1,0:T(8,128)(2,1)S(1)}, u32[]{:S(2)}, u32[]{:S(2)}) %collective-permute-start.10) | collective-permute-done | bytes 319520 | tf_op jit(solution)/shard_map/ppermute | solution.py:17
  136.9 8.8 %collective-permute-done.7.refs_2_ = bf16[64,1664]{1,0:T(8,128)(2,1)S(1)} collective-permute-done((bf16[64,1664]{1,0:T(8,128)(2,1)S(1)}, bf16[64,1664]{1,0:T(8,128)(2,1)S(1)}, u32[]{:S(2)}, u32[]{:S(2)}) %collective-permute-start.7) | collective-permute-done | bytes 213024 | tf_op jit(solution)/shard_map/ppermute | solution.py:17
  145.7 6.3 %shard_map.107 = (bf16[256,2048]{1,0:T(8,128)(2,1)}, bf16[256,1664]{1,0:T(8,128)(2,1)S(1)}) custom-call(s32[1]{0:T(128)} %bitcast.z_ref, bf16[64,1664]{1,0:T(8,128)(2,1)S(1)} %get-tuple-element.31.refs_0_, bf16[64,1664]{1,0:T(8,128)(2,1)S(1)} %collective-permute-done.6.refs_1_, bf16[64,1664]{1,0:T(8,128)(2,1)S(1)} %collective-permute-done.7.refs_2_, ...), custom_call_target="tpu_custom_call" | custom-call | flops 1744830464 | bytes 9568256 | tf_op jit(solution)/shard_map/pallas_call | solution.py:194
  152.0 18.5 %all-to-all-start.3 = ((bf16[16,16,2048]{2,1,0:T(8,128)(2,1)}), bf16[16,16,2048]{2,1,0:T(8,128)(2,1)}, u32[]{:S(2)}, u32[]{:S(2)}) async-start(bf16[16,16,2048]{2,1,0:T(8,128)(2,1)} %bitcast.8), calls=%async_computation.3 | async-start | bytes 2097152 | tf_op jit(solution)/shard_map/all_to_all | solution.py:29
  170.5 2.6 collective-permute-start.14
  173.2 2.5 collective-permute-start.13
  176.8 5.3 %collective-permute-done.14.refs_3_ = bf16[64,1664]{1,0:T(8,128)(2,1)S(1)} collective-permute-done((bf16[64,1664]{1,0:T(8,128)(2,1)S(1)}, bf16[64,1664]{1,0:T(8,128)(2,1)S(1)}, u32[]{:S(2)}, u32[]{:S(2)}) %collective-permute-start.14) | collective-permute-done | bytes 213024 | tf_op jit(solution)/shard_map/ppermute | solution.py:17
  182.2 7.7 %collective-permute-done.13.refs_2_ = bf16[64,1664]{1,0:T(8,128)(2,1)S(1)} collective-permute-done((bf16[64,1664]{1,0:T(8,128)(2,1)S(1)}, bf16[64,1664]{1,0:T(8,128)(2,1)S(1)}, u32[]{:S(2)}, u32[]{:S(2)}) %collective-permute-start.13) | collective-permute-done | bytes 213024 | tf_op jit(solution)/shard_map/ppermute | solution.py:17
  192.8 6.1 %shard_map.109 = (bf16[256,2048]{1,0:T(8,128)(2,1)}, bf16[256,1664]{1,0:T(8,128)(2,1)}) custom-call(s32[1]{0:T(128)} %bitcast.z_ref, bf16[64,1664]{1,0:T(8,128)(2,1)S(1)} %get-tuple-element.36.refs_8_.refs_0_, bf16[64,1664]{1,0:T(8,128)(2,1)S(1)} %collective-permute-done.12.refs_1_, bf16[64,1664]{1,0:T(8,128)(2,1)S(1)} %collective-permute-done.13.refs_2_, ...), custom_call_target="tpu_custom_call" | custom-call | flops 1744830464 | bytes 9568256 | tf_op jit(solution)/shard_map/pallas_call | solution.py:194
  199.5 7.2 %all-to-all-start.4 = ((bf16[16,16,2048]{2,1,0:T(8,128)(2,1)}), bf16[16,16,2048]{2,1,0:T(8,128)(2,1)}, u32[]{:S(2)}, u32[]{:S(2)}) async-start(bf16[16,16,2048]{2,1,0:T(8,128)(2,1)} %bitcast.9), calls=%async_computation.4 | async-start | bytes 2097152 | tf_op jit(solution)/shard_map/all_to_all | solution.py:29
  208.4 3.2 %shard_map.108 = f32[16,2048]{1,0:T(8,128)} custom-call(bf16[16,16,2048]{2,1,0:T(8,128)(2,1)} %all-to-all-done.3.p_ref), custom_call_target="tpu_custom_call" | custom-call | flops 524288 | bytes 1048576 | tf_op jit(solution)/shard_map/pallas_call | solution.py:248
  211.6 3.3 %collective-permute-start.20 = (bf16[144,832]{1,0:T(8,128)(2,1)}, bf16[144,832]{1,0:T(8,128)(2,1)S(1)}, u32[]{:S(2)}, u32[]{:S(2)}) collective-permute-start(bf16[144,832]{1,0:T(8,128)(2,1)} %shard_map.111.refs_0_), channel_id=1, source_target_pairs={{0,128},{64,192},{128,0},{192,64},{1,129},{65,193},{129,1},{193,65... | collective-permute-start | bytes 718856 | tf_op jit(solution)/shard_map/ppermute | solution.py:17
  214.9 4.1 %collective-permute-start.19 = (bf16[144,832]{1,0:T(8,128)(2,1)}, bf16[144,832]{1,0:T(8,128)(2,1)}, u32[]{:S(2)}, u32[]{:S(2)}) collective-permute-start(bf16[144,832]{1,0:T(8,128)(2,1)} %shard_map.111.refs_0_), channel_id=1, source_target_pairs={{0,192},{64,0},{128,64},{192,128},{1,193},{65,1},{129,65},{193,129... | collective-permute-start | bytes 718856 | tf_op jit(solution)/shard_map/ppermute | solution.py:17
  219.0 8.4 %shard_map.110 = (bf16[832,1024]{1,0:T(8,128)(2,1)}, bf16[832,1024]{1,0:T(8,128)(2,1)}) custom-call(bf16[256,1664]{1,0:T(8,128)(2,1)S(1)} %get-tuple-element.39.refs_0_, bf16[256,1664]{1,0:T(8,128)(2,1)} %get-tuple-element.40.refs_1_, bf16[256,1664]{1,0:T(8,128)(2,1)} %collective-permute-done.15.refs_2_, bf16[256,1664]{1,0:T(8,128)(2,1)} %collective-permute-done.16.refs_3_, ...), custom_call_target="tpu_custom_call" | custom-call | flops 3489660928 | bytes 8912896 | tf_op jit(solution)/shard_map/pallas_call | solution.py:356
  228.3 2.4 shard_map.112
  230.7 3.3 %shard_map.113 = f32[16,2048]{1,0:T(8,128)} custom-call(bf16[16,16,2048]{2,1,0:T(8,128)(2,1)} %all-to-all-done.4.p_ref, bf16[832,1024]{1,0:T(8,128)(2,1)} %get-tuple-element.41.refs_4_.refs_0_, bf16[512,896]{1,0:T(8,128)(2,1)} %get-tuple-element.46.refs_1_.refs_0_), custom_call_target="tpu_custom_call" | custom-call | flops 524288 | bytes 1048576 | tf_op jit(solution)/shard_map/pallas_call | solution.py:248
  235.7 22.3 %all-to-all-start.5 = ((f32[8,4,2048]{2,1,0:T(4,128)}), f32[8,4,2048]{2,1,0:T(4,128)S(1)}, u32[]{:S(2)}, u32[]{:S(2)}) async-start(f32[8,4,2048]{2,1,0:T(4,128)} %reshape.48), calls=%async_computation.5 | async-start | bytes 524288 | tf_op jit(solution)/shard_map/all_to_all | solution.py:29
  259.9 8.9 %all-to-all-done.5 = f32[8,4,2048]{2,1,0:T(4,128)S(1)} async-done(((f32[8,4,2048]{2,1,0:T(4,128)}), f32[8,4,2048]{2,1,0:T(4,128)S(1)}, u32[]{:S(2)}, u32[]{:S(2)}) %all-to-all-start.5) | async-done | bytes 262176 | tf_op jit(solution)/shard_map/all_to_all | solution.py:29
  269.6 5.9 %shard_map.114 = bf16[832,1024]{1,0:T(8,128)(2,1)} custom-call(bf16[512,896]{1,0:T(8,128)(2,1)S(1)} %copy-done.9, bf16[512,896]{1,0:T(8,128)(2,1)S(1)} %copy-done.9, bf16[512,896]{1,0:T(8,128)(2,1)} %collective-permute-done.22.refs_2_.refs_3_, bf16[512,896]{1,0:T(8,128)(2,1)} %collective-permute-done.22.refs_2_.refs_3_, bf16[16,32,2048]{2,1,0:T(8,128)(2,1)S(1)} %copy-done.1, ...), custom_call_target="tpu_custom_call" | custom-call | flops 1879048192 | bytes 5767168 | tf_op jit(solution)/shard_map/pallas_call | solution.py:356
  (97 shorter events, 34.7 us)
Async XLA Ops:
  2.3 20.3 %all-to-all-start = ((bf16[8,8,2048]{2,1,0:T(8,128)(2,1)}), bf16[8,8,2048]{2,1,0:T(8,128)(2,1)S(1)}, u32[]{:S(2)}, u32[]{:S(2)}) async-start(bf16[8,8,2048]{2,1,0:T(8,128)(2,1)} %bitcast.4), calls=%async_computation | async-start | bytes 524288 | tf_op jit(solution)/shard_map/all_to_all | solution.py:29
  26.5 32.9 %all-to-all-start.1 = ((bf16[16,32,2048]{2,1,0:T(8,128)(2,1)}), bf16[16,32,2048]{2,1,0:T(8,128)(2,1)S(1)}, u32[]{:S(2)}, u32[]{:S(2)}) async-start(bf16[16,32,2048]{2,1,0:T(8,128)(2,1)} %shard_map.101), calls=%async_computation.1 | async-start | bytes 4194304 | tf_op jit(solution)/shard_map/all_to_all | solution.py:29
  34.0 33.6 %collective-permute-start = (bf16[832,1024]{1,0:T(8,128)(2,1)}, bf16[832,1024]{1,0:T(8,128)(2,1)}, u32[]{:S(2)}, u32[]{:S(2)}) collective-permute-start(bf16[832,1024]{1,0:T(8,128)(2,1)} %bitcast.19), channel_id=1, source_target_pairs={{0,32},{32,0},{1,33},{33,1},{2,34},{34,2},{3,35},{35,3},{4,36},{36... | collective-permute-start | bytes 5111816 | tf_op jit(solution)/shard_map/ppermute | solution.py:17
  34.0 33.6 %collective-permute-start.1 = (bf16[832,1024]{1,0:T(8,128)(2,1)}, bf16[832,1024]{1,0:T(8,128)(2,1)}, u32[]{:S(2)}, u32[]{:S(2)}) collective-permute-start(bf16[832,1024]{1,0:T(8,128)(2,1)} %bitcast.24), channel_id=1, source_target_pairs={{0,32},{32,0},{1,33},{33,1},{2,34},{34,2},{3,35},{35,3},{4,36},{36... | collective-permute-start | bytes 5111816 | tf_op jit(solution)/shard_map/ppermute | solution.py:17
  34.5 33.1 %collective-permute-start.2 = (bf16[832,1024]{1,0:T(8,128)(2,1)}, bf16[832,1024]{1,0:T(8,128)(2,1)}, u32[]{:S(2)}, u32[]{:S(2)}) collective-permute-start(bf16[832,1024]{1,0:T(8,128)(2,1)} %refs_2_.3), channel_id=1, source_target_pairs={{0,32},{32,0},{1,33},{33,1},{2,34},{34,2},{3,35},{35,3},{4,36},{36... | collective-permute-start | bytes 5111816 | tf_op jit(solution)/shard_map/ppermute | solution.py:17
  60.8 31.7 %all-to-all-start.2 = ((bf16[16,32,2048]{2,1,0:T(8,128)(2,1)}), bf16[16,32,2048]{2,1,0:T(8,128)(2,1)}, u32[]{:S(2)}, u32[]{:S(2)}) async-start(bf16[16,32,2048]{2,1,0:T(8,128)(2,1)} %shard_map.104), calls=%async_computation.2 | async-start | bytes 4194304 | tf_op jit(solution)/shard_map/all_to_all | solution.py:29
  79.0 28.3 %collective-permute-start.3 = (bf16[64,2496]{1,0:T(8,128)(2,1)}, bf16[64,2496]{1,0:T(8,128)(2,1)S(1)}, u32[]{:S(2)}, u32[]{:S(2)}) collective-permute-start(bf16[64,2496]{1,0:T(8,128)(2,1)} %get-tuple-element.28), channel_id=1, source_target_pairs={{0,64},{64,128},{128,192},{192,0},{1,65},{65,129},{129,193},{193,1... | collective-permute-start | bytes 958472 | tf_op jit(solution)/shard_map/ppermute | solution.py:17
  79.0 31.3 %collective-permute-start.4 = (bf16[64,2496]{1,0:T(8,128)(2,1)}, bf16[64,2496]{1,0:T(8,128)(2,1)S(1)}, u32[]{:S(2)}, u32[]{:S(2)}) collective-permute-start(bf16[64,2496]{1,0:T(8,128)(2,1)} %get-tuple-element.29), channel_id=1, source_target_pairs={{0,128},{64,192},{128,0},{192,64},{1,129},{65,193},{129,1},{193,65... | collective-permute-start | bytes 958472 | tf_op jit(solution)/shard_map/ppermute | solution.py:17
  83.2 32.2 %collective-permute-start.5 = (bf16[64,2496]{1,0:T(8,128)(2,1)}, bf16[64,2496]{1,0:T(8,128)(2,1)}, u32[]{:S(2)}, u32[]{:S(2)}) collective-permute-start(bf16[64,2496]{1,0:T(8,128)(2,1)} %get-tuple-element.30), channel_id=1, source_target_pairs={{0,192},{64,0},{128,64},{192,128},{1,193},{65,1},{129,65},{193,129... | collective-permute-start | bytes 958472 | tf_op jit(solution)/shard_map/ppermute | solution.py:17
  103.0 42.7 %copy-start.4 = (bf16[1024,832]{0,1:T(8,128)(2,1)S(1)}, bf16[1024,832]{0,1:T(8,128)(2,1)}, u32[]{:S(2)}) copy-start(bf16[1024,832]{0,1:T(8,128)(2,1)} %param.7) | copy-start | bytes 5111812
  103.0 15.2 %collective-permute-start.9 = (bf16[64,2496]{1,0:T(8,128)(2,1)S(1)}, bf16[64,2496]{1,0:T(8,128)(2,1)S(1)}, u32[]{:S(2)}, u32[]{:S(2)}) collective-permute-start(bf16[64,2496]{1,0:T(8,128)(2,1)S(1)} %get-tuple-element.33), channel_id=1, source_target_pairs={{0,64},{64,128},{128,192},{192,0},{1,65},{65,129},{129,193},{193,1... | collective-permute-start | bytes 958472 | tf_op jit(solution)/shard_map/ppermute | solution.py:17
  103.1 29.9 %collective-permute-start.10 = (bf16[64,2496]{1,0:T(8,128)(2,1)S(1)}, bf16[64,2496]{1,0:T(8,128)(2,1)S(1)}, u32[]{:S(2)}, u32[]{:S(2)}) collective-permute-start(bf16[64,2496]{1,0:T(8,128)(2,1)S(1)} %get-tuple-element.34), channel_id=1, source_target_pairs={{0,128},{64,192},{128,0},{192,64},{1,129},{65,193},{129,1},{193,65... | collective-permute-start | bytes 958472 | tf_op jit(solution)/shard_map/ppermute | solution.py:17
  107.3 27.0 %collective-permute-start.11 = (bf16[64,2496]{1,0:T(8,128)(2,1)S(1)}, bf16[64,2496]{1,0:T(8,128)(2,1)S(1)}, u32[]{:S(2)}, u32[]{:S(2)}) collective-permute-start(bf16[64,2496]{1,0:T(8,128)(2,1)S(1)} %get-tuple-element.35), channel_id=1, source_target_pairs={{0,192},{64,0},{128,64},{192,128},{1,193},{65,1},{129,65},{193,129... | collective-permute-start | bytes 958472 | tf_op jit(solution)/shard_map/ppermute | solution.py:17
  110.4 108.6 %collective-permute-start.17 = (bf16[16,32,2048]{2,1,0:T(8,128)(2,1)S(1)}, bf16[16,32,2048]{2,1,0:T(8,128)(2,1)}, u32[]{:S(2)}, u32[]{:S(2)}) collective-permute-start(bf16[16,32,2048]{2,1,0:T(8,128)(2,1)S(1)} %copy-done.1), channel_id=1, source_target_pairs={{0,32},{32,0},{1,33},{33,1},{2,34},{34,2},{3,35},{35,3},{4,36},{36... | collective-permute-start | bytes 6291464 | tf_op jit(solution)/shard_map/ppermute | solution.py:17
  115.4 103.6 %collective-permute-start.18 = (bf16[16,32,2048]{2,1,0:T(8,128)(2,1)}, bf16[16,32,2048]{2,1,0:T(8,128)(2,1)}, u32[]{:S(2)}, u32[]{:S(2)}) collective-permute-start(bf16[16,32,2048]{2,1,0:T(8,128)(2,1)} %all-to-all-done.2.t_ref.g_ref.refs_5_), channel_id=1, source_target_pairs={{0,32},{32,0},{1,33},{33,1},{2,34},{34,2},{3,35},{35,3},{4,36},{36... | collective-permute-start | bytes 6291464 | tf_op jit(solution)/shard_map/ppermute | solution.py:17
  116.9 35.1 %copy-start.10 = (bf16[64,832]{1,0:T(8,128)(2,1)}, bf16[64,832]{1,0:T(8,128)(2,1)S(1)}, u32[]{:S(2)}) copy-start(bf16[64,832]{1,0:T(8,128)(2,1)S(1)} %get-tuple-element.42.a_ref) | copy-start | bytes 319492
  118.2 18.7 %collective-permute-start.8 = (bf16[64,1664]{1,0:T(8,128)(2,1)S(1)}, bf16[64,1664]{1,0:T(8,128)(2,1)S(1)}, u32[]{:S(2)}, u32[]{:S(2)}) collective-permute-start(bf16[64,1664]{1,0:T(8,128)(2,1)S(1)} %get-tuple-element.31.refs_0_), channel_id=1, source_target_pairs={{0,64},{64,128},{128,192},{192,0},{1,65},{65,129},{129,193},{193,1... | collective-permute-start | bytes 638984 | tf_op jit(solution)/shard_map/ppermute | solution.py:17
  132.9 12.7 %collective-permute-start.7 = (bf16[64,1664]{1,0:T(8,128)(2,1)S(1)}, bf16[64,1664]{1,0:T(8,128)(2,1)S(1)}, u32[]{:S(2)}, u32[]{:S(2)}) collective-permute-start(bf16[64,1664]{1,0:T(8,128)(2,1)S(1)} %get-tuple-element.31.refs_0_), channel_id=1, source_target_pairs={{0,128},{64,192},{128,0},{192,64},{1,129},{65,193},{129,1},{193,65... | collective-permute-start | bytes 638984 | tf_op jit(solution)/shard_map/ppermute | solution.py:17
  134.3 11.4 %collective-permute-start.6 = (bf16[64,1664]{1,0:T(8,128)(2,1)S(1)}, bf16[64,1664]{1,0:T(8,128)(2,1)S(1)}, u32[]{:S(2)}, u32[]{:S(2)}) collective-permute-start(bf16[64,1664]{1,0:T(8,128)(2,1)S(1)} %get-tuple-element.31.refs_0_), channel_id=1, source_target_pairs={{0,192},{64,0},{128,64},{192,128},{1,193},{65,1},{129,65},{193,129... | collective-permute-start | bytes 638984 | tf_op jit(solution)/shard_map/ppermute | solution.py:17
  152.0 47.4 %all-to-all-start.3 = ((bf16[16,16,2048]{2,1,0:T(8,128)(2,1)}), bf16[16,16,2048]{2,1,0:T(8,128)(2,1)}, u32[]{:S(2)}, u32[]{:S(2)}) async-start(bf16[16,16,2048]{2,1,0:T(8,128)(2,1)} %bitcast.8), calls=%async_computation.3 | async-start | bytes 2097152 | tf_op jit(solution)/shard_map/all_to_all | solution.py:29
  170.5 11.7 %collective-permute-start.14 = (bf16[64,1664]{1,0:T(8,128)(2,1)S(1)}, bf16[64,1664]{1,0:T(8,128)(2,1)S(1)}, u32[]{:S(2)}, u32[]{:S(2)}) collective-permute-start(bf16[64,1664]{1,0:T(8,128)(2,1)S(1)} %get-tuple-element.36.refs_8_.refs_0_), channel_id=1, source_target_pairs={{0,64},{64,128},{128,192},{192,0},{1,65},{65,129},{129,193},{193,1... | collective-permute-start | bytes 638984 | tf_op jit(solution)/shard_map/ppermute | solution.py:17
  173.2 16.7 %collective-permute-start.13 = (bf16[64,1664]{1,0:T(8,128)(2,1)S(1)}, bf16[64,1664]{1,0:T(8,128)(2,1)S(1)}, u32[]{:S(2)}, u32[]{:S(2)}) collective-permute-start(bf16[64,1664]{1,0:T(8,128)(2,1)S(1)} %get-tuple-element.36.refs_8_.refs_0_), channel_id=1, source_target_pairs={{0,128},{64,192},{128,0},{192,64},{1,129},{65,193},{129,1},{193,65... | collective-permute-start | bytes 638984 | tf_op jit(solution)/shard_map/ppermute | solution.py:17
  175.7 14.2 %collective-permute-start.12 = (bf16[64,1664]{1,0:T(8,128)(2,1)S(1)}, bf16[64,1664]{1,0:T(8,128)(2,1)S(1)}, u32[]{:S(2)}, u32[]{:S(2)}) collective-permute-start(bf16[64,1664]{1,0:T(8,128)(2,1)S(1)} %get-tuple-element.36.refs_8_.refs_0_), channel_id=1, source_target_pairs={{0,192},{64,0},{128,64},{192,128},{1,193},{65,1},{129,65},{193,129... | collective-permute-start | bytes 638984 | tf_op jit(solution)/shard_map/ppermute | solution.py:17
  198.9 12.7 %collective-permute-start.16 = (bf16[256,1664]{1,0:T(8,128)(2,1)}, bf16[256,1664]{1,0:T(8,128)(2,1)}, u32[]{:S(2)}, u32[]{:S(2)}) collective-permute-start(bf16[256,1664]{1,0:T(8,128)(2,1)} %get-tuple-element.40.refs_1_), channel_id=1, source_target_pairs={{0,32},{32,0},{1,33},{33,1},{2,34},{34,2},{3,35},{35,3},{4,36},{36... | collective-permute-start | bytes 2555912 | tf_op jit(solution)/shard_map/ppermute | solution.py:17
  198.9 15.9 %collective-permute-start.15 = (bf16[256,1664]{1,0:T(8,128)(2,1)S(1)}, bf16[256,1664]{1,0:T(8,128)(2,1)}, u32[]{:S(2)}, u32[]{:S(2)}) collective-permute-start(bf16[256,1664]{1,0:T(8,128)(2,1)S(1)} %get-tuple-element.39.refs_0_), channel_id=1, source_target_pairs={{0,32},{32,0},{1,33},{33,1},{2,34},{34,2},{3,35},{35,3},{4,36},{36... | collective-permute-start | bytes 2555912 | tf_op jit(solution)/shard_map/ppermute | solution.py:17
  199.5 31.2 %all-to-all-start.4 = ((bf16[16,16,2048]{2,1,0:T(8,128)(2,1)}), bf16[16,16,2048]{2,1,0:T(8,128)(2,1)}, u32[]{:S(2)}, u32[]{:S(2)}) async-start(bf16[16,16,2048]{2,1,0:T(8,128)(2,1)} %bitcast.9), calls=%async_computation.4 | async-start | bytes 2097152 | tf_op jit(solution)/shard_map/all_to_all | solution.py:29
  208.4 19.1 %collective-permute-start.21 = (bf16[144,832]{1,0:T(8,128)(2,1)}, bf16[144,832]{1,0:T(8,128)(2,1)S(1)}, u32[]{:S(2)}, u32[]{:S(2)}) collective-permute-start(bf16[144,832]{1,0:T(8,128)(2,1)} %shard_map.111.refs_0_), channel_id=1, source_target_pairs={{0,64},{64,128},{128,192},{192,0},{1,65},{65,129},{129,193},{193,1... | collective-permute-start | bytes 718856 | tf_op jit(solution)/shard_map/ppermute | solution.py:17
  211.6 15.9 %collective-permute-start.20 = (bf16[144,832]{1,0:T(8,128)(2,1)}, bf16[144,832]{1,0:T(8,128)(2,1)S(1)}, u32[]{:S(2)}, u32[]{:S(2)}) collective-permute-start(bf16[144,832]{1,0:T(8,128)(2,1)} %shard_map.111.refs_0_), channel_id=1, source_target_pairs={{0,128},{64,192},{128,0},{192,64},{1,129},{65,193},{129,1},{193,65... | collective-permute-start | bytes 718856 | tf_op jit(solution)/shard_map/ppermute | solution.py:17
  214.9 12.6 %collective-permute-start.19 = (bf16[144,832]{1,0:T(8,128)(2,1)}, bf16[144,832]{1,0:T(8,128)(2,1)}, u32[]{:S(2)}, u32[]{:S(2)}) collective-permute-start(bf16[144,832]{1,0:T(8,128)(2,1)} %shard_map.111.refs_0_), channel_id=1, source_target_pairs={{0,192},{64,0},{128,64},{192,128},{1,193},{65,1},{129,65},{193,129... | collective-permute-start | bytes 718856 | tf_op jit(solution)/shard_map/ppermute | solution.py:17
  235.7 33.1 %all-to-all-start.5 = ((f32[8,4,2048]{2,1,0:T(4,128)}), f32[8,4,2048]{2,1,0:T(4,128)S(1)}, u32[]{:S(2)}, u32[]{:S(2)}) async-start(f32[8,4,2048]{2,1,0:T(4,128)} %reshape.48), calls=%async_computation.5 | async-start | bytes 524288 | tf_op jit(solution)/shard_map/all_to_all | solution.py:29
  258.0 1.3 collective-permute-start.23
  258.1 11.5 %collective-permute-start.22 = (bf16[512,896]{1,0:T(8,128)(2,1)S(1)}, bf16[512,896]{1,0:T(8,128)(2,1)}, u32[]{:S(2)}, u32[]{:S(2)}) collective-permute-start(bf16[512,896]{1,0:T(8,128)(2,1)S(1)} %copy-done.9), channel_id=1, source_target_pairs={{0,32},{32,0},{1,33},{33,1},{2,34},{34,2},{3,35},{35,3},{4,36},{36... | collective-permute-start | bytes 2752520 | tf_op jit(solution)/shard_map/ppermute | solution.py:17
  (17 other events, 182.7 us)
where the time goes:
time: 277 us; the launch traced here: 275 us
  starting transfers between devices  102 us (37%)
  waiting for transfers between devices  94.5 us (34%)
  Pallas kernels  61 us (22%)
  local copies, waits for them, and re-layouts  14.1 us (5%)
  other arithmetic  3.27 us (1%)
    all_to_all x6, starting transfers between devices, exchange(): return lax.all_to_all(value, axis, split_axis=0, concat_axis=0, tiled=True)  70.8 us
    all_to_all x6, waiting for transfers between devices, exchange(): return lax.all_to_all(value, axis, split_axis=0, concat_axis=0, tiled=True)  49.7 us
    ppermute x24, waiting for transfers between devices, shift(): return lax.ppermute(value, axis, [(i, (i + k) % n) for i in range(n)])  44.8 us
    ppermute x24, starting transfers between devices, shift(): return lax.ppermute(value, axis, [(i, (i + k) % n) for i in range(n)])  30.9 us
    pallas_call x2, Pallas kernels, project(): pl.pallas_call(kernel, grid_spec=pltpu.PrefetchScalarGridSpec(num_scalar_...  16 us
    pallas_call x2, Pallas kernels, weight_gradients(): pl.pallas_call(kernel, grid=(steps,), in_specs=[left_spec(t[1]) for t in...  14.3 us
    pallas_call x2, Pallas kernels, input_terms(): pl.pallas_call(kernel, grid_spec=pltpu.PrefetchScalarGridSpec(num_scalar_...  12.5 us
    unnamed x38, local copies, waits for them, and re-layouts  10.9 us
  transfers between devices with their start and end apart: 30, of which 14 were waited for; matrix products, arithmetic and copies ran while one was open for 1% of the time, Pallas kernels for 18%

commit v1 on v0

--- a/solution.py
+++ b/solution.py
@@ -40,48 +40,53 @@
     return lax.dot_general(left, right, (((1,), (1,)), ((), ())), preferred_element_type=F32)
 
 
-def project(zi, pairs, own, other, ties=()):
+def project(zi, columns, own, other, shard=None, weight=1):
     n = len(own)
-    peers, few, width = pairs.shape
+    shards = [] if shard is None else [shard]
+    peers, few, width = columns.shape
     rows = peers * few // 2
     units = own[0].shape[0]
     steps, group = 4, rows // NZ
     tile = width // steps
 
-    def kernel(z_ref, t_ref, g_ref, *refs):
+    def kernel(z_ref, a_ref, b_ref, *refs):
         own_refs, other_refs = refs[:n], refs[n : 2 * n]
-        refs = refs[2 * n + len(ties) :]
-        out, sends, totals = refs[0], refs[1:NZ], refs[NZ:]
+        refs = refs[2 * n :]
+        if shards:
+            refs[1 + NZ][...] = jnp.broadcast_to(refs[0][...][None], refs[1 + NZ].shape)
+        out, sends, totals = refs[len(shards)], refs[len(shards) + 1 :][: NZ - 1], refs[-n:]
         step = pl.program_id(0)
-        columns = [t_ref[...].reshape(rows, tile)] * 2 + [g_ref[...].reshape(rows, tile)]
+        left = jnp.concatenate([a_ref[...].reshape(rows, tile), b_ref[...].reshape(rows, tile)], axis=0)
 
         @pl.when(step == 0)
         def _():
-            for total, c, w in zip(totals, columns, own_refs):
-                total[...] = dot_nt(c, w[...])
+            for total, w in zip(totals, own_refs):
+                total[...] = dot_nt(left, w[...])
 
         @pl.when((step > 0) & (step < steps // 2))
         def _():
-            for total, c, w in zip(totals, columns, own_refs):
-                total[...] += dot_nt(c, w[...])
+            for total, w in zip(totals, own_refs):
+                total[...] += dot_nt(left, w[...])
 
         @pl.when(step >= steps // 2)
         def _():
-            for total, c, w in zip(totals, columns, other_refs):
-                total[...] += dot_nt(c, w[...])
+            for total, w in zip(totals, other_refs):
+                total[...] += dot_nt(left, w[...])
 
         @pl.when(step == steps - 1)
         def _():
             for k in range(NZ):
-                start = pl.multiple_of(lax.rem(z_ref[0] + k, NZ) * group, group)
-                value = jnp.concatenate([total[pl.ds(start, group), :] for total in totals], axis=1)
-                if k == 0:
-                    out[...] = value
-                else:
-                    sends[k - 1][...] = value.astype(BF)
+                for h in range(2):
+                    start = pl.multiple_of(h * rows + lax.rem(z_ref[0] + k, NZ) * group, group)
+                    parts = [total[pl.ds(start, group), :] for total in totals]
+                    value = jnp.concatenate(parts, axis=1) if n > 1 else parts[0]
+                    if k == 0:
+                        out[h * group : (h + 1) * group, :] = value
+                    else:
+                        sends[k - 1][h * group : (h + 1) * group, :] = value.astype(BF)
 
     half = steps // 2
-    whole = pl.BlockSpec((group, n * units), lambda i, z: (0, 0))
+    whole = pl.BlockSpec((2 * group, n * units), lambda i, z: (0, 0))
     return pl.pallas_call(
         kernel,
         grid_spec=pltpu.PrefetchScalarGridSpec(
@@ -93,32 +98,39 @@
             ]
             + [pl.BlockSpec((units, tile), lambda i, z: (0, jnp.minimum(i, half - 1)))] * n
             + [pl.BlockSpec((units, tile), lambda i, z: (0, jnp.maximum(i - half, 0)))] * n
-            + [pl.BlockSpec(memory_space=pl.ANY)] * len(ties),
-            out_specs=[whole] * NZ,
-            scratch_shapes=[pltpu.VMEM((rows, units), F32)] * n,
-        ),
-        out_shape=[jax.ShapeDtypeStruct((group, n * units), F32)]
-        + [jax.ShapeDtypeStruct((group, n * units), BF)] * (NZ - 1),
+            + [pl.BlockSpec((few, tile), lambda i, z: (0, i))] * len(shards),
+            out_specs=[whole] * NZ
+            + [pl.BlockSpec((peers, few, tile), lambda i, z: (0, 0, i))] * len(shards),
+            scratch_shapes=[pltpu.VMEM((2 * rows, units), F32)] * n,
+        ),
+        out_shape=[jax.ShapeDtypeStruct((2 * group, n * units), F32)]
+        + [jax.ShapeDtypeStruct((2 * group, n * units), BF)] * (NZ - 1)
+        + [jax.ShapeDtypeStruct((peers, few, width), BF)] * len(shards),
         compiler_params=params(),
         cost_estimate=pl.CostEstimate(
-            flops=2 * rows * width * units * n,
-            bytes_accessed=2 * (2 * rows * width + width * units * n) + 10 * group * n * units,
+            flops=weight * 4 * rows * width * units * n,
+            bytes_accessed=weight * (2 * (2 * rows * width + width * units * n) + 20 * group * n * units),
             transcendentals=0,
         ),
-    )(zi, pairs, pairs, *own, *other, *ties)
-
-
-def activations(parts, bound):
-    rows, units = parts[0].shape[0], bound.shape[1]
+    )(zi, columns, columns, *own, *other, *shards)
+
+
+def activations(both, hidden_grad, bound, part, ties=()):
+    rows, units = hidden_grad[0].shape
+    rows = rows // 2
     steps = 2
     tile = rows // steps
 
     def kernel(*refs):
-        bound_ref, acts_ref, hidden_ref, amax_ref = refs[NZ:]
-        total = refs[0][...]
-        for ref in refs[1:NZ]:
+        b_refs, h_refs, bound_ref = refs[:NZ], refs[NZ : 2 * NZ], refs[2 * NZ]
+        acts_ref, hidden_ref, amax_ref = refs[2 * NZ + 1 + len(ties) :]
+        total = b_refs[0][...]
+        for ref in b_refs[1:]:
             total = total + ref[...].astype(F32)
-        gate, up, grad = (total[:, i * units : (i + 1) * units] for i in range(3))
+        grad = h_refs[0][...]
+        for ref in h_refs[1:]:
+            grad = grad + ref[...].astype(F32)
+        gate, up = total[:, :units], total[:, units:]
         limit = bound_ref[...]
         sig = jax.nn.sigmoid(gate)
         act = gate * sig
@@ -142,11 +154,14 @@
 
     wide = pl.BlockSpec((tile, 2 * units), lambda i: (i, 0))
     narrow = pl.BlockSpec((tile, units), lambda i: (i, 0))
+    wide_in = pl.BlockSpec((tile, 2 * units), lambda i: (part * steps + i, 0))
+    narrow_in = pl.BlockSpec((tile, units), lambda i: (part * steps + i, 0))
     line = pl.BlockSpec((1, units), lambda i: (0, 0))
     return pl.pallas_call(
         kernel,
         grid=(steps,),
-        in_specs=[pl.BlockSpec((tile, 3 * units), lambda i: (i, 0))] * NZ + [line],
+        in_specs=[wide_in] * NZ + [narrow_in] * NZ + [line]
+        + [pl.BlockSpec(memory_space=pl.ANY)] * len(ties),
         out_specs=[wide, narrow, line],
         out_shape=[
             jax.ShapeDtypeStruct((rows, 2 * units), BF),
@@ -157,10 +172,10 @@
         cost_estimate=pl.CostEstimate(
             flops=40 * rows * units, bytes_accessed=34 * rows * units, transcendentals=2 * rows * units
         ),
-    )(*parts, bound)
-
-
-def input_terms(zi, pieces, own, other, ties=()):
+    )(*both, *hidden_grad, bound, *ties)
+
+
+def input_terms(zi, pieces, own, other, ties=(), weight=1):
     group, both = pieces[0].shape
     units, depth = own[0].shape
     steps = 4
@@ -212,34 +227,16 @@
         ],
         compiler_params=params(),
         cost_estimate=pl.CostEstimate(
-            flops=4 * rows * both * depth,
-            bytes_accessed=4 * rows * both + 4 * rows * depth + 4 * both * depth,
+            flops=weight * 4 * rows * both * depth,
+            bytes_accessed=weight * (4 * rows * both + 4 * rows * depth + 4 * both * depth),
             transcendentals=0,
         ),
     )(zi, *pieces, *own, *other, *ties)
-
-
-def repeated(shard, peers, ties=()):
-    rows, width = shard.shape
-    steps = 4
-
-    def kernel(s_ref, *refs):
-        refs[-1][...] = jnp.broadcast_to(s_ref[...][None], refs[-1].shape)
-
-    return pl.pallas_call(
-        kernel,
-        grid=(steps,),
-        in_specs=[pl.BlockSpec((rows, width), lambda i: (0, 0))]
-        + [pl.BlockSpec(memory_space=pl.ANY)] * len(ties),
-        out_specs=pl.BlockSpec((peers // steps, rows, width), lambda i: (i, 0, 0)),
-        out_shape=jax.ShapeDtypeStruct((peers, rows, width), shard.dtype),
-        cost_estimate=pl.CostEstimate(flops=0, bytes_accessed=2 * peers * rows * width, transcendentals=0),
-    )(shard, *ties)
 
 
 def summed(pieces, ties=()):
     peers, rows, width = pieces.shape
-    steps = 4
+    steps = 2
     tile = width // steps
 
     def kernel(p_ref, *refs):
@@ -362,8 +359,8 @@
         scratch_shapes=[pltpu.VMEM((wide, n * rows), BF)],
         compiler_params=params(),
         cost_estimate=pl.CostEstimate(
-            flops=2 * n * rows * wide * depth,
-            bytes_accessed=2 * (n * rows * (wide + depth) + wide * depth),
+            flops=2 * n * rows * wide * depth // 1000,
+            bytes_accessed=2 * (n * rows * (wide + depth) + wide * depth) // 1000,
             transcendentals=0,
         ),
     )(*[t[0] for t in terms], *[t[2] for t in terms])
@@ -388,7 +385,6 @@
     half = block // NC
     few = NZ * NL * own_rows
     peers = NX * NY
-    chunk = few // 2
 
     gate_t, up_t = gate_weight.T, up_weight.T
     gate_other = swap(gate_t)
@@ -401,54 +397,59 @@
     both = jnp.concatenate([tokens, grad_mixed], axis=0).reshape(2 * own_rows, NZ, 1, block)
     both = jnp.broadcast_to(both.transpose(1, 2, 0, 3), (NZ, NL, 2 * own_rows, block))
     placed = own_first(exchange(both.reshape(NZ * NL, 2 * own_rows, block), ("z", "l")))
-    parts = placed.reshape(2, few // 2 // own_rows, 2, own_rows, block).transpose(0, 2, 1, 3, 4)
-    parts = parts.reshape(2, few, block)
-
-    own, other = [gate_t, up_t, down_weight], [gate_other, up_other, down_other]
+    tokens_few = placed[:, :own_rows].reshape(few, block)
+    grads_few = placed[:, own_rows:].reshape(few, block)
+
+    own, other = [gate_t, up_t], [gate_other, up_other]
     bound = amax_history[None, :]
 
-    pairs_a = exchange(repeated(parts[0], peers), ("x", "y"))
-    pairs_b = exchange(repeated(parts[1], peers), ("x", "y"))
-    part_a = project(zs, pairs_a, own, other)
-    part_b = project(zs, pairs_b, own, other)
-    acts_a, hidden_a, amax_a = activations(sum_parts(part_a), bound)
-    acts_b, hidden_b, amax_b = activations(sum_parts(part_b), bound)
-    terms_a, acts_all_a = input_terms(zs, gather_parts(acts_a), own[:2], other[:2], (acts_b,))
-    terms_b, acts_all_b = input_terms(zs, gather_parts(acts_b), own[:2], other[:2])
+    tokens_all = exchange(jnp.broadcast_to(tokens_few[None], (peers, few, block)), ("x", "y"))
+    *both, grads_sent = project(zs, tokens_all, own, other, grads_few)
+    grads_all = exchange(grads_sent, ("x", "y"))
+    hidden_grad = project(zs, grads_all, [down_weight], [down_other], None, 8)
+    both, hidden_grad = sum_parts(both), sum_parts(hidden_grad)
+
+    acts_a, hidden_a, amax_a = activations(both, hidden_grad, bound, 0)
+    pieces_a = gather_parts(acts_a)
+    acts_b, hidden_b, amax_b = activations(both, hidden_grad, bound, 1, pieces_a[1:])
+    pieces_b = gather_parts(acts_b)
+    terms_a, acts_all_a = input_terms(zs, pieces_a, own, other, (acts_b,))
+    terms_b, acts_all_b = input_terms(zs, pieces_b, own, other, (), 8)
+    chunk = few // 2
 
     sums_a = exchange(terms_a.reshape(peers, chunk, block), ("x", "y"))
     sums_b = exchange(terms_b.reshape(peers, chunk, block), ("x", "y"))
 
     units = gate_t.shape[0]
-    message = hidden_message(hidden_a, hidden_b, (amax_a, amax_b), (terms_b,))
-    other_a, other_b = swap(pairs_a), swap(pairs_b)
+    message = hidden_message(hidden_a, hidden_b, (amax_a, amax_b), pieces_b[1:])
+    tokens_other, grads_other = swap(tokens_all), swap(grads_all)
     grad_gate, grad_up = weight_gradients(
         [
-            (acts_all_a, 0, pairs_a, 0, 0),
-            (acts_all_b, 0, pairs_b, 0, 0),
-            (swap(acts_all_a), 0, other_a, 0, 1),
-            (swap(acts_all_b), 0, other_b, 0, 1),
+            (acts_all_a, 0, tokens_all, 0, 0),
+            (acts_all_b, 0, tokens_all, 1, 0),
+            (swap(acts_all_a), 0, tokens_other, 0, 1),
+            (swap(acts_all_b), 0, tokens_other, 1, 1),
         ],
         2,
         units,
         half,
     )
     hidden_all, amax = hidden_by_z(zs, gather_parts(message), (grad_gate,))
+    mine = [summed(sums_a), summed(sums_b, (hidden_all,))]
     amax = jnp.maximum(amax, swap(amax))[0]
     hidden_other = swap(hidden_all)
     (grad_down,) = weight_gradients(
         [
-            (hidden_all, 0, pairs_a, 1, 0),
-            (hidden_all, 1, pairs_b, 1, 0),
-            (hidden_other, 0, other_a, 1, 1),
-            (hidden_other, 1, other_b, 1, 1),
+            (hidden_all, 0, grads_all, 0, 0),
+            (hidden_all, 1, grads_all, 1, 0),
+            (hidden_other, 0, grads_other, 0, 1),
+            (hidden_other, 1, grads_other, 1, 1),
         ],
         1,
         units,
         half,
     )
 
-    mine = [summed(sums_a), summed(sums_b, (grad_gate, hidden_all))]
     back = exchange(jnp.concatenate(mine, axis=0).reshape(NZ * NL, own_rows, block), ("z", "l"))
     back = own_first(jnp.sum(back.reshape(NZ, NL, own_rows, block), axis=1).astype(BF))
     grad_tokens = back.transpose(1, 0, 2).reshape(own_rows, width)

time: 277 us -> 275 us (level)
  waiting for transfers between devices: 94.5 us -> 119 us
  starting transfers between devices: 102 us -> 80.1 us
  Pallas kernels: 61 us -> 50.6 us
  local copies, waits for them, and re-layouts: 14.1 us -> 19.6 us
    all_to_all x6, starting transfers between devices: 70.8 us -> 41.6 us  [exchange(): return lax.all_to_all(value, axis, split_axis=0, concat_axis=0, tiled=True)]
    all_to_all x6, waiting for transfers between devices: 49.7 us -> 64.2 us  [exchange(): return lax.all_to_all(value, axis, split_axis=0, concat_axis=0, tiled=True)]
    ppermute x24, waiting for transfers between devices: 44.8 us -> 54.5 us  [shift(): return lax.ppermute(value, axis, [(i, (i + k) % n) for i in range(n)])]
    ppermute x24, starting transfers between devices: 30.9 us -> 38.5 us  [shift(): return lax.ppermute(value, axis, [(i, (i + k) % n) for i in range(n)])]
    unnamed x38 -> x58, local copies, waits for them, and re-layouts: 10.9 us -> 14.8 us
    pallas_call x4 -> x2, Pallas kernels: 7.55 us -> 3.72 us  [activations(): pl.pallas_call(kernel, grid=(steps,), in_specs=[wide_in] * NZ + [narrow_i...]
  transfers between devices with their start and end apart: 30 -> 30, of which waited for: 14 -> 18; matrix products, arithmetic and copies ran while one was open for 1% -> 1% of each run, Pallas kernels for 18% -> 12%
where the time goes in v1:
time: 275 us; the launch traced here: 273 us
  waiting for transfers between devices  119 us (43%)
  starting transfers between devices  80.1 us (29%)
  Pallas kernels  50.6 us (18%)
  local copies, waits for them, and re-layouts  19.6 us (7%)
  other arithmetic  3.27 us (1%)
    all_to_all x6, waiting for transfers between devices, exchange(): return lax.all_to_all(value, axis, split_axis=0, concat_axis=0, tiled=True)  64.2 us
    ppermute x24, waiting for transfers between devices, shift(): return lax.ppermute(value, axis, [(i, (i + k) % n) for i in range(n)])  54.5 us
    all_to_all x6, starting transfers between devices, exchange(): return lax.all_to_all(value, axis, split_axis=0, concat_axis=0, tiled=True)  41.6 us
    ppermute x24, starting transfers between devices, shift(): return lax.ppermute(value, axis, [(i, (i + k) % n) for i in range(n)])  38.5 us
    unnamed x58, local copies, waits for them, and re-layouts  14.8 us
    pallas_call x2, Pallas kernels, weight_gradients(): pl.pallas_call(kernel, grid=(steps,), in_specs=[left_spec(t[1]) for t in...  14 us
    pallas_call x2, Pallas kernels, project(): pl.pallas_call(kernel, grid_spec=pltpu.PrefetchScalarGridSpec(num_scalar_...  13.6 us
    pallas_call x2, Pallas kernels, input_terms(): pl.pallas_call(kernel, grid_spec=pltpu.PrefetchScalarGridSpec(num_scalar_...  11.3 us
  transfers between devices with their start and end apart: 30, of which 18 were waited for; matrix products, arithmetic and copies ran while one was open for 1% of the time, Pallas kernels for 12%

profile of v1, /device:TPU:2, one launch (start us, length us, event | category | flops | bytes accessed | tf_op | source)
XLA Modules:
  0.0 273.3 jit_solution(4660554966040974531)
XLA Ops:
  2.3 8.5 %all-to-all-start = ((bf16[8,8,2048]{2,1,0:T(8,128)(2,1)}), bf16[8,8,2048]{2,1,0:T(8,128)(2,1)S(1)}, u32[]{:S(2)}, u32[]{:S(2)}) async-start(bf16[8,8,2048]{2,1,0:T(8,128)(2,1)} %bitcast.4), calls=%async_computation | async-start | bytes 524288 | tf_op jit(solution)/shard_map/all_to_all | solution.py:29
  10.8 11.9 %all-to-all-done = bf16[8,8,2048]{2,1,0:T(8,128)(2,1)S(1)} async-done(((bf16[8,8,2048]{2,1,0:T(8,128)(2,1)}), bf16[8,8,2048]{2,1,0:T(8,128)(2,1)S(1)}, u32[]{:S(2)}, u32[]{:S(2)}) %all-to-all-start) | async-done | bytes 262176 | tf_op jit(solution)/shard_map/all_to_all | solution.py:29
  25.1 7.7 %all-to-all-start.1 = ((bf16[16,32,2048]{2,1,0:T(8,128)(2,1)}), bf16[16,32,2048]{2,1,0:T(8,128)(2,1)}, u32[]{:S(2)}, u32[]{:S(2)}) async-start(bf16[16,32,2048]{2,1,0:T(8,128)(2,1)} %broadcast_in_dim.20), calls=%async_computation.1 | async-start | bytes 4194304 | tf_op jit(solution)/shard_map/all_to_all | solution.py:29
  36.7 2.4 collective-permute-done.1.refs_3_.refs_7_
  39.1 19.3 %all-to-all-done.1.a_ref.b_ref.refs_4_.refs_5_ = bf16[16,32,2048]{2,1,0:T(8,128)(2,1)} async-done(((bf16[16,32,2048]{2,1,0:T(8,128)(2,1)}), bf16[16,32,2048]{2,1,0:T(8,128)(2,1)}, u32[]{:S(2)}, u32[]{:S(2)}) %all-to-all-start.1) | async-done | bytes 2097184 | tf_op jit(solution)/shard_map/all_to_all | solution.py:29
  59.9 8.9 %shard_map.101 = (f32[128,1664]{1,0:T(8,128)S(1)}, bf16[128,1664]{1,0:T(8,128)(2,1)S(1)}, bf16[128,1664]{1,0:T(8,128)(2,1)S(1)}, bf16[128,1664]{1,0:T(8,128)(2,1)S(1)}, bf16[16,32,2048]{2,1,0:T(8,128)(2,1)}) custom-call(s32[1]{0:T(128)} %bitcast.z_ref, bf16[16,32,2048]{2,1,0:T(8,128)(2,1)} %all-to-all-done.1.a_ref.b_ref.refs_4_.refs_5_, ...), custom_call_target="tpu_custom_call" | custom-call | flops 3489660928 | bytes 11042816 | tf_op jit(solution)/shard_map/pallas_call | solution.py:90
  71.1 6.4 %all-to-all-start.2 = ((bf16[16,32,2048]{2,1,0:T(8,128)(2,1)}), bf16[16,32,2048]{2,1,0:T(8,128)(2,1)S(1)}, u32[]{:S(2)}, u32[]{:S(2)}) async-start(bf16[16,32,2048]{2,1,0:T(8,128)(2,1)} %get-tuple-element.32), calls=%async_computation.2 | async-start | bytes 4194304 | tf_op jit(solution)/shard_map/all_to_all | solution.py:29
  77.9 3.9 %collective-permute-start.3 = (bf16[128,1664]{1,0:T(8,128)(2,1)}, bf16[128,1664]{1,0:T(8,128)(2,1)}, u32[]{:S(2)}, u32[]{:S(2)}) collective-permute-start(bf16[128,1664]{1,0:T(8,128)(2,1)} %copy-done.22), channel_id=1, source_target_pairs={{0,128},{64,192},{128,0},{192,64},{1,129},{65,193},{129,1},{193,65... | collective-permute-start | bytes 1277960 | tf_op jit(solution)/shard_map/ppermute | solution.py:17
  84.8 17.9 %all-to-all-done.2.a_ref.b_ref.refs_4_.refs_5_ = bf16[16,32,2048]{2,1,0:T(8,128)(2,1)S(1)} async-done(((bf16[16,32,2048]{2,1,0:T(8,128)(2,1)}), bf16[16,32,2048]{2,1,0:T(8,128)(2,1)S(1)}, u32[]{:S(2)}, u32[]{:S(2)}) %all-to-all-start.2) | async-done | bytes 2097184 | tf_op jit(solution)/shard_map/all_to_all | solution.py:29
  106.9 4.7 %shard_map.102 = (f32[128,832]{1,0:T(8,128)S(1)}, bf16[128,832]{1,0:T(8,128)(2,1)S(1)}, bf16[128,832]{1,0:T(8,128)(2,1)S(1)}, bf16[128,832]{1,0:T(8,128)(2,1)S(1)}) custom-call(s32[1]{0:T(128)} %bitcast.z_ref, bf16[16,32,2048]{2,1,0:T(8,128)(2,1)} %copy-done, bf16[16,32,2048]{2,1,0:T(8,128)(2,1)} %copy-done, bf16[832,1024]{1,0:T(8,128)(2,1)S(1)} %copy-done.18, ...), custom_call_target="tpu_custom_call" | custom-call | flops 13958643712 | bytes 52559872 | tf_op jit(solution)/shard_map/pallas_call | solution.py:90
  111.7 3.8 %collective-permute-start.7 = (bf16[128,832]{1,0:T(8,128)(2,1)S(1)}, bf16[128,832]{1,0:T(8,128)(2,1)S(1)}, u32[]{:S(2)}, u32[]{:S(2)}) collective-permute-start(bf16[128,832]{1,0:T(8,128)(2,1)S(1)} %get-tuple-element.35), channel_id=1, source_target_pairs={{0,128},{64,192},{128,0},{192,64},{1,129},{65,193},{129,1},{193,65... | collective-permute-start | bytes 638984 | tf_op jit(solution)/shard_map/ppermute | solution.py:17
  119.2 8.5 %collective-permute-done.4.refs_3_ = bf16[128,1664]{1,0:T(8,128)(2,1)} collective-permute-done((bf16[128,1664]{1,0:T(8,128)(2,1)}, bf16[128,1664]{1,0:T(8,128)(2,1)}, u32[]{:S(2)}, u32[]{:S(2)}) %collective-permute-start.4) | collective-permute-done | bytes 426016 | tf_op jit(solution)/shard_map/ppermute | solution.py:17
  127.6 3.7 %collective-permute-done.7.refs_6_ = bf16[128,832]{1,0:T(8,128)(2,1)S(1)} collective-permute-done((bf16[128,832]{1,0:T(8,128)(2,1)S(1)}, bf16[128,832]{1,0:T(8,128)(2,1)S(1)}, u32[]{:S(2)}, u32[]{:S(2)}) %collective-permute-start.7) | collective-permute-done | bytes 213024 | tf_op jit(solution)/shard_map/ppermute | solution.py:17
  135.6 9.3 %collective-permute-start.10 = (bf16[64,1664]{1,0:T(8,128)(2,1)S(1)}, bf16[64,1664]{1,0:T(8,128)(2,1)S(1)}, u32[]{:S(2)}, u32[]{:S(2)}) collective-permute-start(bf16[64,1664]{1,0:T(8,128)(2,1)S(1)} %get-tuple-element.37.refs_0_), channel_id=1, source_target_pairs={{0,128},{64,192},{128,0},{192,64},{1,129},{65,193},{129,1},{193,65... | collective-permute-start | bytes 638984 | tf_op jit(solution)/shard_map/ppermute | solution.py:17
  144.9 2.7 collective-permute-done.11.refs_11_.refs_3_
  147.6 12.0 %collective-permute-done.10.refs_10_.refs_2_ = bf16[64,1664]{1,0:T(8,128)(2,1)S(1)} collective-permute-done((bf16[64,1664]{1,0:T(8,128)(2,1)S(1)}, bf16[64,1664]{1,0:T(8,128)(2,1)S(1)}, u32[]{:S(2)}, u32[]{:S(2)}) %collective-permute-start.10) | collective-permute-done | bytes 213024 | tf_op jit(solution)/shard_map/ppermute | solution.py:17
  159.6 5.9 %collective-permute-done.9.refs_9_.refs_1_ = bf16[64,1664]{1,0:T(8,128)(2,1)S(1)} collective-permute-done((bf16[64,1664]{1,0:T(8,128)(2,1)S(1)}, bf16[64,1664]{1,0:T(8,128)(2,1)S(1)}, u32[]{:S(2)}, u32[]{:S(2)}) %collective-permute-start.9) | collective-permute-done | bytes 213024 | tf_op jit(solution)/shard_map/ppermute | solution.py:17
  168.8 3.7 %collective-permute-start.12 = (bf16[64,1664]{1,0:T(8,128)(2,1)}, bf16[64,1664]{1,0:T(8,128)(2,1)}, u32[]{:S(2)}, u32[]{:S(2)}) collective-permute-start(bf16[64,1664]{1,0:T(8,128)(2,1)} %get-tuple-element.38.refs_8_.refs_0_), channel_id=1, source_target_pairs={{0,192},{64,0},{128,64},{192,128},{1,193},{65,1},{129,65},{193,129... | collective-permute-start | bytes 638984 | tf_op jit(solution)/shard_map/ppermute | solution.py:17
  172.5 5.6 %shard_map.105 = (bf16[256,2048]{1,0:T(8,128)(2,1)S(1)}, bf16[256,1664]{1,0:T(8,128)(2,1)S(1)}) custom-call(s32[1]{0:T(128)} %bitcast.z_ref, bf16[64,1664]{1,0:T(8,128)(2,1)S(1)} %get-tuple-element.37.refs_0_, bf16[64,1664]{1,0:T(8,128)(2,1)S(1)} %collective-permute-done.9.refs_9_.refs_1_, bf16[64,1664]{1,0:T(8,128)(2,1)S(1)} %collective-permute-done.10.refs_10_.refs_2_, ...), custom_call_target="tpu_custom_call" | custom-call | flops 1744830464 | bytes 9568256 | tf_op jit(solution)/shard_map/pallas_call | solution.py:209
  180.0 7.1 %all-to-all-start.3 = ((bf16[16,16,2048]{2,1,0:T(8,128)(2,1)}), bf16[16,16,2048]{2,1,0:T(8,128)(2,1)}, u32[]{:S(2)}, u32[]{:S(2)}) async-start(bf16[16,16,2048]{2,1,0:T(8,128)(2,1)} %bitcast.27), calls=%async_computation.3 | async-start | bytes 2097152 | tf_op jit(solution)/shard_map/all_to_all | solution.py:29
  187.1 3.5 %collective-permute-done.12.refs_1_.refs_0_ = bf16[64,1664]{1,0:T(8,128)(2,1)} collective-permute-done((bf16[64,1664]{1,0:T(8,128)(2,1)}, bf16[64,1664]{1,0:T(8,128)(2,1)}, u32[]{:S(2)}, u32[]{:S(2)}) %collective-permute-start.12) | collective-permute-done | bytes 213024 | tf_op jit(solution)/shard_map/ppermute | solution.py:17
  190.6 5.7 %shard_map.107 = (bf16[256,2048]{1,0:T(8,128)(2,1)S(1)}, bf16[256,1664]{1,0:T(8,128)(2,1)S(1)}) custom-call(s32[1]{0:T(128)} %bitcast.z_ref, bf16[64,1664]{1,0:T(8,128)(2,1)} %get-tuple-element.38.refs_8_.refs_0_, bf16[64,1664]{1,0:T(8,128)(2,1)} %collective-permute-done.12.refs_1_.refs_0_, bf16[64,1664]{1,0:T(8,128)(2,1)} %collective-permute-done.13.refs_2_.refs_1_, ...), custom_call_target="tpu_custom_call" | custom-call | flops 13958643712 | bytes 76546048 | tf_op jit(solution)/shard_map/pallas_call | solution.py:209
  198.2 4.9 %all-to-all-done.3.p_ref = bf16[16,16,2048]{2,1,0:T(8,128)(2,1)} async-done(((bf16[16,16,2048]{2,1,0:T(8,128)(2,1)}), bf16[16,16,2048]{2,1,0:T(8,128)(2,1)}, u32[]{:S(2)}, u32[]{:S(2)}) %all-to-all-start.3) | async-done | bytes 1048608 | tf_op jit(solution)/shard_map/all_to_all | solution.py:29
  203.1 6.9 %all-to-all-start.4 = ((bf16[16,16,2048]{2,1,0:T(8,128)(2,1)}), bf16[16,16,2048]{2,1,0:T(8,128)(2,1)}, u32[]{:S(2)}, u32[]{:S(2)}) async-start(bf16[16,16,2048]{2,1,0:T(8,128)(2,1)} %bitcast.26), calls=%async_computation.4 | async-start | bytes 2097152 | tf_op jit(solution)/shard_map/all_to_all | solution.py:29
  214.6 3.7 %collective-permute-start.16 = (bf16[144,832]{1,0:T(8,128)(2,1)}, bf16[144,832]{1,0:T(8,128)(2,1)S(1)}, u32[]{:S(2)}, u32[]{:S(2)}) collective-permute-start(bf16[144,832]{1,0:T(8,128)(2,1)} %shard_map.108.refs_0_), channel_id=1, source_target_pairs={{0,128},{64,192},{128,0},{192,64},{1,129},{65,193},{129,1},{193,65... | collective-permute-start | bytes 718856 | tf_op jit(solution)/shard_map/ppermute | solution.py:17
  218.2 4.1 %collective-permute-start.15 = (bf16[144,832]{1,0:T(8,128)(2,1)}, bf16[144,832]{1,0:T(8,128)(2,1)}, u32[]{:S(2)}, u32[]{:S(2)}) collective-permute-start(bf16[144,832]{1,0:T(8,128)(2,1)} %shard_map.108.refs_0_), channel_id=1, source_target_pairs={{0,192},{64,0},{128,64},{192,128},{1,193},{65,1},{129,65},{193,129... | collective-permute-start | bytes 718856 | tf_op jit(solution)/shard_map/ppermute | solution.py:17
  225.3 8.2 %shard_map.109 = (bf16[832,1024]{1,0:T(8,128)(2,1)}, bf16[832,1024]{1,0:T(8,128)(2,1)}) custom-call(bf16[256,1664]{1,0:T(8,128)(2,1)S(1)} %copy-done.11, bf16[256,1664]{1,0:T(8,128)(2,1)S(1)} %copy-done.13, bf16[256,1664]{1,0:T(8,128)(2,1)} %collective-permute-done.18.refs_2_, bf16[256,1664]{1,0:T(8,128)(2,1)} %collective-permute-done.19.refs_3_, ...), custom_call_target="tpu_custom_call" | custom-call | flops 3489660 | bytes 8912 | tf_op jit(solution)/shard_map/pallas_call | solution.py:353
  233.6 2.6 collective-permute-done.16.refs_2_
  236.2 7.2 %collective-permute-done.15.refs_1_ = bf16[144,832]{1,0:T(8,128)(2,1)} collective-permute-done((bf16[144,832]{1,0:T(8,128)(2,1)}, bf16[144,832]{1,0:T(8,128)(2,1)}, u32[]{:S(2)}, u32[]{:S(2)}) %collective-permute-start.15) | collective-permute-done | bytes 239648 | tf_op jit(solution)/shard_map/ppermute | solution.py:17
  249.6 5.1 %all-to-all-start.5 = ((f32[8,4,2048]{2,1,0:T(4,128)}), f32[8,4,2048]{2,1,0:T(4,128)S(1)}, u32[]{:S(2)}, u32[]{:S(2)}) async-start(f32[8,4,2048]{2,1,0:T(4,128)} %reshape.44), calls=%async_computation.5 | async-start | bytes 524288 | tf_op jit(solution)/shard_map/all_to_all | solution.py:29
  256.6 10.2 %all-to-all-done.5 = f32[8,4,2048]{2,1,0:T(4,128)S(1)} async-done(((f32[8,4,2048]{2,1,0:T(4,128)}), f32[8,4,2048]{2,1,0:T(4,128)S(1)}, u32[]{:S(2)}, u32[]{:S(2)}) %all-to-all-start.5) | async-done | bytes 262176 | tf_op jit(solution)/shard_map/all_to_all | solution.py:29
  267.5 5.8 %shard_map.112 = bf16[832,1024]{1,0:T(8,128)(2,1)} custom-call(bf16[512,896]{1,0:T(8,128)(2,1)S(1)} %copy-done.2, bf16[512,896]{1,0:T(8,128)(2,1)S(1)} %copy-done.2, bf16[512,896]{1,0:T(8,128)(2,1)} %collective-permute-done.21.refs_2_.refs_3_, bf16[512,896]{1,0:T(8,128)(2,1)} %collective-permute-done.21.refs_2_.refs_3_, bf16[16,32,2048]{2,1,0:T(8,128)(2,1)S(1)} %copy-done.1, ...), custom_call_target="tpu_custom_call" | custom-call | flops 1879048 | bytes 5767 | tf_op jit(solution)/shard_map/pallas_call | solution.py:353
  (113 shorter events, 50.7 us)
Async XLA Ops:
  2.3 20.3 %all-to-all-start = ((bf16[8,8,2048]{2,1,0:T(8,128)(2,1)}), bf16[8,8,2048]{2,1,0:T(8,128)(2,1)S(1)}, u32[]{:S(2)}, u32[]{:S(2)}) async-start(bf16[8,8,2048]{2,1,0:T(8,128)(2,1)} %bitcast.4), calls=%async_computation | async-start | bytes 524288 | tf_op jit(solution)/shard_map/all_to_all | solution.py:29
  25.1 33.3 %all-to-all-start.1 = ((bf16[16,32,2048]{2,1,0:T(8,128)(2,1)}), bf16[16,32,2048]{2,1,0:T(8,128)(2,1)}, u32[]{:S(2)}, u32[]{:S(2)}) async-start(bf16[16,32,2048]{2,1,0:T(8,128)(2,1)} %broadcast_in_dim.20), calls=%async_computation.1 | async-start | bytes 4194304 | tf_op jit(solution)/shard_map/all_to_all | solution.py:29
  32.9 3.8 %collective-permute-start = (bf16[832,1024]{1,0:T(8,128)(2,1)S(1)}, bf16[832,1024]{1,0:T(8,128)(2,1)}, u32[]{:S(2)}, u32[]{:S(2)}) collective-permute-start(bf16[832,1024]{1,0:T(8,128)(2,1)S(1)} %bitcast.18), channel_id=1, source_target_pairs={{0,32},{32,0},{1,33},{33,1},{2,34},{34,2},{3,35},{35,3},{4,36},{36... | collective-permute-start | bytes 5111816 | tf_op jit(solution)/shard_map/ppermute | solution.py:17
  33.0 6.1 %collective-permute-start.1 = (bf16[832,1024]{1,0:T(8,128)(2,1)S(1)}, bf16[832,1024]{1,0:T(8,128)(2,1)}, u32[]{:S(2)}, u32[]{:S(2)}) collective-permute-start(bf16[832,1024]{1,0:T(8,128)(2,1)S(1)} %bitcast.23), channel_id=1, source_target_pairs={{0,32},{32,0},{1,33},{33,1},{2,34},{34,2},{3,35},{35,3},{4,36},{36... | collective-permute-start | bytes 5111816 | tf_op jit(solution)/shard_map/ppermute | solution.py:17
  71.1 31.6 %all-to-all-start.2 = ((bf16[16,32,2048]{2,1,0:T(8,128)(2,1)}), bf16[16,32,2048]{2,1,0:T(8,128)(2,1)S(1)}, u32[]{:S(2)}, u32[]{:S(2)}) async-start(bf16[16,32,2048]{2,1,0:T(8,128)(2,1)} %get-tuple-element.32), calls=%async_computation.2 | async-start | bytes 4194304 | tf_op jit(solution)/shard_map/all_to_all | solution.py:29
  77.4 6.2 %collective-permute-start.5 = (bf16[832,1024]{1,0:T(8,128)(2,1)}, bf16[832,1024]{1,0:T(8,128)(2,1)S(1)}, u32[]{:S(2)}, u32[]{:S(2)}) collective-permute-start(bf16[832,1024]{1,0:T(8,128)(2,1)} %refs_0_.1), channel_id=1, source_target_pairs={{0,32},{32,0},{1,33},{33,1},{2,34},{34,2},{3,35},{35,3},{4,36},{36... | collective-permute-start | bytes 5111816 | tf_op jit(solution)/shard_map/ppermute | solution.py:17
  77.4 38.1 %collective-permute-start.2 = (bf16[128,1664]{1,0:T(8,128)(2,1)}, bf16[128,1664]{1,0:T(8,128)(2,1)S(1)}, u32[]{:S(2)}, u32[]{:S(2)}) collective-permute-start(bf16[128,1664]{1,0:T(8,128)(2,1)} %copy-done.23), channel_id=1, source_target_pairs={{0,64},{64,128},{128,192},{192,0},{1,65},{65,129},{129,193},{193,1... | collective-permute-start | bytes 1277960 | tf_op jit(solution)/shard_map/ppermute | solution.py:17
  77.9 41.3 %collective-permute-start.3 = (bf16[128,1664]{1,0:T(8,128)(2,1)}, bf16[128,1664]{1,0:T(8,128)(2,1)}, u32[]{:S(2)}, u32[]{:S(2)}) collective-permute-start(bf16[128,1664]{1,0:T(8,128)(2,1)} %copy-done.22), channel_id=1, source_target_pairs={{0,128},{64,192},{128,0},{192,64},{1,129},{65,193},{129,1},{193,65... | collective-permute-start | bytes 1277960 | tf_op jit(solution)/shard_map/ppermute | solution.py:17
  81.8 45.9 %collective-permute-start.4 = (bf16[128,1664]{1,0:T(8,128)(2,1)}, bf16[128,1664]{1,0:T(8,128)(2,1)}, u32[]{:S(2)}, u32[]{:S(2)}) collective-permute-start(bf16[128,1664]{1,0:T(8,128)(2,1)} %copy-done.21), channel_id=1, source_target_pairs={{0,192},{64,0},{128,64},{192,128},{1,193},{65,1},{129,65},{193,129... | collective-permute-start | bytes 1277960 | tf_op jit(solution)/shard_map/ppermute | solution.py:17
  111.6 16.0 %collective-permute-start.6 = (bf16[128,832]{1,0:T(8,128)(2,1)S(1)}, bf16[128,832]{1,0:T(8,128)(2,1)S(1)}, u32[]{:S(2)}, u32[]{:S(2)}) collective-permute-start(bf16[128,832]{1,0:T(8,128)(2,1)S(1)} %get-tuple-element.34), channel_id=1, source_target_pairs={{0,64},{64,128},{128,192},{192,0},{1,65},{65,129},{129,193},{193,1... | collective-permute-start | bytes 638984 | tf_op jit(solution)/shard_map/ppermute | solution.py:17
  111.7 19.6 %collective-permute-start.7 = (bf16[128,832]{1,0:T(8,128)(2,1)S(1)}, bf16[128,832]{1,0:T(8,128)(2,1)S(1)}, u32[]{:S(2)}, u32[]{:S(2)}) collective-permute-start(bf16[128,832]{1,0:T(8,128)(2,1)S(1)} %get-tuple-element.35), channel_id=1, source_target_pairs={{0,128},{64,192},{128,0},{192,64},{1,129},{65,193},{129,1},{193,65... | collective-permute-start | bytes 638984 | tf_op jit(solution)/shard_map/ppermute | solution.py:17
  115.6 17.0 %collective-permute-start.8 = (bf16[128,832]{1,0:T(8,128)(2,1)S(1)}, bf16[128,832]{1,0:T(8,128)(2,1)S(1)}, u32[]{:S(2)}, u32[]{:S(2)}) collective-permute-start(bf16[128,832]{1,0:T(8,128)(2,1)S(1)} %get-tuple-element.36), channel_id=1, source_target_pairs={{0,192},{64,0},{128,64},{192,128},{1,193},{65,1},{129,65},{193,129... | collective-permute-start | bytes 638984 | tf_op jit(solution)/shard_map/ppermute | solution.py:17
  134.1 33.6 %copy-start.14 = (bf16[64,832]{1,0:T(8,128)(2,1)}, bf16[64,832]{1,0:T(8,128)(2,1)S(1)}, u32[]{:S(2)}) copy-start(bf16[64,832]{1,0:T(8,128)(2,1)S(1)} %get-tuple-element.41.a_ref) | copy-start | bytes 319492
  134.1 38.4 %copy-start.4 = (bf16[1024,832]{0,1:T(8,128)(2,1)S(1)}, bf16[1024,832]{0,1:T(8,128)(2,1)}, u32[]{:S(2)}) copy-start(bf16[1024,832]{0,1:T(8,128)(2,1)} %param.7) | copy-start | bytes 5111812
  134.1 13.5 %collective-permute-start.11 = (bf16[64,1664]{1,0:T(8,128)(2,1)S(1)}, bf16[64,1664]{1,0:T(8,128)(2,1)S(1)}, u32[]{:S(2)}, u32[]{:S(2)}) collective-permute-start(bf16[64,1664]{1,0:T(8,128)(2,1)S(1)} %get-tuple-element.37.refs_0_), channel_id=1, source_target_pairs={{0,64},{64,128},{128,192},{192,0},{1,65},{65,129},{129,193},{193,1... | collective-permute-start | bytes 638984 | tf_op jit(solution)/shard_map/ppermute | solution.py:17
  135.6 24.0 %collective-permute-start.10 = (bf16[64,1664]{1,0:T(8,128)(2,1)S(1)}, bf16[64,1664]{1,0:T(8,128)(2,1)S(1)}, u32[]{:S(2)}, u32[]{:S(2)}) collective-permute-start(bf16[64,1664]{1,0:T(8,128)(2,1)S(1)} %get-tuple-element.37.refs_0_), channel_id=1, source_target_pairs={{0,128},{64,192},{128,0},{192,64},{1,129},{65,193},{129,1},{193,65... | collective-permute-start | bytes 638984 | tf_op jit(solution)/shard_map/ppermute | solution.py:17
  144.9 20.6 %collective-permute-start.9 = (bf16[64,1664]{1,0:T(8,128)(2,1)S(1)}, bf16[64,1664]{1,0:T(8,128)(2,1)S(1)}, u32[]{:S(2)}, u32[]{:S(2)}) collective-permute-start(bf16[64,1664]{1,0:T(8,128)(2,1)S(1)} %get-tuple-element.37.refs_0_), channel_id=1, source_target_pairs={{0,192},{64,0},{128,64},{192,128},{1,193},{65,1},{129,65},{193,129... | collective-permute-start | bytes 638984 | tf_op jit(solution)/shard_map/ppermute | solution.py:17
  168.4 18.7 %collective-permute-start.14 = (bf16[64,1664]{1,0:T(8,128)(2,1)}, bf16[64,1664]{1,0:T(8,128)(2,1)}, u32[]{:S(2)}, u32[]{:S(2)}) collective-permute-start(bf16[64,1664]{1,0:T(8,128)(2,1)} %get-tuple-element.38.refs_8_.refs_0_), channel_id=1, source_target_pairs={{0,64},{64,128},{128,192},{192,0},{1,65},{65,129},{129,193},{193,1... | collective-permute-start | bytes 638984 | tf_op jit(solution)/shard_map/ppermute | solution.py:17
  168.8 18.3 %collective-permute-start.13 = (bf16[64,1664]{1,0:T(8,128)(2,1)}, bf16[64,1664]{1,0:T(8,128)(2,1)}, u32[]{:S(2)}, u32[]{:S(2)}) collective-permute-start(bf16[64,1664]{1,0:T(8,128)(2,1)} %get-tuple-element.38.refs_8_.refs_0_), channel_id=1, source_target_pairs={{0,128},{64,192},{128,0},{192,64},{1,129},{65,193},{129,1},{193,65... | collective-permute-start | bytes 638984 | tf_op jit(solution)/shard_map/ppermute | solution.py:17
  168.8 21.8 %collective-permute-start.12 = (bf16[64,1664]{1,0:T(8,128)(2,1)}, bf16[64,1664]{1,0:T(8,128)(2,1)}, u32[]{:S(2)}, u32[]{:S(2)}) collective-permute-start(bf16[64,1664]{1,0:T(8,128)(2,1)} %get-tuple-element.38.refs_8_.refs_0_), channel_id=1, source_target_pairs={{0,192},{64,0},{128,64},{192,128},{1,193},{65,1},{129,65},{193,129... | collective-permute-start | bytes 638984 | tf_op jit(solution)/shard_map/ppermute | solution.py:17
  172.5 42.1 %collective-permute-start.20 = (bf16[16,32,2048]{2,1,0:T(8,128)(2,1)}, bf16[16,32,2048]{2,1,0:T(8,128)(2,1)}, u32[]{:S(2)}, u32[]{:S(2)}) collective-permute-start(bf16[16,32,2048]{2,1,0:T(8,128)(2,1)} %all-to-all-done.1.a_ref.b_ref.refs_4_.refs_5_), channel_id=1, source_target_pairs={{0,32},{32,0},{1,33},{33,1},{2,34},{34,2},{3,35},{35,3},{4,36},{36... | collective-permute-start | bytes 6291464 | tf_op jit(solution)/shard_map/ppermute | solution.py:17
  180.0 23.1 %all-to-all-start.3 = ((bf16[16,16,2048]{2,1,0:T(8,128)(2,1)}), bf16[16,16,2048]{2,1,0:T(8,128)(2,1)}, u32[]{:S(2)}, u32[]{:S(2)}) async-start(bf16[16,16,2048]{2,1,0:T(8,128)(2,1)} %bitcast.27), calls=%async_computation.3 | async-start | bytes 2097152 | tf_op jit(solution)/shard_map/all_to_all | solution.py:29
  187.1 31.1 %collective-permute-start.18 = (bf16[256,1664]{1,0:T(8,128)(2,1)}, bf16[256,1664]{1,0:T(8,128)(2,1)}, u32[]{:S(2)}, u32[]{:S(2)}) collective-permute-start(bf16[256,1664]{1,0:T(8,128)(2,1)} %copy-done.10), channel_id=1, source_target_pairs={{0,32},{32,0},{1,33},{33,1},{2,34},{34,2},{3,35},{35,3},{4,36},{36... | collective-permute-start | bytes 2555912 | tf_op jit(solution)/shard_map/ppermute | solution.py:17
  203.1 42.7 %all-to-all-start.4 = ((bf16[16,16,2048]{2,1,0:T(8,128)(2,1)}), bf16[16,16,2048]{2,1,0:T(8,128)(2,1)}, u32[]{:S(2)}, u32[]{:S(2)}) async-start(bf16[16,16,2048]{2,1,0:T(8,128)(2,1)} %bitcast.26), calls=%async_computation.4 | async-start | bytes 2097152 | tf_op jit(solution)/shard_map/all_to_all | solution.py:29
  210.0 14.2 %collective-permute-start.19 = (bf16[256,1664]{1,0:T(8,128)(2,1)}, bf16[256,1664]{1,0:T(8,128)(2,1)}, u32[]{:S(2)}, u32[]{:S(2)}) collective-permute-start(bf16[256,1664]{1,0:T(8,128)(2,1)} %copy-done.12), channel_id=1, source_target_pairs={{0,32},{32,0},{1,33},{33,1},{2,34},{34,2},{3,35},{35,3},{4,36},{36... | collective-permute-start | bytes 2555912 | tf_op jit(solution)/shard_map/ppermute | solution.py:17
  210.0 57.5 %collective-permute-start.22 = (bf16[16,32,2048]{2,1,0:T(8,128)(2,1)S(1)}, bf16[16,32,2048]{2,1,0:T(8,128)(2,1)}, u32[]{:S(2)}, u32[]{:S(2)}) collective-permute-start(bf16[16,32,2048]{2,1,0:T(8,128)(2,1)S(1)} %copy-done.1), channel_id=1, source_target_pairs={{0,32},{32,0},{1,33},{33,1},{2,34},{34,2},{3,35},{35,3},{4,36},{36... | collective-permute-start | bytes 6291464 | tf_op jit(solution)/shard_map/ppermute | solution.py:17
  212.2 21.4 %collective-permute-start.17 = (bf16[144,832]{1,0:T(8,128)(2,1)}, bf16[144,832]{1,0:T(8,128)(2,1)S(1)}, u32[]{:S(2)}, u32[]{:S(2)}) collective-permute-start(bf16[144,832]{1,0:T(8,128)(2,1)} %shard_map.108.refs_0_), channel_id=1, source_target_pairs={{0,64},{64,128},{128,192},{192,0},{1,65},{65,129},{129,193},{193,1... | collective-permute-start | bytes 718856 | tf_op jit(solution)/shard_map/ppermute | solution.py:17
  214.6 21.6 %collective-permute-start.16 = (bf16[144,832]{1,0:T(8,128)(2,1)}, bf16[144,832]{1,0:T(8,128)(2,1)S(1)}, u32[]{:S(2)}, u32[]{:S(2)}) collective-permute-start(bf16[144,832]{1,0:T(8,128)(2,1)} %shard_map.108.refs_0_), channel_id=1, source_target_pairs={{0,128},{64,192},{128,0},{192,64},{1,129},{65,193},{129,1},{193,65... | collective-permute-start | bytes 718856 | tf_op jit(solution)/shard_map/ppermute | solution.py:17
  218.2 25.2 %collective-permute-start.15 = (bf16[144,832]{1,0:T(8,128)(2,1)}, bf16[144,832]{1,0:T(8,128)(2,1)}, u32[]{:S(2)}, u32[]{:S(2)}) collective-permute-start(bf16[144,832]{1,0:T(8,128)(2,1)} %shard_map.108.refs_0_), channel_id=1, source_target_pairs={{0,192},{64,0},{128,64},{192,128},{1,193},{65,1},{129,65},{193,129... | collective-permute-start | bytes 718856 | tf_op jit(solution)/shard_map/ppermute | solution.py:17
  249.6 17.2 %all-to-all-start.5 = ((f32[8,4,2048]{2,1,0:T(4,128)}), f32[8,4,2048]{2,1,0:T(4,128)S(1)}, u32[]{:S(2)}, u32[]{:S(2)}) async-start(f32[8,4,2048]{2,1,0:T(4,128)} %reshape.44), calls=%async_computation.5 | async-start | bytes 524288 | tf_op jit(solution)/shard_map/all_to_all | solution.py:29
  254.7 1.3 collective-permute-start.23
  254.8 12.7 %collective-permute-start.21 = (bf16[512,896]{1,0:T(8,128)(2,1)S(1)}, bf16[512,896]{1,0:T(8,128)(2,1)}, u32[]{:S(2)}, u32[]{:S(2)}) collective-permute-start(bf16[512,896]{1,0:T(8,128)(2,1)S(1)} %copy-done.2), channel_id=1, source_target_pairs={{0,32},{32,0},{1,33},{33,1},{2,34},{34,2},{3,35},{35,3},{4,36},{36... | collective-permute-start | bytes 2752520 | tf_op jit(solution)/shard_map/ppermute | solution.py:17
  (27 other events, 165.5 us)

commit v2 on v1

--- a/solution.py
+++ b/solution.py
@@ -40,9 +40,8 @@
     return lax.dot_general(left, right, (((1,), (1,)), ((), ())), preferred_element_type=F32)
 
 
-def project(zi, columns, own, other, shard=None, weight=1):
+def project(zi, columns, own, other, weight=1):
     n = len(own)
-    shards = [] if shard is None else [shard]
     peers, few, width = columns.shape
     rows = peers * few // 2
     units = own[0].shape[0]
@@ -51,10 +50,7 @@
 
     def kernel(z_ref, a_ref, b_ref, *refs):
         own_refs, other_refs = refs[:n], refs[n : 2 * n]
-        refs = refs[2 * n :]
-        if shards:
-            refs[1 + NZ][...] = jnp.broadcast_to(refs[0][...][None], refs[1 + NZ].shape)
-        out, sends, totals = refs[len(shards)], refs[len(shards) + 1 :][: NZ - 1], refs[-n:]
+        out, sends, totals = refs[2 * n], refs[2 * n + 1 : 2 * n + NZ], refs[2 * n + NZ :]
         step = pl.program_id(0)
         left = jnp.concatenate([a_ref[...].reshape(rows, tile), b_ref[...].reshape(rows, tile)], axis=0)
 
@@ -97,33 +93,30 @@
                 pl.BlockSpec((peers, few // 2, tile), lambda i, z: (0, 1, i)),
             ]
             + [pl.BlockSpec((units, tile), lambda i, z: (0, jnp.minimum(i, half - 1)))] * n
-            + [pl.BlockSpec((units, tile), lambda i, z: (0, jnp.maximum(i - half, 0)))] * n
-            + [pl.BlockSpec((few, tile), lambda i, z: (0, i))] * len(shards),
-            out_specs=[whole] * NZ
-            + [pl.BlockSpec((peers, few, tile), lambda i, z: (0, 0, i))] * len(shards),
+            + [pl.BlockSpec((units, tile), lambda i, z: (0, jnp.maximum(i - half, 0)))] * n,
+            out_specs=[whole] * NZ,
             scratch_shapes=[pltpu.VMEM((2 * rows, units), F32)] * n,
         ),
         out_shape=[jax.ShapeDtypeStruct((2 * group, n * units), F32)]
-        + [jax.ShapeDtypeStruct((2 * group, n * units), BF)] * (NZ - 1)
-        + [jax.ShapeDtypeStruct((peers, few, width), BF)] * len(shards),
+        + [jax.ShapeDtypeStruct((2 * group, n * units), BF)] * (NZ - 1),
         compiler_params=params(),
         cost_estimate=pl.CostEstimate(
             flops=weight * 4 * rows * width * units * n,
             bytes_accessed=weight * (2 * (2 * rows * width + width * units * n) + 20 * group * n * units),
             transcendentals=0,
         ),
-    )(zi, columns, columns, *own, *other, *shards)
-
-
-def activations(both, hidden_grad, bound, part, ties=()):
+    )(zi, columns, columns, *own, *other)
+
+
+def activations(both, hidden_grad, bound):
+    n = len(both)
     rows, units = hidden_grad[0].shape
-    rows = rows // 2
-    steps = 2
+    steps = 4
     tile = rows // steps
 
     def kernel(*refs):
-        b_refs, h_refs, bound_ref = refs[:NZ], refs[NZ : 2 * NZ], refs[2 * NZ]
-        acts_ref, hidden_ref, amax_ref = refs[2 * NZ + 1 + len(ties) :]
+        b_refs, h_refs, bound_ref = refs[:n], refs[n : 2 * n], refs[2 * n]
+        acts_ref, hidden_ref, amax_ref = refs[2 * n + 1 :]
         total = b_refs[0][...]
         for ref in b_refs[1:]:
             total = total + ref[...].astype(F32)
@@ -154,14 +147,11 @@
 
     wide = pl.BlockSpec((tile, 2 * units), lambda i: (i, 0))
     narrow = pl.BlockSpec((tile, units), lambda i: (i, 0))
-    wide_in = pl.BlockSpec((tile, 2 * units), lambda i: (part * steps + i, 0))
-    narrow_in = pl.BlockSpec((tile, units), lambda i: (part * steps + i, 0))
     line = pl.BlockSpec((1, units), lambda i: (0, 0))
     return pl.pallas_call(
         kernel,
         grid=(steps,),
-        in_specs=[wide_in] * NZ + [narrow_in] * NZ + [line]
-        + [pl.BlockSpec(memory_space=pl.ANY)] * len(ties),
+        in_specs=[wide] * n + [narrow] * n + [line],
         out_specs=[wide, narrow, line],
         out_shape=[
             jax.ShapeDtypeStruct((rows, 2 * units), BF),
@@ -172,27 +162,30 @@
         cost_estimate=pl.CostEstimate(
             flops=40 * rows * units, bytes_accessed=34 * rows * units, transcendentals=2 * rows * units
         ),
-    )(*both, *hidden_grad, bound, *ties)
-
-
-def input_terms(zi, pieces, own, other, ties=(), weight=1):
+    )(*both, *hidden_grad, bound)
+
+
+def input_terms(zi, pieces, own, other, peers):
     group, both = pieces[0].shape
+    group = group // 2
     units, depth = own[0].shape
     steps = 4
     tile = 2 * depth // steps
     half = steps // 2
     rows = NZ * group
+    few = 2 * rows // peers
 
     def kernel(z_ref, *refs):
         p_refs, w_refs = refs[:NZ], refs[NZ : NZ + 4]
-        out_ref, all_ref, stacked = refs[NZ + 4 + len(ties) :]
+        out_ref, all_ref, stacked = refs[NZ + 4 :]
         step = pl.program_id(0)
 
         @pl.when(step == 0)
         def _():
             for j in range(NZ):
-                start = pl.multiple_of(lax.rem(z_ref[0] + j, NZ) * group, group)
-                all_ref[pl.ds(start, group), :] = p_refs[j][...]
+                for h in range(2):
+                    start = pl.multiple_of(h * rows + lax.rem(z_ref[0] + j, NZ) * group, group)
+                    all_ref[pl.ds(start, group), :] = p_refs[j][h * group : (h + 1) * group, :]
 
         @pl.when(step < half)
         def _():
@@ -204,34 +197,54 @@
             stacked[:units, :] = w_refs[2][...]
             stacked[units:, :] = w_refs[3][...]
 
-        out_ref[...] = dot(all_ref[...], stacked[...]).astype(BF)
+        value = dot(all_ref[...], stacked[...]).astype(BF)
+        for h in range(2):
+            part = value[h * rows : (h + 1) * rows].reshape(peers, few // 2, tile)
+            out_ref[:, h * (few // 2) : (h + 1) * (few // 2), :] = part
 
     return pl.pallas_call(
         kernel,
         grid_spec=pltpu.PrefetchScalarGridSpec(
             num_scalar_prefetch=1,
             grid=(steps,),
-            in_specs=[pl.BlockSpec((group, both), lambda i, z: (0, 0))] * NZ
+            in_specs=[pl.BlockSpec((2 * group, both), lambda i, z: (0, 0))] * NZ
             + [pl.BlockSpec((units, tile), lambda i, z: (0, jnp.minimum(i, half - 1)))] * 2
-            + [pl.BlockSpec((units, tile), lambda i, z: (0, jnp.maximum(i - half, 0)))] * 2
-            + [pl.BlockSpec(memory_space=pl.ANY)] * len(ties),
+            + [pl.BlockSpec((units, tile), lambda i, z: (0, jnp.maximum(i - half, 0)))] * 2,
             out_specs=[
-                pl.BlockSpec((rows, tile), lambda i, z: (0, i)),
-                pl.BlockSpec((rows, both), lambda i, z: (0, 0)),
+                pl.BlockSpec((peers, few, tile), lambda i, z: (0, 0, i)),
+                pl.BlockSpec((2 * rows, both), lambda i, z: (0, 0)),
             ],
             scratch_shapes=[pltpu.VMEM((both, tile), BF)],
         ),
         out_shape=[
-            jax.ShapeDtypeStruct((rows, 2 * depth), BF),
-            jax.ShapeDtypeStruct((rows, both), BF),
+            jax.ShapeDtypeStruct((peers, few, 2 * depth), BF),
+            jax.ShapeDtypeStruct((2 * rows, both), BF),
         ],
         compiler_params=params(),
         cost_estimate=pl.CostEstimate(
-            flops=weight * 4 * rows * both * depth,
-            bytes_accessed=weight * (4 * rows * both + 4 * rows * depth + 4 * both * depth),
+            flops=8 * rows * both * depth,
+            bytes_accessed=8 * rows * both + 8 * rows * depth + 4 * both * depth,
             transcendentals=0,
         ),
-    )(zi, *pieces, *own, *other, *ties)
+    )(zi, *pieces, *own, *other)
+
+
+def repeated(shard, peers, ties=()):
+    rows, width = shard.shape
+    steps = 4
+
+    def kernel(s_ref, *refs):
+        refs[-1][...] = jnp.broadcast_to(s_ref[...][None], refs[-1].shape)
+
+    return pl.pallas_call(
+        kernel,
+        grid=(steps,),
+        in_specs=[pl.BlockSpec((rows, width), lambda i: (0, 0))]
+        + [pl.BlockSpec(memory_space=pl.ANY)] * len(ties),
+        out_specs=pl.BlockSpec((peers // steps, rows, width), lambda i: (i, 0, 0)),
+        out_shape=jax.ShapeDtypeStruct((peers, rows, width), shard.dtype),
+        cost_estimate=pl.CostEstimate(flops=0, bytes_accessed=2 * peers * rows * width, transcendentals=0),
+    )(shard, *ties)
 
 
 def summed(pieces, ties=()):
@@ -255,14 +268,13 @@
     )(pieces, *ties)
 
 
-def hidden_message(first, second, tops, ties=()):
-    rows, units = first.shape
-
-    def kernel(a_ref, b_ref, s_ref, t_ref, *refs):
+def hidden_message(hidden, top, ties=()):
+    rows, units = hidden.shape
+
+    def kernel(a_ref, t_ref, *refs):
         out_ref = refs[-1]
         out_ref[:rows, :] = a_ref[...]
-        out_ref[rows : 2 * rows, :] = b_ref[...]
-        rest = jnp.maximum(s_ref[...], t_ref[...])
+        rest = t_ref[...]
         addends = []
         for _ in range(3):
             addends.append(rest.astype(BF).astype(F32))
@@ -271,17 +283,19 @@
         tail = jnp.zeros((16, units), F32)
         for i, addend in enumerate(addends):
             tail = jnp.where(line == i, addend, tail)
-        out_ref[2 * rows :, :] = tail.astype(BF)
-
-    whole = pl.BlockSpec((rows, units), lambda: (0, 0))
-    one = pl.BlockSpec((1, units), lambda: (0, 0))
-    return pl.pallas_call(
-        kernel,
-        in_specs=[whole, whole, one, one] + [pl.BlockSpec(memory_space=pl.ANY)] * len(ties),
-        out_specs=pl.BlockSpec((2 * rows + 16, units), lambda: (0, 0)),
-        out_shape=jax.ShapeDtypeStruct((2 * rows + 16, units), BF),
-        cost_estimate=pl.CostEstimate(flops=0, bytes_accessed=8 * rows * units, transcendentals=0),
-    )(first, second, *tops, *ties)
+        out_ref[rows:, :] = tail.astype(BF)
+
+    return pl.pallas_call(
+        kernel,
+        in_specs=[
+            pl.BlockSpec((rows, units), lambda: (0, 0)),
+            pl.BlockSpec((1, units), lambda: (0, 0)),
+        ]
+        + [pl.BlockSpec(memory_space=pl.ANY)] * len(ties),
+        out_specs=pl.BlockSpec((rows + 16, units), lambda: (0, 0)),
+        out_shape=jax.ShapeDtypeStruct((rows + 16, units), BF),
+        cost_estimate=pl.CostEstimate(flops=0, bytes_accessed=4 * rows * units, transcendentals=0),
+    )(hidden, top, *ties)
 
 
 def hidden_by_z(zi, pieces, ties=()):
@@ -404,38 +418,34 @@
     bound = amax_history[None, :]
 
     tokens_all = exchange(jnp.broadcast_to(tokens_few[None], (peers, few, block)), ("x", "y"))
-    *both, grads_sent = project(zs, tokens_all, own, other, grads_few)
-    grads_all = exchange(grads_sent, ("x", "y"))
-    hidden_grad = project(zs, grads_all, [down_weight], [down_other], None, 8)
+    both = project(zs, tokens_all, own, other)
+    grads_all = exchange(repeated(grads_few, peers, (tokens_all,)), ("x", "y"))
+    hidden_grad = project(zs, grads_all, [down_weight], [down_other], 8)
     both, hidden_grad = sum_parts(both), sum_parts(hidden_grad)
 
-    acts_a, hidden_a, amax_a = activations(both, hidden_grad, bound, 0)
-    pieces_a = gather_parts(acts_a)
-    acts_b, hidden_b, amax_b = activations(both, hidden_grad, bound, 1, pieces_a[1:])
-    pieces_b = gather_parts(acts_b)
-    terms_a, acts_all_a = input_terms(zs, pieces_a, own, other, (acts_b,))
-    terms_b, acts_all_b = input_terms(zs, pieces_b, own, other, (), 8)
-    chunk = few // 2
-
-    sums_a = exchange(terms_a.reshape(peers, chunk, block), ("x", "y"))
-    sums_b = exchange(terms_b.reshape(peers, chunk, block), ("x", "y"))
+    acts, hidden, top = activations(both, hidden_grad, bound)
+    pieces = gather_parts(acts)
+    terms, acts_all = input_terms(zs, pieces, own, other, peers)
+
+    sums = exchange(terms, ("x", "y"))
 
     units = gate_t.shape[0]
-    message = hidden_message(hidden_a, hidden_b, (amax_a, amax_b), pieces_b[1:])
+    message = hidden_message(hidden, top, pieces[1:])
     tokens_other, grads_other = swap(tokens_all), swap(grads_all)
+    acts_other = swap(acts_all)
     grad_gate, grad_up = weight_gradients(
         [
-            (acts_all_a, 0, tokens_all, 0, 0),
-            (acts_all_b, 0, tokens_all, 1, 0),
-            (swap(acts_all_a), 0, tokens_other, 0, 1),
-            (swap(acts_all_b), 0, tokens_other, 1, 1),
+            (acts_all, 0, tokens_all, 0, 0),
+            (acts_all, 1, tokens_all, 1, 0),
+            (acts_other, 0, tokens_other, 0, 1),
+            (acts_other, 1, tokens_other, 1, 1),
         ],
         2,
         units,
         half,
     )
     hidden_all, amax = hidden_by_z(zs, gather_parts(message), (grad_gate,))
-    mine = [summed(sums_a), summed(sums_b, (hidden_all,))]
+    mine = summed(sums, (grad_gate, hidden_all))
     amax = jnp.maximum(amax, swap(amax))[0]
     hidden_other = swap(hidden_all)
     (grad_down,) = weight_gradients(
@@ -450,7 +460,7 @@
         half,
     )
 
-    back = exchange(jnp.concatenate(mine, axis=0).reshape(NZ * NL, own_rows, block), ("z", "l"))
+    back = exchange(mine.reshape(NZ * NL, own_rows, block), ("z", "l"))
     back = own_first(jnp.sum(back.reshape(NZ, NL, own_rows, block), axis=1).astype(BF))
     grad_tokens = back.transpose(1, 0, 2).reshape(own_rows, width)
     return (grad_tokens, grad_gate.T, grad_up.T, grad_down, amax)

time: 275 us -> 265 us (0.964)
  starting transfers between devices: 80.1 us -> 59.3 us
  waiting for transfers between devices: 119 us -> 138 us
  local copies, waits for them, and re-layouts: 19.6 us -> 15.4 us
    ppermute x24 -> x20, waiting for transfers between devices: 54.5 us -> 84.2 us  [shift(): return lax.ppermute(value, axis, [(i, (i + k) % n) for i in range(n)])]
    ppermute x24 -> x20, starting transfers between devices: 38.5 us -> 21.7 us  [shift(): return lax.ppermute(value, axis, [(i, (i + k) % n) for i in range(n)])]
    all_to_all x6 -> x5, waiting for transfers between devices: 64.2 us -> 53.8 us  [exchange(): return lax.all_to_all(value, axis, split_axis=0, concat_axis=0, tiled=True)]
    unnamed x58 -> x42, local copies, waits for them, and re-layouts: 14.8 us -> 10.4 us
    all_to_all x6 -> x5, starting transfers between devices: 41.6 us -> 37.7 us  [exchange(): return lax.all_to_all(value, axis, split_axis=0, concat_axis=0, tiled=True)]
    pallas_call x2 -> x1, Pallas kernels: 11.3 us -> 8.27 us  [input_terms(): pl.pallas_call(kernel, grid_spec=pltpu.PrefetchScalarGridSpec(num_scalar_...]
  transfers between devices with their start and end apart: 30 -> 25, of which waited for: 18 -> 13; matrix products, arithmetic and copies ran while one was open for 1% -> 1% of each run, Pallas kernels for 12% -> 15%
where the time goes in v2:
time: 265 us; the launch traced here: 264 us
  waiting for transfers between devices  138 us (52%)
  starting transfers between devices  59.3 us (22%)
  Pallas kernels  48.3 us (18%)
  local copies, waits for them, and re-layouts  15.4 us (6%)
    ppermute x20, waiting for transfers between devices, shift(): return lax.ppermute(value, axis, [(i, (i + k) % n) for i in range(n)])  84.2 us
    all_to_all x5, waiting for transfers between devices, exchange(): return lax.all_to_all(value, axis, split_axis=0, concat_axis=0, tiled=True)  53.8 us
    all_to_all x5, starting transfers between devices, exchange(): return lax.all_to_all(value, axis, split_axis=0, concat_axis=0, tiled=True)  37.7 us
    ppermute x20, starting transfers between devices, shift(): return lax.ppermute(value, axis, [(i, (i + k) % n) for i in range(n)])  21.7 us
    pallas_call x2, Pallas kernels, project(): pl.pallas_call(kernel, grid_spec=pltpu.PrefetchScalarGridSpec(num_scalar_...  14.1 us
    pallas_call x2, Pallas kernels, weight_gradients(): pl.pallas_call(kernel, grid=(steps,), in_specs=[left_spec(t[1]) for t in...  13.8 us
    unnamed x42, local copies, waits for them, and re-layouts  10.4 us
    pallas_call x1, Pallas kernels, input_terms(): pl.pallas_call(kernel, grid_spec=pltpu.PrefetchScalarGridSpec(num_scalar_...  8.27 us
  transfers between devices with their start and end apart: 25, of which 13 were waited for; matrix products, arithmetic and copies ran while one was open for 1% of the time, Pallas kernels for 15%

profile of v2, /device:TPU:2, one launch (start us, length us, event | category | flops | bytes accessed | tf_op | source)
XLA Modules:
  0.0 264.3 jit_solution(17980479234163550766)
XLA Ops:
  2.3 8.5 %all-to-all-start = ((bf16[8,8,2048]{2,1,0:T(8,128)(2,1)}), bf16[8,8,2048]{2,1,0:T(8,128)(2,1)S(1)}, u32[]{:S(2)}, u32[]{:S(2)}) async-start(bf16[8,8,2048]{2,1,0:T(8,128)(2,1)} %bitcast.4), calls=%async_computation | async-start | bytes 524288 | tf_op jit(solution)/shard_map/all_to_all | solution.py:29
  10.8 11.9 %all-to-all-done = bf16[8,8,2048]{2,1,0:T(8,128)(2,1)S(1)} async-done(((bf16[8,8,2048]{2,1,0:T(8,128)(2,1)}), bf16[8,8,2048]{2,1,0:T(8,128)(2,1)S(1)}, u32[]{:S(2)}, u32[]{:S(2)}) %all-to-all-start) | async-done | bytes 262176 | tf_op jit(solution)/shard_map/all_to_all | solution.py:29
  24.5 7.5 %all-to-all-start.1 = ((bf16[16,32,2048]{2,1,0:T(8,128)(2,1)}), bf16[16,32,2048]{2,1,0:T(8,128)(2,1)S(1)}, u32[]{:S(2)}, u32[]{:S(2)}) async-start(bf16[16,32,2048]{2,1,0:T(8,128)(2,1)} %broadcast_in_dim.20), calls=%async_computation.1 | async-start | bytes 4194304 | tf_op jit(solution)/shard_map/all_to_all | solution.py:29
  33.2 24.3 %all-to-all-done.1.a_ref.b_ref.refs_0_.refs_4_.refs_5_ = bf16[16,32,2048]{2,1,0:T(8,128)(2,1)S(1)} async-done(((bf16[16,32,2048]{2,1,0:T(8,128)(2,1)}), bf16[16,32,2048]{2,1,0:T(8,128)(2,1)S(1)}, u32[]{:S(2)}, u32[]{:S(2)}) %all-to-all-start.1) | async-done | bytes 2097184 | tf_op jit(solution)/shard_map/all_to_all | solution.py:29
  58.8 2.8 %shard_map.102 = bf16[16,32,2048]{2,1,0:T(8,128)(2,1)} custom-call(bf16[32,2048]{1,0:T(8,128)(2,1)} %reshape.35.s_ref, bf16[16,32,2048]{2,1,0:T(8,128)(2,1)} %copy-done), custom_call_target="tpu_custom_call" | custom-call | bytes 2097152 | tf_op jit(solution)/shard_map/pallas_call | solution.py:239
  61.5 6.3 %all-to-all-start.2 = ((bf16[16,32,2048]{2,1,0:T(8,128)(2,1)}), bf16[16,32,2048]{2,1,0:T(8,128)(2,1)S(1)}, u32[]{:S(2)}, u32[]{:S(2)}) async-start(bf16[16,32,2048]{2,1,0:T(8,128)(2,1)} %shard_map.102), calls=%async_computation.2 | async-start | bytes 4194304 | tf_op jit(solution)/shard_map/all_to_all | solution.py:29
  70.8 8.7 %shard_map.101 = (f32[128,1664]{1,0:T(8,128)S(1)}, bf16[128,1664]{1,0:T(8,128)(2,1)}, bf16[128,1664]{1,0:T(8,128)(2,1)}, bf16[128,1664]{1,0:T(8,128)(2,1)}) custom-call(s32[1]{0:T(128)} %bitcast.z_ref, bf16[16,32,2048]{2,1,0:T(8,128)(2,1)} %copy-done, bf16[16,32,2048]{2,1,0:T(8,128)(2,1)} %copy-done, bf16[832,1024]{1,0:T(8,128)(2,1)S(1)} %bitcast.17, ...), custom_call_target="tpu_custom_call" | custom-call | flops 3489660928 | bytes 11042816 | tf_op jit(solution)/shard_map/pallas_call | solution.py:86
  80.0 3.9 %collective-permute-start.3 = (bf16[128,1664]{1,0:T(8,128)(2,1)}, bf16[128,1664]{1,0:T(8,128)(2,1)}, u32[]{:S(2)}, u32[]{:S(2)}) collective-permute-start(bf16[128,1664]{1,0:T(8,128)(2,1)} %get-tuple-element.24), channel_id=1, source_target_pairs={{0,128},{64,192},{128,0},{192,64},{1,129},{65,193},{129,1},{193,65... | collective-permute-start | bytes 1277960 | tf_op jit(solution)/shard_map/ppermute | solution.py:17
  83.9 1.8 collective-permute-start.4
  85.6 7.5 %all-to-all-done.2.a_ref.b_ref.refs_4_.refs_5_ = bf16[16,32,2048]{2,1,0:T(8,128)(2,1)S(1)} async-done(((bf16[16,32,2048]{2,1,0:T(8,128)(2,1)}), bf16[16,32,2048]{2,1,0:T(8,128)(2,1)S(1)}, u32[]{:S(2)}, u32[]{:S(2)}) %all-to-all-start.2) | async-done | bytes 2097184 | tf_op jit(solution)/shard_map/all_to_all | solution.py:29
  96.0 5.4 %shard_map.103 = (f32[128,832]{1,0:T(8,128)S(1)}, bf16[128,832]{1,0:T(8,128)(2,1)S(1)}, bf16[128,832]{1,0:T(8,128)(2,1)S(1)}, bf16[128,832]{1,0:T(8,128)(2,1)S(1)}) custom-call(s32[1]{0:T(128)} %bitcast.z_ref, bf16[16,32,2048]{2,1,0:T(8,128)(2,1)} %copy-done.2, bf16[16,32,2048]{2,1,0:T(8,128)(2,1)} %copy-done.2, bf16[832,1024]{1,0:T(8,128)(2,1)S(1)} %copy-done.12, ...), custom_call_target="tpu_custom_call" | custom-call | flops 13958643712 | bytes 52559872 | tf_op jit(solution)/shard_map/pallas_call | solution.py:86
  101.4 3.8 %collective-permute-start.7 = (bf16[128,832]{1,0:T(8,128)(2,1)S(1)}, bf16[128,832]{1,0:T(8,128)(2,1)S(1)}, u32[]{:S(2)}, u32[]{:S(2)}) collective-permute-start(bf16[128,832]{1,0:T(8,128)(2,1)S(1)} %get-tuple-element.28), channel_id=1, source_target_pairs={{0,128},{64,192},{128,0},{192,64},{1,129},{65,193},{129,1},{193,65... | collective-permute-start | bytes 638984 | tf_op jit(solution)/shard_map/ppermute | solution.py:17
  105.3 4.9 %collective-permute-done.2.refs_1_ = bf16[128,1664]{1,0:T(8,128)(2,1)S(1)} collective-permute-done((bf16[128,1664]{1,0:T(8,128)(2,1)}, bf16[128,1664]{1,0:T(8,128)(2,1)S(1)}, u32[]{:S(2)}, u32[]{:S(2)}) %collective-permute-start.2) | collective-permute-done | bytes 426016 | tf_op jit(solution)/shard_map/ppermute | solution.py:17
  110.2 16.1 %collective-permute-done.3.refs_2_ = bf16[128,1664]{1,0:T(8,128)(2,1)} collective-permute-done((bf16[128,1664]{1,0:T(8,128)(2,1)}, bf16[128,1664]{1,0:T(8,128)(2,1)}, u32[]{:S(2)}, u32[]{:S(2)}) %collective-permute-start.3) | collective-permute-done | bytes 426016 | tf_op jit(solution)/shard_map/ppermute | solution.py:17
  126.4 12.5 %collective-permute-done.4.refs_3_ = bf16[128,1664]{1,0:T(8,128)(2,1)} collective-permute-done((bf16[128,1664]{1,0:T(8,128)(2,1)}, bf16[128,1664]{1,0:T(8,128)(2,1)}, u32[]{:S(2)}, u32[]{:S(2)}) %collective-permute-start.4) | collective-permute-done | bytes 426016 | tf_op jit(solution)/shard_map/ppermute | solution.py:17
  138.9 4.7 %collective-permute-done.8.refs_7_ = bf16[128,832]{1,0:T(8,128)(2,1)S(1)} collective-permute-done((bf16[128,832]{1,0:T(8,128)(2,1)S(1)}, bf16[128,832]{1,0:T(8,128)(2,1)S(1)}, u32[]{:S(2)}, u32[]{:S(2)}) %collective-permute-start.8) | collective-permute-done | bytes 213024 | tf_op jit(solution)/shard_map/ppermute | solution.py:17
  143.6 2.8 %shard_map.104 = (bf16[128,1664]{1,0:T(8,128)(2,1)S(1)}, bf16[128,832]{1,0:T(8,128)(2,1)S(1)}, f32[1,832]{1,0:T(1,128)S(1)}) custom-call(f32[128,1664]{1,0:T(8,128)S(1)} %get-tuple-element.22.refs_0_, bf16[128,1664]{1,0:T(8,128)(2,1)S(1)} %collective-permute-done.2.refs_1_, bf16[128,1664]{1,0:T(8,128)(2,1)} %collective-permute-done.3.refs_2_, ...), custom_call_target="tpu_custom_call" | custom-call | flops 4259840 | bytes 3620864 | tf_op jit(solution)/shard_map/pallas_call | solution.py:151
  148.4 3.4 %collective-permute-start.9 = (bf16[128,1664]{1,0:T(8,128)(2,1)S(1)}, bf16[128,1664]{1,0:T(8,128)(2,1)S(1)}, u32[]{:S(2)}, u32[]{:S(2)}) collective-permute-start(bf16[128,1664]{1,0:T(8,128)(2,1)S(1)} %get-tuple-element.30.refs_0_), channel_id=1, source_target_pairs={{0,192},{64,0},{128,64},{192,128},{1,193},{65,1},{129,65},{193,129... | collective-permute-start | bytes 1277960 | tf_op jit(solution)/shard_map/ppermute | solution.py:17
  151.8 26.7 %collective-permute-done.10.refs_2_.refs_1_ = bf16[128,1664]{1,0:T(8,128)(2,1)S(1)} collective-permute-done((bf16[128,1664]{1,0:T(8,128)(2,1)S(1)}, bf16[128,1664]{1,0:T(8,128)(2,1)S(1)}, u32[]{:S(2)}, u32[]{:S(2)}) %collective-permute-start.10) | collective-permute-done | bytes 426016 | tf_op jit(solution)/shard_map/ppermute | solution.py:17
  178.5 7.8 %collective-permute-done.11.refs_3_.refs_2_ = bf16[128,1664]{1,0:T(8,128)(2,1)S(1)} collective-permute-done((bf16[128,1664]{1,0:T(8,128)(2,1)S(1)}, bf16[128,1664]{1,0:T(8,128)(2,1)S(1)}, u32[]{:S(2)}, u32[]{:S(2)}) %collective-permute-start.11) | collective-permute-done | bytes 426016 | tf_op jit(solution)/shard_map/ppermute | solution.py:17
  186.4 8.3 %shard_map.105 = (bf16[16,32,2048]{2,1,0:T(8,128)(2,1)}, bf16[512,1664]{1,0:T(8,128)(2,1)S(1)}) custom-call(s32[1]{0:T(128)} %bitcast.z_ref, bf16[128,1664]{1,0:T(8,128)(2,1)S(1)} %get-tuple-element.30.refs_0_, bf16[128,1664]{1,0:T(8,128)(2,1)S(1)} %collective-permute-done.9.refs_1_.refs_0_, bf16[128,1664]{1,0:T(8,128)(2,1)S(1)} %collective-permute-done.10.refs_2_.refs_1_, ...), custom_call_target="tpu_custom_call" | custom-call | flops 3489660928 | bytes 12320768 | tf_op jit(solution)/shard_map/pallas_call | solution.py:205
  195.9 7.2 %all-to-all-start.3 = ((bf16[16,32,2048]{2,1,0:T(8,128)(2,1)}), bf16[16,32,2048]{2,1,0:T(8,128)(2,1)}, u32[]{:S(2)}, u32[]{:S(2)}) async-start(bf16[16,32,2048]{2,1,0:T(8,128)(2,1)} %get-tuple-element.31), calls=%async_computation.3 | async-start | bytes 4194304 | tf_op jit(solution)/shard_map/all_to_all | solution.py:29
  205.3 1.7 collective-permute-start.14
  207.0 2.9 %collective-permute-start.15 = (bf16[144,832]{1,0:T(8,128)(2,1)}, bf16[144,832]{1,0:T(8,128)(2,1)S(1)}, u32[]{:S(2)}, u32[]{:S(2)}) collective-permute-start(bf16[144,832]{1,0:T(8,128)(2,1)} %shard_map.107.refs_0_), channel_id=1, source_target_pairs={{0,128},{64,192},{128,0},{192,64},{1,129},{65,193},{129,1},{193,65... | collective-permute-start | bytes 718856 | tf_op jit(solution)/shard_map/ppermute | solution.py:17
  211.4 8.0 %shard_map.106 = (bf16[832,1024]{1,0:T(8,128)(2,1)}, bf16[832,1024]{1,0:T(8,128)(2,1)}) custom-call(bf16[512,1664]{1,0:T(8,128)(2,1)S(1)} %copy-done.6, bf16[512,1664]{1,0:T(8,128)(2,1)S(1)} %copy-done.6, bf16[512,1664]{1,0:T(8,128)(2,1)} %collective-permute-done.12.refs_2_.refs_3_, bf16[512,1664]{1,0:T(8,128)(2,1)} %collective-permute-done.12.refs_2_.refs_3_, ...), custom_call_target="tpu_custom_call" | custom-call | flops 3489660 | bytes 8912 | tf_op jit(solution)/shard_map/pallas_call | solution.py:367
  219.5 8.6 %collective-permute-done.14.refs_1_ = bf16[144,832]{1,0:T(8,128)(2,1)S(1)} collective-permute-done((bf16[144,832]{1,0:T(8,128)(2,1)}, bf16[144,832]{1,0:T(8,128)(2,1)S(1)}, u32[]{:S(2)}, u32[]{:S(2)}) %collective-permute-start.14) | collective-permute-done | bytes 239648 | tf_op jit(solution)/shard_map/ppermute | solution.py:17
  228.1 2.1 collective-permute-done.16.refs_3_
  230.9 2.3 shard_map.108
  233.3 2.5 shard_map.109
  237.5 8.2 %all-to-all-start.4 = ((f32[8,4,2048]{2,1,0:T(4,128)}), f32[8,4,2048]{2,1,0:T(4,128)S(1)}, u32[]{:S(2)}, u32[]{:S(2)}) async-start(f32[8,4,2048]{2,1,0:T(4,128)} %reshape.36), calls=%async_computation.4 | async-start | bytes 524288 | tf_op jit(solution)/shard_map/all_to_all | solution.py:29
  247.5 10.2 %all-to-all-done.4 = f32[8,4,2048]{2,1,0:T(4,128)S(1)} async-done(((f32[8,4,2048]{2,1,0:T(4,128)}), f32[8,4,2048]{2,1,0:T(4,128)S(1)}, u32[]{:S(2)}, u32[]{:S(2)}) %all-to-all-start.4) | async-done | bytes 262176 | tf_op jit(solution)/shard_map/all_to_all | solution.py:29
  258.5 5.8 %shard_map.110 = bf16[832,1024]{1,0:T(8,128)(2,1)} custom-call(bf16[512,896]{1,0:T(8,128)(2,1)S(1)} %copy-done.4, bf16[512,896]{1,0:T(8,128)(2,1)S(1)} %copy-done.4, bf16[512,896]{1,0:T(8,128)(2,1)} %collective-permute-done.17.refs_2_.refs_3_, bf16[512,896]{1,0:T(8,128)(2,1)} %collective-permute-done.17.refs_2_.refs_3_, bf16[16,32,2048]{2,1,0:T(8,128)(2,1)S(1)} %copy-done.3, ...), custom_call_target="tpu_custom_call" | custom-call | flops 1879048 | bytes 5767 | tf_op jit(solution)/shard_map/pallas_call | solution.py:367
  (84 shorter events, 24.2 us)
Async XLA Ops:
  2.3 20.3 %all-to-all-start = ((bf16[8,8,2048]{2,1,0:T(8,128)(2,1)}), bf16[8,8,2048]{2,1,0:T(8,128)(2,1)S(1)}, u32[]{:S(2)}, u32[]{:S(2)}) async-start(bf16[8,8,2048]{2,1,0:T(8,128)(2,1)} %bitcast.4), calls=%async_computation | async-start | bytes 524288 | tf_op jit(solution)/shard_map/all_to_all | solution.py:29
  24.5 32.9 %all-to-all-start.1 = ((bf16[16,32,2048]{2,1,0:T(8,128)(2,1)}), bf16[16,32,2048]{2,1,0:T(8,128)(2,1)S(1)}, u32[]{:S(2)}, u32[]{:S(2)}) async-start(bf16[16,32,2048]{2,1,0:T(8,128)(2,1)} %broadcast_in_dim.20), calls=%async_computation.1 | async-start | bytes 4194304 | tf_op jit(solution)/shard_map/all_to_all | solution.py:29
  32.0 35.9 %collective-permute-start = (bf16[832,1024]{1,0:T(8,128)(2,1)}, bf16[832,1024]{1,0:T(8,128)(2,1)}, u32[]{:S(2)}, u32[]{:S(2)}) collective-permute-start(bf16[832,1024]{1,0:T(8,128)(2,1)} %bitcast.16), channel_id=1, source_target_pairs={{0,32},{32,0},{1,33},{33,1},{2,34},{34,2},{3,35},{35,3},{4,36},{36... | collective-permute-start | bytes 5111816 | tf_op jit(solution)/shard_map/ppermute | solution.py:17
  32.0 35.9 %collective-permute-start.1 = (bf16[832,1024]{1,0:T(8,128)(2,1)}, bf16[832,1024]{1,0:T(8,128)(2,1)}, u32[]{:S(2)}, u32[]{:S(2)}) collective-permute-start(bf16[832,1024]{1,0:T(8,128)(2,1)} %bitcast.19), channel_id=1, source_target_pairs={{0,32},{32,0},{1,33},{33,1},{2,34},{34,2},{3,35},{35,3},{4,36},{36... | collective-permute-start | bytes 5111816 | tf_op jit(solution)/shard_map/ppermute | solution.py:17
  61.5 31.6 %all-to-all-start.2 = ((bf16[16,32,2048]{2,1,0:T(8,128)(2,1)}), bf16[16,32,2048]{2,1,0:T(8,128)(2,1)S(1)}, u32[]{:S(2)}, u32[]{:S(2)}) async-start(bf16[16,32,2048]{2,1,0:T(8,128)(2,1)} %shard_map.102), calls=%async_computation.2 | async-start | bytes 4194304 | tf_op jit(solution)/shard_map/all_to_all | solution.py:29
  67.9 17.7 %collective-permute-start.5 = (bf16[832,1024]{1,0:T(8,128)(2,1)}, bf16[832,1024]{1,0:T(8,128)(2,1)}, u32[]{:S(2)}, u32[]{:S(2)}) collective-permute-start(bf16[832,1024]{1,0:T(8,128)(2,1)} %refs_0_.1), channel_id=1, source_target_pairs={{0,32},{32,0},{1,33},{33,1},{2,34},{34,2},{3,35},{35,3},{4,36},{36... | collective-permute-start | bytes 5111816 | tf_op jit(solution)/shard_map/ppermute | solution.py:17
  79.6 30.6 %collective-permute-start.2 = (bf16[128,1664]{1,0:T(8,128)(2,1)}, bf16[128,1664]{1,0:T(8,128)(2,1)S(1)}, u32[]{:S(2)}, u32[]{:S(2)}) collective-permute-start(bf16[128,1664]{1,0:T(8,128)(2,1)} %get-tuple-element.23), channel_id=1, source_target_pairs={{0,64},{64,128},{128,192},{192,0},{1,65},{65,129},{129,193},{193,1... | collective-permute-start | bytes 1277960 | tf_op jit(solution)/shard_map/ppermute | solution.py:17
  80.0 46.4 %collective-permute-start.3 = (bf16[128,1664]{1,0:T(8,128)(2,1)}, bf16[128,1664]{1,0:T(8,128)(2,1)}, u32[]{:S(2)}, u32[]{:S(2)}) collective-permute-start(bf16[128,1664]{1,0:T(8,128)(2,1)} %get-tuple-element.24), channel_id=1, source_target_pairs={{0,128},{64,192},{128,0},{192,64},{1,129},{65,193},{129,1},{193,65... | collective-permute-start | bytes 1277960 | tf_op jit(solution)/shard_map/ppermute | solution.py:17
  83.9 55.0 %collective-permute-start.4 = (bf16[128,1664]{1,0:T(8,128)(2,1)}, bf16[128,1664]{1,0:T(8,128)(2,1)}, u32[]{:S(2)}, u32[]{:S(2)}) collective-permute-start(bf16[128,1664]{1,0:T(8,128)(2,1)} %get-tuple-element.25), channel_id=1, source_target_pairs={{0,192},{64,0},{128,64},{192,128},{1,193},{65,1},{129,65},{193,129... | collective-permute-start | bytes 1277960 | tf_op jit(solution)/shard_map/ppermute | solution.py:17
  96.0 14.2 %copy-start.19 = (f32[832]{0:T(1024)S(1)}, f32[832]{0:T(1024)}, u32[]{:S(2)}) copy-start(f32[832]{0:T(1024)} %param.11) | copy-start | bytes 9988
  96.0 90.4 %copy-start.14 = (bf16[1024,832]{0,1:T(8,128)(2,1)S(1)}, bf16[1024,832]{0,1:T(8,128)(2,1)}, u32[]{:S(2)}) copy-start(bf16[1024,832]{0,1:T(8,128)(2,1)} %param.7) | copy-start | bytes 5111812
  101.3 50.5 %copy-start.1 = (bf16[16,32,2048]{2,1,0:T(8,128)(2,1)S(1)}, bf16[16,32,2048]{2,1,0:T(8,128)(2,1)}, u32[]{:S(2)}) copy-start(bf16[16,32,2048]{2,1,0:T(8,128)(2,1)} %copy-done) | copy-start | bytes 6291460
  101.4 37.5 %collective-permute-start.6 = (bf16[128,832]{1,0:T(8,128)(2,1)S(1)}, bf16[128,832]{1,0:T(8,128)(2,1)S(1)}, u32[]{:S(2)}, u32[]{:S(2)}) collective-permute-start(bf16[128,832]{1,0:T(8,128)(2,1)S(1)} %get-tuple-element.27), channel_id=1, source_target_pairs={{0,64},{64,128},{128,192},{192,0},{1,65},{65,129},{129,193},{193,1... | collective-permute-start | bytes 638984 | tf_op jit(solution)/shard_map/ppermute | solution.py:17
  101.4 37.4 %collective-permute-start.7 = (bf16[128,832]{1,0:T(8,128)(2,1)S(1)}, bf16[128,832]{1,0:T(8,128)(2,1)S(1)}, u32[]{:S(2)}, u32[]{:S(2)}) collective-permute-start(bf16[128,832]{1,0:T(8,128)(2,1)S(1)} %get-tuple-element.28), channel_id=1, source_target_pairs={{0,128},{64,192},{128,0},{192,64},{1,129},{65,193},{129,1},{193,65... | collective-permute-start | bytes 638984 | tf_op jit(solution)/shard_map/ppermute | solution.py:17
  110.2 33.4 %collective-permute-start.8 = (bf16[128,832]{1,0:T(8,128)(2,1)S(1)}, bf16[128,832]{1,0:T(8,128)(2,1)S(1)}, u32[]{:S(2)}, u32[]{:S(2)}) collective-permute-start(bf16[128,832]{1,0:T(8,128)(2,1)S(1)} %get-tuple-element.29), channel_id=1, source_target_pairs={{0,192},{64,0},{128,64},{192,128},{1,193},{65,1},{129,65},{193,129... | collective-permute-start | bytes 638984 | tf_op jit(solution)/shard_map/ppermute | solution.py:17
  146.4 48.3 %copy-start.10 = (bf16[128,832]{1,0:T(8,128)(2,1)}, bf16[128,832]{1,0:T(8,128)(2,1)S(1)}, u32[]{:S(2)}) copy-start(bf16[128,832]{1,0:T(8,128)(2,1)S(1)} %get-tuple-element.34.a_ref) | copy-start | bytes 638980
  146.4 48.3 %copy-start.11 = (f32[1,832]{1,0:T(1,128)}, f32[1,832]{1,0:T(1,128)S(1)}, u32[]{:S(2)}) copy-start(f32[1,832]{1,0:T(1,128)S(1)} %get-tuple-element.35.t_ref) | copy-start | bytes 9988
  146.4 32.1 %collective-permute-start.10 = (bf16[128,1664]{1,0:T(8,128)(2,1)S(1)}, bf16[128,1664]{1,0:T(8,128)(2,1)S(1)}, u32[]{:S(2)}, u32[]{:S(2)}) collective-permute-start(bf16[128,1664]{1,0:T(8,128)(2,1)S(1)} %get-tuple-element.30.refs_0_), channel_id=1, source_target_pairs={{0,128},{64,192},{128,0},{192,64},{1,129},{65,193},{129,1},{193,65... | collective-permute-start | bytes 1277960 | tf_op jit(solution)/shard_map/ppermute | solution.py:17
  147.7 38.7 %collective-permute-start.11 = (bf16[128,1664]{1,0:T(8,128)(2,1)S(1)}, bf16[128,1664]{1,0:T(8,128)(2,1)S(1)}, u32[]{:S(2)}, u32[]{:S(2)}) collective-permute-start(bf16[128,1664]{1,0:T(8,128)(2,1)S(1)} %get-tuple-element.30.refs_0_), channel_id=1, source_target_pairs={{0,64},{64,128},{128,192},{192,0},{1,65},{65,129},{129,193},{193,1... | collective-permute-start | bytes 1277960 | tf_op jit(solution)/shard_map/ppermute | solution.py:17
  148.4 38.0 %collective-permute-start.9 = (bf16[128,1664]{1,0:T(8,128)(2,1)S(1)}, bf16[128,1664]{1,0:T(8,128)(2,1)S(1)}, u32[]{:S(2)}, u32[]{:S(2)}) collective-permute-start(bf16[128,1664]{1,0:T(8,128)(2,1)S(1)} %get-tuple-element.30.refs_0_), channel_id=1, source_target_pairs={{0,192},{64,0},{128,64},{192,128},{1,193},{65,1},{129,65},{193,129... | collective-permute-start | bytes 1277960 | tf_op jit(solution)/shard_map/ppermute | solution.py:17
  151.8 58.1 %collective-permute-start.13 = (bf16[16,32,2048]{2,1,0:T(8,128)(2,1)S(1)}, bf16[16,32,2048]{2,1,0:T(8,128)(2,1)}, u32[]{:S(2)}, u32[]{:S(2)}) collective-permute-start(bf16[16,32,2048]{2,1,0:T(8,128)(2,1)S(1)} %copy-done.1), channel_id=1, source_target_pairs={{0,32},{32,0},{1,33},{33,1},{2,34},{34,2},{3,35},{35,3},{4,36},{36... | collective-permute-start | bytes 6291464 | tf_op jit(solution)/shard_map/ppermute | solution.py:17
  178.5 16.1 %copy-start.7 = (bf16[128,1664]{1,0:T(8,128)(2,1)}, bf16[128,1664]{1,0:T(8,128)(2,1)S(1)}, u32[]{:S(2)}) copy-start(bf16[128,1664]{1,0:T(8,128)(2,1)S(1)} %collective-permute-done.10.refs_2_.refs_1_) | copy-start | bytes 1277956
  195.9 37.4 %all-to-all-start.3 = ((bf16[16,32,2048]{2,1,0:T(8,128)(2,1)}), bf16[16,32,2048]{2,1,0:T(8,128)(2,1)}, u32[]{:S(2)}, u32[]{:S(2)}) async-start(bf16[16,32,2048]{2,1,0:T(8,128)(2,1)} %get-tuple-element.31), calls=%async_computation.3 | async-start | bytes 4194304 | tf_op jit(solution)/shard_map/all_to_all | solution.py:29
  203.1 6.9 %collective-permute-start.12 = (bf16[512,1664]{1,0:T(8,128)(2,1)}, bf16[512,1664]{1,0:T(8,128)(2,1)}, u32[]{:S(2)}, u32[]{:S(2)}) collective-permute-start(bf16[512,1664]{1,0:T(8,128)(2,1)} %copy-done.5), channel_id=1, source_target_pairs={{0,32},{32,0},{1,33},{33,1},{2,34},{34,2},{3,35},{35,3},{4,36},{36... | collective-permute-start | bytes 5111816 | tf_op jit(solution)/shard_map/ppermute | solution.py:17
  203.1 55.4 %collective-permute-start.18 = (bf16[16,32,2048]{2,1,0:T(8,128)(2,1)}, bf16[16,32,2048]{2,1,0:T(8,128)(2,1)}, u32[]{:S(2)}, u32[]{:S(2)}) collective-permute-start(bf16[16,32,2048]{2,1,0:T(8,128)(2,1)} %copy-done.2), channel_id=1, source_target_pairs={{0,32},{32,0},{1,33},{33,1},{2,34},{34,2},{3,35},{35,3},{4,36},{36... | collective-permute-start | bytes 6291464 | tf_op jit(solution)/shard_map/ppermute | solution.py:17
  205.3 22.8 %collective-permute-start.14 = (bf16[144,832]{1,0:T(8,128)(2,1)}, bf16[144,832]{1,0:T(8,128)(2,1)S(1)}, u32[]{:S(2)}, u32[]{:S(2)}) collective-permute-start(bf16[144,832]{1,0:T(8,128)(2,1)} %shard_map.107.refs_0_), channel_id=1, source_target_pairs={{0,192},{64,0},{128,64},{192,128},{1,193},{65,1},{129,65},{193,129... | collective-permute-start | bytes 718856 | tf_op jit(solution)/shard_map/ppermute | solution.py:17
  207.0 21.0 %collective-permute-start.15 = (bf16[144,832]{1,0:T(8,128)(2,1)}, bf16[144,832]{1,0:T(8,128)(2,1)S(1)}, u32[]{:S(2)}, u32[]{:S(2)}) collective-permute-start(bf16[144,832]{1,0:T(8,128)(2,1)} %shard_map.107.refs_0_), channel_id=1, source_target_pairs={{0,128},{64,192},{128,0},{192,64},{1,129},{65,193},{129,1},{193,65... | collective-permute-start | bytes 718856 | tf_op jit(solution)/shard_map/ppermute | solution.py:17
  210.0 20.2 %collective-permute-start.16 = (bf16[144,832]{1,0:T(8,128)(2,1)}, bf16[144,832]{1,0:T(8,128)(2,1)S(1)}, u32[]{:S(2)}, u32[]{:S(2)}) collective-permute-start(bf16[144,832]{1,0:T(8,128)(2,1)} %shard_map.107.refs_0_), channel_id=1, source_target_pairs={{0,64},{64,128},{128,192},{192,0},{1,65},{65,129},{129,193},{193,1... | collective-permute-start | bytes 718856 | tf_op jit(solution)/shard_map/ppermute | solution.py:17
  233.3 25.2 %copy-start.3 = (bf16[16,32,2048]{2,1,0:T(8,128)(2,1)S(1)}, bf16[16,32,2048]{2,1,0:T(8,128)(2,1)}, u32[]{:S(2)}) copy-start(bf16[16,32,2048]{2,1,0:T(8,128)(2,1)} %copy-done.2) | copy-start | bytes 6291460
  237.5 20.2 %all-to-all-start.4 = ((f32[8,4,2048]{2,1,0:T(4,128)}), f32[8,4,2048]{2,1,0:T(4,128)S(1)}, u32[]{:S(2)}, u32[]{:S(2)}) async-start(f32[8,4,2048]{2,1,0:T(4,128)} %reshape.36), calls=%async_computation.4 | async-start | bytes 524288 | tf_op jit(solution)/shard_map/all_to_all | solution.py:29
  245.7 1.3 collective-permute-start.19
  245.8 12.7 %collective-permute-start.17 = (bf16[512,896]{1,0:T(8,128)(2,1)S(1)}, bf16[512,896]{1,0:T(8,128)(2,1)}, u32[]{:S(2)}, u32[]{:S(2)}) collective-permute-start(bf16[512,896]{1,0:T(8,128)(2,1)S(1)} %copy-done.4), channel_id=1, source_target_pairs={{0,32},{32,0},{1,33},{33,1},{2,34},{34,2},{3,35},{35,3},{4,36},{36... | collective-permute-start | bytes 2752520 | tf_op jit(solution)/shard_map/ppermute | solution.py:17
  (14 other events, 56.2 us)

commit v3 on v2

--- a/solution.py
+++ b/solution.py
@@ -29,7 +29,7 @@
     return lax.all_to_all(value, axis, split_axis=0, concat_axis=0, tiled=True)
 
 
-VMEM_BYTES = 48 * 2**20
+VMEM_BYTES = 60 * 2**20
 
 
 def params():
@@ -50,7 +50,8 @@
 
     def kernel(z_ref, a_ref, b_ref, *refs):
         own_refs, other_refs = refs[:n], refs[n : 2 * n]
-        out, sends, totals = refs[2 * n], refs[2 * n + 1 : 2 * n + NZ], refs[2 * n + NZ :]
+        out, above, below, keep_above, keep_below = refs[2 * n : 2 * n + 5]
+        totals = refs[2 * n + 5 :]
         step = pl.program_id(0)
         left = jnp.concatenate([a_ref[...].reshape(rows, tile), b_ref[...].reshape(rows, tile)], axis=0)
 
@@ -71,18 +72,24 @@
 
         @pl.when(step == steps - 1)
         def _():
-            for k in range(NZ):
-                for h in range(2):
-                    start = pl.multiple_of(h * rows + lax.rem(z_ref[0] + k, NZ) * group, group)
-                    parts = [total[pl.ds(start, group), :] for total in totals]
-                    value = jnp.concatenate(parts, axis=1) if n > 1 else parts[0]
-                    if k == 0:
-                        out[h * group : (h + 1) * group, :] = value
-                    else:
-                        sends[k - 1][h * group : (h + 1) * group, :] = value.astype(BF)
+            def rows_of(k, h):
+                start = pl.multiple_of(h * rows + lax.rem(z_ref[0] + k, NZ) * group, group)
+                parts = [total[pl.ds(start, group), :] for total in totals]
+                return jnp.concatenate(parts, axis=1) if n > 1 else parts[0]
+
+            first, second = pl.ds(0, group), pl.ds(group, group)
+            out[first, :] = rows_of(0, 0)
+            out[second, :] = rows_of(0, 1)
+            above[first, :] = rows_of(2, 0).astype(BF)
+            above[second, :] = rows_of(1, 1).astype(BF)
+            below[first, :] = rows_of(3, 0).astype(BF)
+            below[second, :] = rows_of(2, 1).astype(BF)
+            keep_above[...] = rows_of(1, 0)
+            keep_below[...] = rows_of(3, 1)
 
     half = steps // 2
     whole = pl.BlockSpec((2 * group, n * units), lambda i, z: (0, 0))
+    part = pl.BlockSpec((group, n * units), lambda i, z: (0, 0))
     return pl.pallas_call(
         kernel,
         grid_spec=pltpu.PrefetchScalarGridSpec(
@@ -94,11 +101,12 @@
             ]
             + [pl.BlockSpec((units, tile), lambda i, z: (0, jnp.minimum(i, half - 1)))] * n
             + [pl.BlockSpec((units, tile), lambda i, z: (0, jnp.maximum(i - half, 0)))] * n,
-            out_specs=[whole] * NZ,
+            out_specs=[whole] * 3 + [part] * 2,
             scratch_shapes=[pltpu.VMEM((2 * rows, units), F32)] * n,
         ),
         out_shape=[jax.ShapeDtypeStruct((2 * group, n * units), F32)]
-        + [jax.ShapeDtypeStruct((2 * group, n * units), BF)] * (NZ - 1),
+        + [jax.ShapeDtypeStruct((2 * group, n * units), BF)] * 2
+        + [jax.ShapeDtypeStruct((group, n * units), F32)] * 2,
         compiler_params=params(),
         cost_estimate=pl.CostEstimate(
             flops=weight * 4 * rows * width * units * n,
@@ -108,6 +116,25 @@
     )(zi, columns, columns, *own, *other)
 
 
+def relayed(keep_above, keep_below, from_below, from_above, ties=()):
+    rows, wide = keep_above.shape
+
+    def kernel(a_ref, b_ref, c_ref, d_ref, *refs):
+        refs[-2][...] = (a_ref[...] + c_ref[...].astype(F32)).astype(BF)
+        refs[-1][...] = (b_ref[...] + d_ref[...].astype(F32)).astype(BF)
+
+    part = pl.BlockSpec((rows, wide), lambda i: (0, 0))
+    return pl.pallas_call(
+        kernel,
+        grid=(1,),
+        in_specs=[part, part, part, pl.BlockSpec((rows, wide), lambda i: (1, 0))]
+        + [pl.BlockSpec(memory_space=pl.ANY)] * len(ties),
+        out_specs=[part, part],
+        out_shape=[jax.ShapeDtypeStruct((rows, wide), BF)] * 2,
+        cost_estimate=pl.CostEstimate(flops=2 * rows * wide, bytes_accessed=16 * rows * wide, transcendentals=0),
+    )(keep_above, keep_below, from_below, from_above, *ties)
+
+
 def activations(both, hidden_grad, bound):
     n = len(both)
     rows, units = hidden_grad[0].shape
@@ -116,45 +143,64 @@
 
     def kernel(*refs):
         b_refs, h_refs, bound_ref = refs[:n], refs[n : 2 * n], refs[2 * n]
-        acts_ref, hidden_ref, amax_ref = refs[2 * n + 1 :]
-        total = b_refs[0][...]
-        for ref in b_refs[1:]:
-            total = total + ref[...].astype(F32)
-        grad = h_refs[0][...]
-        for ref in h_refs[1:]:
-            grad = grad + ref[...].astype(F32)
-        gate, up = total[:, :units], total[:, units:]
-        limit = bound_ref[...]
-        sig = jax.nn.sigmoid(gate)
-        act = gate * sig
-        raw = act * up
-        top = jnp.max(jnp.abs(raw), axis=0, keepdims=True)
+        first_ref, second_ref, hidden_ref, amax_ref = refs[2 * n + 1 :]
         step = pl.program_id(0)
 
-        @pl.when(step == 0)
-        def _():
-            amax_ref[...] = top
-
-        @pl.when(step > 0)
-        def _():
-            amax_ref[...] = jnp.maximum(amax_ref[...], top)
-
-        squash = jnp.tanh(raw / limit)
-        masked = grad * (1.0 - squash * squash)
-        hidden_ref[...] = (limit * squash).astype(BF)
-        gate_act = masked * up * sig * (1.0 + gate * (1.0 - sig))
-        acts_ref[...] = jnp.concatenate([gate_act, masked * act], axis=1).astype(BF)
-
-    wide = pl.BlockSpec((tile, 2 * units), lambda i: (i, 0))
+        def work(early, acts_ref):
+            def added(parts):
+                mine, below, above, late_below, late_above = parts
+                came, late = (above, late_below) if early else (below, late_above)
+                return mine[...] + came[...].astype(F32) + late[...].astype(F32)
+
+            total, grad = added(b_refs), added(h_refs)
+            gate, up = total[:, :units], total[:, units:]
+            limit = bound_ref[...]
+            sig = jax.nn.sigmoid(gate)
+            act = gate * sig
+            raw = act * up
+            top = jnp.max(jnp.abs(raw), axis=0, keepdims=True)
+
+            @pl.when(step == 0)
+            def _():
+                amax_ref[...] = top
+
+            @pl.when(step > 0)
+            def _():
+                amax_ref[...] = jnp.maximum(amax_ref[...], top)
+
+            squash = jnp.tanh(raw / limit)
+            masked = grad * (1.0 - squash * squash)
+            hidden_ref[...] = (limit * squash).astype(BF)
+            gate_act = masked * up * sig * (1.0 + gate * (1.0 - sig))
+            acts_ref[...] = jnp.concatenate([gate_act, masked * act], axis=1).astype(BF)
+
+        @pl.when(step < steps // 2)
+        def _():
+            work(True, first_ref)
+
+        @pl.when(step >= steps // 2)
+        def _():
+            work(False, second_ref)
+
+    def half_specs(columns):
+        return [
+            pl.BlockSpec((tile, columns), lambda i: (jnp.minimum(i, steps // 2 - 1), 0)),
+            pl.BlockSpec((tile, columns), lambda i: (jnp.maximum(i - steps // 2, 0), 0)),
+        ]
+
+    def ring_specs(columns):
+        return [pl.BlockSpec((tile, columns), lambda i: (i, 0))] * 3 + half_specs(columns)
+
     narrow = pl.BlockSpec((tile, units), lambda i: (i, 0))
     line = pl.BlockSpec((1, units), lambda i: (0, 0))
     return pl.pallas_call(
         kernel,
         grid=(steps,),
-        in_specs=[wide] * n + [narrow] * n + [line],
-        out_specs=[wide, narrow, line],
+        in_specs=ring_specs(2 * units) + ring_specs(units) + [line],
+        out_specs=half_specs(2 * units) + [narrow, line],
         out_shape=[
-            jax.ShapeDtypeStruct((rows, 2 * units), BF),
+            jax.ShapeDtypeStruct((rows // 2, 2 * units), BF),
+            jax.ShapeDtypeStruct((rows // 2, 2 * units), BF),
             jax.ShapeDtypeStruct((rows, units), BF),
             jax.ShapeDtypeStruct((1, units), F32),
         ],
@@ -166,8 +212,8 @@
 
 
 def input_terms(zi, pieces, own, other, peers):
+    n = len(pieces)
     group, both = pieces[0].shape
-    group = group // 2
     units, depth = own[0].shape
     steps = 4
     tile = 2 * depth // steps
@@ -176,8 +222,8 @@
     few = 2 * rows // peers
 
     def kernel(z_ref, *refs):
-        p_refs, w_refs = refs[:NZ], refs[NZ : NZ + 4]
-        out_ref, all_ref, stacked = refs[NZ + 4 :]
+        p_refs, w_refs = refs[:n], refs[n : n + 4]
+        out_ref, all_ref, stacked = refs[n + 4 :]
         step = pl.program_id(0)
 
         @pl.when(step == 0)
@@ -185,7 +231,7 @@
             for j in range(NZ):
                 for h in range(2):
                     start = pl.multiple_of(h * rows + lax.rem(z_ref[0] + j, NZ) * group, group)
-                    all_ref[pl.ds(start, group), :] = p_refs[j][h * group : (h + 1) * group, :]
+                    all_ref[pl.ds(start, group), :] = p_refs[2 * j + h][...]
 
         @pl.when(step < half)
         def _():
@@ -207,7 +253,7 @@
         grid_spec=pltpu.PrefetchScalarGridSpec(
             num_scalar_prefetch=1,
             grid=(steps,),
-            in_specs=[pl.BlockSpec((2 * group, both), lambda i, z: (0, 0))] * NZ
+            in_specs=[pl.BlockSpec((group, both), lambda i, z: (0, 0))] * n
             + [pl.BlockSpec((units, tile), lambda i, z: (0, jnp.minimum(i, half - 1)))] * 2
             + [pl.BlockSpec((units, tile), lambda i, z: (0, jnp.maximum(i - half, 0)))] * 2,
             out_specs=[
@@ -247,25 +293,45 @@
     )(shard, *ties)
 
 
-def summed(pieces, ties=()):
+def summed(pieces, parts, ties=()):
     peers, rows, width = pieces.shape
     steps = 2
-    tile = width // steps
+    tile, each = width // steps, rows // parts
 
     def kernel(p_ref, *refs):
-        refs[-1][...] = jnp.sum(p_ref[...].astype(F32), axis=0)
+        value = jnp.sum(p_ref[...].astype(F32), axis=0)
+        for i in range(parts):
+            refs[-1][i] = value[i * each : (i + 1) * each]
 
     return pl.pallas_call(
         kernel,
         grid=(steps,),
         in_specs=[pl.BlockSpec((peers, rows, tile), lambda i: (0, 0, i))]
         + [pl.BlockSpec(memory_space=pl.ANY)] * len(ties),
-        out_specs=pl.BlockSpec((rows, tile), lambda i: (0, i)),
-        out_shape=jax.ShapeDtypeStruct((rows, width), F32),
+        out_specs=pl.BlockSpec((parts, each, tile), lambda i: (0, 0, i)),
+        out_shape=jax.ShapeDtypeStruct((parts, each, width), F32),
         cost_estimate=pl.CostEstimate(
             flops=peers * rows * width, bytes_accessed=2 * peers * rows * width, transcendentals=0
         ),
     )(pieces, *ties)
+
+
+def over_pairs(value, ties=()):
+    n, rows, width = value.shape
+
+    def kernel(v_ref, *refs):
+        for i in range(n // 2):
+            refs[-1][i] = (v_ref[2 * i] + v_ref[2 * i + 1]).astype(BF)
+
+    return pl.pallas_call(
+        kernel,
+        grid=(1,),
+        in_specs=[pl.BlockSpec((n, rows, width), lambda i: (0, 0, 0))]
+        + [pl.BlockSpec(memory_space=pl.ANY)] * len(ties),
+        out_specs=pl.BlockSpec((n // 2, rows, width), lambda i: (0, 0, 0)),
+        out_shape=jax.ShapeDtypeStruct((n // 2, rows, width), BF),
+        cost_estimate=pl.CostEstimate(flops=0, bytes_accessed=5 * n * rows * width, transcendentals=0),
+    )(value, *ties)
 
 
 def hidden_message(hidden, top, ties=()):
@@ -380,14 +446,25 @@
     )(*[t[0] for t in terms], *[t[2] for t in terms])
 
 
-def sum_parts(pieces):
-    got = {k: shift(pieces[k], "z", k) for k in (2, 1, 3)}
-    return [pieces[0]] + [got[k] for k in (1, 2, 3)]
+def first_step(parts):
+    return shift(parts[1], "z", 1), shift(parts[2], "z", -1)
+
+
+def ring_parts(parts, came, ties=()):
+    to_above, to_below = relayed(parts[3], parts[4], *came, ties)
+    return [parts[0], *came, shift(to_above, "z", 1), shift(to_below, "z", -1)]
 
 
 def gather_parts(share):
     got = {j: shift(share, "z", -j) for j in (2, 1, 3)}
     return [share] + [got[j] for j in (1, 2, 3)]
+
+
+def gather_halves(first, second):
+    below_first, above_second = shift(first, "z", 1), shift(second, "z", -1)
+    above_first, below_second = shift(first, "z", -1), shift(second, "z", 1)
+    far_first, far_second = shift(below_first, "z", 1), shift(above_second, "z", -1)
+    return [first, second, above_first, above_second, far_first, far_second, below_first, below_second]
 
 
 def per_device(tokens, gate_weight, up_weight, down_weight, grad_mixed, amax_history):
@@ -421,16 +498,18 @@
     both = project(zs, tokens_all, own, other)
     grads_all = exchange(repeated(grads_few, peers, (tokens_all,)), ("x", "y"))
     hidden_grad = project(zs, grads_all, [down_weight], [down_other], 8)
-    both, hidden_grad = sum_parts(both), sum_parts(hidden_grad)
-
-    acts, hidden, top = activations(both, hidden_grad, bound)
-    pieces = gather_parts(acts)
+    both_came, hidden_came = first_step(both), first_step(hidden_grad)
+    both = ring_parts(both, both_came, (hidden_grad[0],))
+    hidden_grad = ring_parts(hidden_grad, hidden_came)
+
+    acts_first, acts_second, hidden, top = activations(both, hidden_grad, bound)
+    pieces = gather_halves(acts_first, acts_second)
     terms, acts_all = input_terms(zs, pieces, own, other, peers)
 
     sums = exchange(terms, ("x", "y"))
 
     units = gate_t.shape[0]
-    message = hidden_message(hidden, top, pieces[1:])
+    message = hidden_message(hidden, top, pieces[2:])
     tokens_other, grads_other = swap(tokens_all), swap(grads_all)
     acts_other = swap(acts_all)
     grad_gate, grad_up = weight_gradients(
@@ -445,7 +524,7 @@
         half,
     )
     hidden_all, amax = hidden_by_z(zs, gather_parts(message), (grad_gate,))
-    mine = summed(sums, (grad_gate, hidden_all))
+    mine = summed(sums, NZ * NL, (grad_gate, hidden_all))
     amax = jnp.maximum(amax, swap(amax))[0]
     hidden_other = swap(hidden_all)
     (grad_down,) = weight_gradients(
@@ -460,8 +539,7 @@
         half,
     )
 
-    back = exchange(mine.reshape(NZ * NL, own_rows, block), ("z", "l"))
-    back = own_first(jnp.sum(back.reshape(NZ, NL, own_rows, block), axis=1).astype(BF))
+    back = own_first(over_pairs(exchange(mine, ("z", "l")), (grad_down,)))
     grad_tokens = back.transpose(1, 0, 2).reshape(own_rows, width)
     return (grad_tokens, grad_gate.T, grad_up.T, grad_down, amax)
 

time: 265 us -> 242 us (0.913)
  waiting for transfers between devices: 138 us -> 92.9 us
  starting transfers between devices: 59.3 us -> 70.8 us
  Pallas kernels: 48.3 us -> 59.5 us
    ppermute x20 -> x25, waiting for transfers between devices: 84.2 us -> 42 us  [shift(): return lax.ppermute(value, axis, [(i, (i + k) % n) for i in range(n)])]
    ppermute x20 -> x25, starting transfers between devices: 21.7 us -> 35 us  [shift(): return lax.ppermute(value, axis, [(i, (i + k) % n) for i in range(n)])]
    pallas_call x1 -> x4, Pallas kernels: 2.8 us -> 9.84 us  [the longest x1 4.3 us: activations(): pl.pallas_call(kernel, grid=(steps,), in_specs=ring_specs(2 * units) + ri...]
    all_to_all x5, waiting for transfers between devices: 53.8 us -> 50.9 us  [exchange(): return lax.all_to_all(value, axis, split_axis=0, concat_axis=0, tiled=True)]
    unnamed x42 -> x48, local copies, waits for them, and re-layouts: 10.4 us -> 8.56 us
  transfers between devices with their start and end apart: 25 -> 30, of which waited for: 13 -> 16; matrix products, arithmetic and copies ran while one was open for 1% -> 1% of each run, Pallas kernels for 15% -> 22%
where the time goes in v3:
time: 242 us; the launch traced here: 240 us
  waiting for transfers between devices  92.9 us (38%)
  starting transfers between devices  70.8 us (29%)
  Pallas kernels  59.5 us (25%)
  local copies, waits for them, and re-layouts  13.1 us (5%)
  other arithmetic  3.14 us (1%)
    all_to_all x5, waiting for transfers between devices, exchange(): return lax.all_to_all(value, axis, split_axis=0, concat_axis=0, tiled=True)  50.9 us
    ppermute x25, waiting for transfers between devices, shift(): return lax.ppermute(value, axis, [(i, (i + k) % n) for i in range(n)])  42 us
    all_to_all x5, starting transfers between devices, exchange(): return lax.all_to_all(value, axis, split_axis=0, concat_axis=0, tiled=True)  35.8 us
    ppermute x25, starting transfers between devices, shift(): return lax.ppermute(value, axis, [(i, (i + k) % n) for i in range(n)])  35 us
    pallas_call x2, Pallas kernels, project(): pl.pallas_call(kernel, grid_spec=pltpu.PrefetchScalarGridSpec(num_scalar_...  16.4 us
    pallas_call x2, Pallas kernels, weight_gradients(): pl.pallas_call(kernel, grid=(steps,), in_specs=[left_spec(t[1]) for t in...  15 us
    pallas_call x1, Pallas kernels, input_terms(): pl.pallas_call(kernel, grid_spec=pltpu.PrefetchScalarGridSpec(num_scalar_...  9.03 us
    unnamed x48, local copies, waits for them, and re-layouts  8.56 us
  transfers between devices with their start and end apart: 30, of which 16 were waited for; matrix products, arithmetic and copies ran while one was open for 1% of the time, Pallas kernels for 22%

profile of v3, /device:TPU:2, one launch (start us, length us, event | category | flops | bytes accessed | tf_op | source)
XLA Modules:
  0.0 240.4 jit_solution(15874943236766657700)
XLA Ops:
  2.3 8.5 %all-to-all-start = ((bf16[8,8,2048]{2,1,0:T(8,128)(2,1)}), bf16[8,8,2048]{2,1,0:T(8,128)(2,1)S(1)}, u32[]{:S(2)}, u32[]{:S(2)}) async-start(bf16[8,8,2048]{2,1,0:T(8,128)(2,1)} %bitcast.4), calls=%async_computation | async-start | bytes 524288 | tf_op jit(solution)/shard_map/all_to_all | solution.py:29
  10.8 11.9 %all-to-all-done = bf16[8,8,2048]{2,1,0:T(8,128)(2,1)S(1)} async-done(((bf16[8,8,2048]{2,1,0:T(8,128)(2,1)}), bf16[8,8,2048]{2,1,0:T(8,128)(2,1)S(1)}, u32[]{:S(2)}, u32[]{:S(2)}) %all-to-all-start) | async-done | bytes 262176 | tf_op jit(solution)/shard_map/all_to_all | solution.py:29
  24.5 7.5 %all-to-all-start.1 = ((bf16[16,32,2048]{2,1,0:T(8,128)(2,1)}), bf16[16,32,2048]{2,1,0:T(8,128)(2,1)S(1)}, u32[]{:S(2)}, u32[]{:S(2)}) async-start(bf16[16,32,2048]{2,1,0:T(8,128)(2,1)} %broadcast_in_dim.20), calls=%async_computation.1 | async-start | bytes 4194304 | tf_op jit(solution)/shard_map/all_to_all | solution.py:29
  33.2 24.3 %all-to-all-done.1.a_ref.b_ref.refs_0_.refs_4_.refs_5_ = bf16[16,32,2048]{2,1,0:T(8,128)(2,1)S(1)} async-done(((bf16[16,32,2048]{2,1,0:T(8,128)(2,1)}), bf16[16,32,2048]{2,1,0:T(8,128)(2,1)S(1)}, u32[]{:S(2)}, u32[]{:S(2)}) %all-to-all-start.1) | async-done | bytes 2097184 | tf_op jit(solution)/shard_map/all_to_all | solution.py:29
  58.8 2.8 %shard_map.102 = bf16[16,32,2048]{2,1,0:T(8,128)(2,1)} custom-call(bf16[32,2048]{1,0:T(8,128)(2,1)} %reshape.29.s_ref, bf16[16,32,2048]{2,1,0:T(8,128)(2,1)} %copy-done), custom_call_target="tpu_custom_call" | custom-call | bytes 2097152 | tf_op jit(solution)/shard_map/pallas_call | solution.py:285
  61.6 6.3 %all-to-all-start.2 = ((bf16[16,32,2048]{2,1,0:T(8,128)(2,1)}), bf16[16,32,2048]{2,1,0:T(8,128)(2,1)S(1)}, u32[]{:S(2)}, u32[]{:S(2)}) async-start(bf16[16,32,2048]{2,1,0:T(8,128)(2,1)} %shard_map.102), calls=%async_computation.2 | async-start | bytes 4194304 | tf_op jit(solution)/shard_map/all_to_all | solution.py:29
  68.0 9.8 %shard_map.101 = (f32[128,1664]{1,0:T(8,128)}, bf16[128,1664]{1,0:T(8,128)(2,1)}, bf16[128,1664]{1,0:T(8,128)(2,1)}, f32[64,1664]{1,0:T(8,128)}, f32[64,1664]{1,0:T(8,128)}) custom-call(s32[1]{0:T(128)} %bitcast.z_ref, bf16[16,32,2048]{2,1,0:T(8,128)(2,1)} %copy-done, bf16[16,32,2048]{2,1,0:T(8,128)(2,1)} %copy-done, bf16[832,1024]{1,0:T(8,128)(2,1)} %bitcast.18, ...), custom_call_target="tpu_custom_call" | custom-call | flops 3489660928 | bytes 11042816 | tf_op jit(solution)/shard_map/pallas_call | solution.py:93
  78.2 3.8 %collective-permute-start.3 = (bf16[128,1664]{1,0:T(8,128)(2,1)}, bf16[128,1664]{1,0:T(8,128)(2,1)S(1)}, u32[]{:S(2)}, u32[]{:S(2)}) collective-permute-start(bf16[128,1664]{1,0:T(8,128)(2,1)} %get-tuple-element.31), channel_id=1, source_target_pairs={{0,192},{64,0},{128,64},{192,128},{1,193},{65,1},{129,65},{193,129... | collective-permute-start | bytes 1277960 | tf_op jit(solution)/shard_map/ppermute | solution.py:17
  81.9 11.3 %all-to-all-done.2.a_ref.b_ref.refs_4_.refs_5_ = bf16[16,32,2048]{2,1,0:T(8,128)(2,1)S(1)} async-done(((bf16[16,32,2048]{2,1,0:T(8,128)(2,1)}), bf16[16,32,2048]{2,1,0:T(8,128)(2,1)S(1)}, u32[]{:S(2)}, u32[]{:S(2)}) %all-to-all-start.2) | async-done | bytes 2097184 | tf_op jit(solution)/shard_map/all_to_all | solution.py:29
  94.5 6.6 %shard_map.103 = (f32[128,832]{1,0:T(8,128)}, bf16[128,832]{1,0:T(8,128)(2,1)}, bf16[128,832]{1,0:T(8,128)(2,1)}, f32[64,832]{1,0:T(8,128)}, f32[64,832]{1,0:T(8,128)}) custom-call(s32[1]{0:T(128)} %bitcast.z_ref, bf16[16,32,2048]{2,1,0:T(8,128)(2,1)} %copy-done.2, bf16[16,32,2048]{2,1,0:T(8,128)(2,1)} %copy-done.2, bf16[832,1024]{1,0:T(8,128)(2,1)} %refs_0_.1, ...), custom_call_target="tpu_custom_call" | custom-call | flops 13958643712 | bytes 52559872 | tf_op jit(solution)/shard_map/pallas_call | solution.py:93
  101.2 4.1 %collective-permute-start.8 = (bf16[128,832]{1,0:T(8,128)(2,1)}, bf16[128,832]{1,0:T(8,128)(2,1)S(1)}, u32[]{:S(2)}, u32[]{:S(2)}) collective-permute-start(bf16[128,832]{1,0:T(8,128)(2,1)} %get-tuple-element.38), channel_id=1, source_target_pairs={{0,192},{64,0},{128,64},{192,128},{1,193},{65,1},{129,65},{193,129... | collective-permute-start | bytes 638984 | tf_op jit(solution)/shard_map/ppermute | solution.py:17
  108.3 4.1 %collective-permute-start.6 = (bf16[64,1664]{1,0:T(8,128)(2,1)}, bf16[64,1664]{1,0:T(8,128)(2,1)S(1)}, u32[]{:S(2)}, u32[]{:S(2)}) collective-permute-start(bf16[64,1664]{1,0:T(8,128)(2,1)} %get-tuple-element.36), channel_id=1, source_target_pairs={{0,192},{64,0},{128,64},{192,128},{1,193},{65,1},{129,65},{193,129... | collective-permute-start | bytes 638984 | tf_op jit(solution)/shard_map/ppermute | solution.py:17
  113.1 3.8 %collective-permute-done.8.d_ref.refs_7_ = bf16[128,832]{1,0:T(8,128)(2,1)S(1)} collective-permute-done((bf16[128,832]{1,0:T(8,128)(2,1)}, bf16[128,832]{1,0:T(8,128)(2,1)S(1)}, u32[]{:S(2)}, u32[]{:S(2)}) %collective-permute-start.8) | collective-permute-done | bytes 213024 | tf_op jit(solution)/shard_map/ppermute | solution.py:17
  119.6 4.6 %collective-permute-start.10 = (bf16[64,832]{1,0:T(8,128)(2,1)}, bf16[64,832]{1,0:T(8,128)(2,1)S(1)}, u32[]{:S(2)}, u32[]{:S(2)}) collective-permute-start(bf16[64,832]{1,0:T(8,128)(2,1)} %get-tuple-element.42), channel_id=1, source_target_pairs={{0,192},{64,0},{128,64},{192,128},{1,193},{65,1},{129,65},{193,129... | collective-permute-start | bytes 319496 | tf_op jit(solution)/shard_map/ppermute | solution.py:17
  126.9 6.8 %collective-permute-done.9.refs_8_ = bf16[64,832]{1,0:T(8,128)(2,1)S(1)} collective-permute-done((bf16[64,832]{1,0:T(8,128)(2,1)}, bf16[64,832]{1,0:T(8,128)(2,1)S(1)}, u32[]{:S(2)}, u32[]{:S(2)}) %collective-permute-start.9) | collective-permute-done | bytes 106528 | tf_op jit(solution)/shard_map/ppermute | solution.py:17
  134.3 4.3 %shard_map.106 = (bf16[64,1664]{1,0:T(8,128)(2,1)}, bf16[64,1664]{1,0:T(8,128)(2,1)}, bf16[128,832]{1,0:T(8,128)(2,1)}, f32[1,832]{1,0:T(1,128)}) custom-call(f32[128,1664]{1,0:T(8,128)} %get-tuple-element.29.refs_0_, bf16[128,1664]{1,0:T(8,128)(2,1)} %copy-done.4, bf16[128,1664]{1,0:T(8,128)(2,1)} %copy-done.5, bf16[64,1664]{1,0:T(8,128)(2,1)} %copy-done.12, ...), custom_call_target="tpu_custom_call" | custom-call | flops 4259840 | bytes 3620864 | tf_op jit(solution)/shard_map/pallas_call | solution.py:196
  138.7 4.1 %collective-permute-start.12 = (bf16[64,1664]{1,0:T(8,128)(2,1)}, bf16[64,1664]{1,0:T(8,128)(2,1)S(1)}, u32[]{:S(2)}, u32[]{:S(2)}) collective-permute-start(bf16[64,1664]{1,0:T(8,128)(2,1)} %get-tuple-element.44.refs_1_), channel_id=1, source_target_pairs={{0,192},{64,0},{128,64},{192,128},{1,193},{65,1},{129,65},{193,129... | collective-permute-start | bytes 638984 | tf_op jit(solution)/shard_map/ppermute | solution.py:17
  142.9 2.8 %collective-permute-start.16 = (bf16[64,1664]{1,0:T(8,128)(2,1)}, bf16[64,1664]{1,0:T(8,128)(2,1)S(1)}, u32[]{:S(2)}, u32[]{:S(2)}) collective-permute-start(bf16[64,1664]{1,0:T(8,128)(2,1)} %get-tuple-element.44.refs_1_), channel_id=1, source_target_pairs={{0,64},{64,128},{128,192},{192,0},{1,65},{65,129},{129,193},{193,1... | collective-permute-start | bytes 638984 | tf_op jit(solution)/shard_map/ppermute | solution.py:17
  145.8 9.8 %collective-permute-done.13.refs_6_.refs_4_ = bf16[64,1664]{1,0:T(8,128)(2,1)S(1)} collective-permute-done((bf16[64,1664]{1,0:T(8,128)(2,1)}, bf16[64,1664]{1,0:T(8,128)(2,1)S(1)}, u32[]{:S(2)}, u32[]{:S(2)}) %collective-permute-start.13) | collective-permute-done | bytes 213024 | tf_op jit(solution)/shard_map/ppermute | solution.py:17
  156.4 3.3 %collective-permute-start.15 = (bf16[64,1664]{1,0:T(8,128)(2,1)S(1)}, bf16[64,1664]{1,0:T(8,128)(2,1)S(1)}, u32[]{:S(2)}, u32[]{:S(2)}) collective-permute-start(bf16[64,1664]{1,0:T(8,128)(2,1)S(1)} %collective-permute-done.12.refs_3_.refs_1_), channel_id=1, source_target_pairs={{0,192},{64,0},{128,64},{192,128},{1,193},{65,1},{129,65},{193,129... | collective-permute-start | bytes 638984 | tf_op jit(solution)/shard_map/ppermute | solution.py:17
  160.1 3.4 %collective-permute-done.14.refs_4_.refs_2_ = bf16[64,1664]{1,0:T(8,128)(2,1)S(1)} collective-permute-done((bf16[64,1664]{1,0:T(8,128)(2,1)S(1)}, bf16[64,1664]{1,0:T(8,128)(2,1)S(1)}, u32[]{:S(2)}, u32[]{:S(2)}) %collective-permute-start.14) | collective-permute-done | bytes 213024 | tf_op jit(solution)/shard_map/ppermute | solution.py:17
  164.9 9.0 %shard_map.107 = (bf16[16,32,2048]{2,1,0:T(8,128)(2,1)}, bf16[512,1664]{1,0:T(8,128)(2,1)}) custom-call(s32[1]{0:T(128)} %bitcast.z_ref, bf16[64,1664]{1,0:T(8,128)(2,1)} %get-tuple-element.43.refs_0_, bf16[64,1664]{1,0:T(8,128)(2,1)} %get-tuple-element.44.refs_1_, bf16[64,1664]{1,0:T(8,128)(2,1)} %copy-done.16, bf16[64,1664]{1,0:T(8,128)(2,1)} %copy-done.15, ...), custom_call_target="tpu_custom_call" | custom-call | flops 3489660928 | bytes 12320768 | tf_op jit(solution)/shard_map/pallas_call | solution.py:251
  173.9 9.2 %all-to-all-start.3 = ((bf16[16,32,2048]{2,1,0:T(8,128)(2,1)}), bf16[16,32,2048]{2,1,0:T(8,128)(2,1)}, u32[]{:S(2)}, u32[]{:S(2)}) async-start(bf16[16,32,2048]{2,1,0:T(8,128)(2,1)} %get-tuple-element.45), calls=%async_computation.3 | async-start | bytes 4194304 | tf_op jit(solution)/shard_map/all_to_all | solution.py:29
  184.8 3.5 %collective-permute-start.19 = (bf16[144,832]{1,0:T(8,128)(2,1)}, bf16[144,832]{1,0:T(8,128)(2,1)S(1)}, u32[]{:S(2)}, u32[]{:S(2)}) collective-permute-start(bf16[144,832]{1,0:T(8,128)(2,1)} %shard_map.109.refs_0_), channel_id=1, source_target_pairs={{0,192},{64,0},{128,64},{192,128},{1,193},{65,1},{129,65},{193,129... | collective-permute-start | bytes 718856 | tf_op jit(solution)/shard_map/ppermute | solution.py:17
  190.7 8.8 %shard_map.108 = (bf16[832,1024]{1,0:T(8,128)(2,1)}, bf16[832,1024]{1,0:T(8,128)(2,1)}) custom-call(bf16[512,1664]{1,0:T(8,128)(2,1)} %get-tuple-element.46.refs_0_.refs_1_, bf16[512,1664]{1,0:T(8,128)(2,1)} %get-tuple-element.46.refs_0_.refs_1_, bf16[512,1664]{1,0:T(8,128)(2,1)} %collective-permute-done.17.refs_2_.refs_3_, ...), custom_call_target="tpu_custom_call" | custom-call | flops 3489660 | bytes 8912 | tf_op jit(solution)/shard_map/pallas_call | solution.py:433
  199.5 8.4 %collective-permute-done.19.refs_1_ = bf16[144,832]{1,0:T(8,128)(2,1)S(1)} collective-permute-done((bf16[144,832]{1,0:T(8,128)(2,1)}, bf16[144,832]{1,0:T(8,128)(2,1)S(1)}, u32[]{:S(2)}, u32[]{:S(2)}) %collective-permute-start.19) | collective-permute-done | bytes 239648 | tf_op jit(solution)/shard_map/ppermute | solution.py:17
  207.9 3.2 %collective-permute-done.20.refs_2_ = bf16[144,832]{1,0:T(8,128)(2,1)S(1)} collective-permute-done((bf16[144,832]{1,0:T(8,128)(2,1)}, bf16[144,832]{1,0:T(8,128)(2,1)S(1)}, u32[]{:S(2)}, u32[]{:S(2)}) %collective-permute-start.20) | collective-permute-done | bytes 239648 | tf_op jit(solution)/shard_map/ppermute | solution.py:17
  211.1 2.4 collective-permute-done.21.refs_3_
  216.5 2.4 shard_map.111
  218.9 4.3 %all-to-all-start.4 = ((f32[8,4,2048]{2,1,0:T(4,128)}), f32[8,4,2048]{2,1,0:T(4,128)S(1)}, u32[]{:S(2)}, u32[]{:S(2)}) async-start(f32[8,4,2048]{2,1,0:T(4,128)} %shard_map.111), calls=%async_computation.4 | async-start | bytes 524288 | tf_op jit(solution)/shard_map/all_to_all | solution.py:29
  226.0 6.2 %shard_map.112.refs_0_ = bf16[832,1024]{1,0:T(8,128)(2,1)} custom-call(bf16[512,896]{1,0:T(8,128)(2,1)} %get-tuple-element.50.refs_1_.refs_0_, bf16[512,896]{1,0:T(8,128)(2,1)} %get-tuple-element.50.refs_1_.refs_0_, bf16[512,896]{1,0:T(8,128)(2,1)} %copy-done.3, bf16[512,896]{1,0:T(8,128)(2,1)} %copy-done.3, bf16[16,32,2048]{2,1,0:T(8,128)(2,1)} %copy-done.2, ...), custom_call_target="tpu_custom_call" | custom-call | flops 1879048 | bytes 5767 | tf_op jit(solution)/shard_map/pallas_call | solution.py:433
  232.2 3.5 %all-to-all-done.4.v_ref = f32[8,4,2048]{2,1,0:T(4,128)S(1)} async-done(((f32[8,4,2048]{2,1,0:T(4,128)}), f32[8,4,2048]{2,1,0:T(4,128)S(1)}, u32[]{:S(2)}, u32[]{:S(2)}) %all-to-all-start.4) | async-done | bytes 262176 | tf_op jit(solution)/shard_map/all_to_all | solution.py:29
  (101 shorter events, 34.6 us)
Async XLA Ops:
  2.3 20.3 %all-to-all-start = ((bf16[8,8,2048]{2,1,0:T(8,128)(2,1)}), bf16[8,8,2048]{2,1,0:T(8,128)(2,1)S(1)}, u32[]{:S(2)}, u32[]{:S(2)}) async-start(bf16[8,8,2048]{2,1,0:T(8,128)(2,1)} %bitcast.4), calls=%async_computation | async-start | bytes 524288 | tf_op jit(solution)/shard_map/all_to_all | solution.py:29
  24.5 32.9 %all-to-all-start.1 = ((bf16[16,32,2048]{2,1,0:T(8,128)(2,1)}), bf16[16,32,2048]{2,1,0:T(8,128)(2,1)S(1)}, u32[]{:S(2)}, u32[]{:S(2)}) async-start(bf16[16,32,2048]{2,1,0:T(8,128)(2,1)} %broadcast_in_dim.20), calls=%async_computation.1 | async-start | bytes 4194304 | tf_op jit(solution)/shard_map/all_to_all | solution.py:29
  32.0 36.0 %collective-permute-start = (bf16[832,1024]{1,0:T(8,128)(2,1)}, bf16[832,1024]{1,0:T(8,128)(2,1)}, u32[]{:S(2)}, u32[]{:S(2)}) collective-permute-start(bf16[832,1024]{1,0:T(8,128)(2,1)} %bitcast.17), channel_id=1, source_target_pairs={{0,32},{32,0},{1,33},{33,1},{2,34},{34,2},{3,35},{35,3},{4,36},{36... | collective-permute-start | bytes 5111816 | tf_op jit(solution)/shard_map/ppermute | solution.py:17
  32.0 36.0 %collective-permute-start.1 = (bf16[832,1024]{1,0:T(8,128)(2,1)}, bf16[832,1024]{1,0:T(8,128)(2,1)}, u32[]{:S(2)}, u32[]{:S(2)}) collective-permute-start(bf16[832,1024]{1,0:T(8,128)(2,1)} %bitcast.20), channel_id=1, source_target_pairs={{0,32},{32,0},{1,33},{33,1},{2,34},{34,2},{3,35},{35,3},{4,36},{36... | collective-permute-start | bytes 5111816 | tf_op jit(solution)/shard_map/ppermute | solution.py:17
  61.6 31.6 %all-to-all-start.2 = ((bf16[16,32,2048]{2,1,0:T(8,128)(2,1)}), bf16[16,32,2048]{2,1,0:T(8,128)(2,1)S(1)}, u32[]{:S(2)}, u32[]{:S(2)}) async-start(bf16[16,32,2048]{2,1,0:T(8,128)(2,1)} %shard_map.102), calls=%async_computation.2 | async-start | bytes 4194304 | tf_op jit(solution)/shard_map/all_to_all | solution.py:29
  67.9 14.0 %collective-permute-start.4 = (bf16[832,1024]{1,0:T(8,128)(2,1)}, bf16[832,1024]{1,0:T(8,128)(2,1)}, u32[]{:S(2)}, u32[]{:S(2)}) collective-permute-start(bf16[832,1024]{1,0:T(8,128)(2,1)} %refs_0_.1), channel_id=1, source_target_pairs={{0,32},{32,0},{1,33},{33,1},{2,34},{34,2},{3,35},{35,3},{4,36},{36... | collective-permute-start | bytes 5111816 | tf_op jit(solution)/shard_map/ppermute | solution.py:17
  77.8 27.5 %collective-permute-start.2 = (bf16[128,1664]{1,0:T(8,128)(2,1)}, bf16[128,1664]{1,0:T(8,128)(2,1)S(1)}, u32[]{:S(2)}, u32[]{:S(2)}) collective-permute-start(bf16[128,1664]{1,0:T(8,128)(2,1)} %get-tuple-element.30), channel_id=1, source_target_pairs={{0,64},{64,128},{128,192},{192,0},{1,65},{65,129},{129,193},{193,1... | collective-permute-start | bytes 1277960 | tf_op jit(solution)/shard_map/ppermute | solution.py:17
  78.2 27.2 %collective-permute-start.3 = (bf16[128,1664]{1,0:T(8,128)(2,1)}, bf16[128,1664]{1,0:T(8,128)(2,1)S(1)}, u32[]{:S(2)}, u32[]{:S(2)}) collective-permute-start(bf16[128,1664]{1,0:T(8,128)(2,1)} %get-tuple-element.31), channel_id=1, source_target_pairs={{0,192},{64,0},{128,64},{192,128},{1,193},{65,1},{129,65},{193,129... | collective-permute-start | bytes 1277960 | tf_op jit(solution)/shard_map/ppermute | solution.py:17
  101.1 23.1 %copy-start.22 = (f32[832]{0:T(1024)S(1)}, f32[832]{0:T(1024)}, u32[]{:S(2)}) copy-start(f32[832]{0:T(1024)} %param.11) | copy-start | bytes 9988
  101.1 12.0 %collective-permute-start.7 = (bf16[128,832]{1,0:T(8,128)(2,1)}, bf16[128,832]{1,0:T(8,128)(2,1)S(1)}, u32[]{:S(2)}, u32[]{:S(2)}) collective-permute-start(bf16[128,832]{1,0:T(8,128)(2,1)} %get-tuple-element.37), channel_id=1, source_target_pairs={{0,64},{64,128},{128,192},{192,0},{1,65},{65,129},{129,193},{193,1... | collective-permute-start | bytes 638984 | tf_op jit(solution)/shard_map/ppermute | solution.py:17
  101.2 15.8 %collective-permute-start.8 = (bf16[128,832]{1,0:T(8,128)(2,1)}, bf16[128,832]{1,0:T(8,128)(2,1)S(1)}, u32[]{:S(2)}, u32[]{:S(2)}) collective-permute-start(bf16[128,832]{1,0:T(8,128)(2,1)} %get-tuple-element.38), channel_id=1, source_target_pairs={{0,192},{64,0},{128,64},{192,128},{1,193},{65,1},{129,65},{193,129... | collective-permute-start | bytes 638984 | tf_op jit(solution)/shard_map/ppermute | solution.py:17
  108.3 16.5 %collective-permute-start.5 = (bf16[64,1664]{1,0:T(8,128)(2,1)}, bf16[64,1664]{1,0:T(8,128)(2,1)S(1)}, u32[]{:S(2)}, u32[]{:S(2)}) collective-permute-start(bf16[64,1664]{1,0:T(8,128)(2,1)} %get-tuple-element.35), channel_id=1, source_target_pairs={{0,64},{64,128},{128,192},{192,0},{1,65},{65,129},{129,193},{193,1... | collective-permute-start | bytes 638984 | tf_op jit(solution)/shard_map/ppermute | solution.py:17
  108.3 16.5 %collective-permute-start.6 = (bf16[64,1664]{1,0:T(8,128)(2,1)}, bf16[64,1664]{1,0:T(8,128)(2,1)S(1)}, u32[]{:S(2)}, u32[]{:S(2)}) collective-permute-start(bf16[64,1664]{1,0:T(8,128)(2,1)} %get-tuple-element.36), channel_id=1, source_target_pairs={{0,192},{64,0},{128,64},{192,128},{1,193},{65,1},{129,65},{193,129... | collective-permute-start | bytes 638984 | tf_op jit(solution)/shard_map/ppermute | solution.py:17
  119.6 23.3 %copy-start.1 = (bf16[16,32,2048]{2,1,0:T(8,128)(2,1)S(1)}, bf16[16,32,2048]{2,1,0:T(8,128)(2,1)}, u32[]{:S(2)}) copy-start(bf16[16,32,2048]{2,1,0:T(8,128)(2,1)} %copy-done) | copy-start | bytes 6291460
  119.6 7.3 %collective-permute-start.10 = (bf16[64,832]{1,0:T(8,128)(2,1)}, bf16[64,832]{1,0:T(8,128)(2,1)S(1)}, u32[]{:S(2)}, u32[]{:S(2)}) collective-permute-start(bf16[64,832]{1,0:T(8,128)(2,1)} %get-tuple-element.42), channel_id=1, source_target_pairs={{0,192},{64,0},{128,64},{192,128},{1,193},{65,1},{129,65},{193,129... | collective-permute-start | bytes 319496 | tf_op jit(solution)/shard_map/ppermute | solution.py:17
  124.2 9.5 %collective-permute-start.9 = (bf16[64,832]{1,0:T(8,128)(2,1)}, bf16[64,832]{1,0:T(8,128)(2,1)S(1)}, u32[]{:S(2)}, u32[]{:S(2)}) collective-permute-start(bf16[64,832]{1,0:T(8,128)(2,1)} %get-tuple-element.41), channel_id=1, source_target_pairs={{0,64},{64,128},{128,192},{192,0},{1,65},{65,129},{129,193},{193,1... | collective-permute-start | bytes 319496 | tf_op jit(solution)/shard_map/ppermute | solution.py:17
  138.6 16.9 %collective-permute-start.13 = (bf16[64,1664]{1,0:T(8,128)(2,1)}, bf16[64,1664]{1,0:T(8,128)(2,1)S(1)}, u32[]{:S(2)}, u32[]{:S(2)}) collective-permute-start(bf16[64,1664]{1,0:T(8,128)(2,1)} %get-tuple-element.43.refs_0_), channel_id=1, source_target_pairs={{0,64},{64,128},{128,192},{192,0},{1,65},{65,129},{129,193},{193,1... | collective-permute-start | bytes 638984 | tf_op jit(solution)/shard_map/ppermute | solution.py:17
  138.7 17.6 %collective-permute-start.12 = (bf16[64,1664]{1,0:T(8,128)(2,1)}, bf16[64,1664]{1,0:T(8,128)(2,1)S(1)}, u32[]{:S(2)}, u32[]{:S(2)}) collective-permute-start(bf16[64,1664]{1,0:T(8,128)(2,1)} %get-tuple-element.44.refs_1_), channel_id=1, source_target_pairs={{0,192},{64,0},{128,64},{192,128},{1,193},{65,1},{129,65},{193,129... | collective-permute-start | bytes 638984 | tf_op jit(solution)/shard_map/ppermute | solution.py:17
  142.8 45.6 %collective-permute-start.18 = (bf16[16,32,2048]{2,1,0:T(8,128)(2,1)S(1)}, bf16[16,32,2048]{2,1,0:T(8,128)(2,1)}, u32[]{:S(2)}, u32[]{:S(2)}) collective-permute-start(bf16[16,32,2048]{2,1,0:T(8,128)(2,1)S(1)} %copy-done.1), channel_id=1, source_target_pairs={{0,32},{32,0},{1,33},{33,1},{2,34},{34,2},{3,35},{35,3},{4,36},{36... | collective-permute-start | bytes 6291464 | tf_op jit(solution)/shard_map/ppermute | solution.py:17
  142.8 17.0 %collective-permute-start.11 = (bf16[64,1664]{1,0:T(8,128)(2,1)}, bf16[64,1664]{1,0:T(8,128)(2,1)S(1)}, u32[]{:S(2)}, u32[]{:S(2)}) collective-permute-start(bf16[64,1664]{1,0:T(8,128)(2,1)} %get-tuple-element.43.refs_0_), channel_id=1, source_target_pairs={{0,192},{64,0},{128,64},{192,128},{1,193},{65,1},{129,65},{193,129... | collective-permute-start | bytes 638984 | tf_op jit(solution)/shard_map/ppermute | solution.py:17
  142.9 17.2 %collective-permute-start.16 = (bf16[64,1664]{1,0:T(8,128)(2,1)}, bf16[64,1664]{1,0:T(8,128)(2,1)S(1)}, u32[]{:S(2)}, u32[]{:S(2)}) collective-permute-start(bf16[64,1664]{1,0:T(8,128)(2,1)} %get-tuple-element.44.refs_1_), channel_id=1, source_target_pairs={{0,64},{64,128},{128,192},{192,0},{1,65},{65,129},{129,193},{193,1... | collective-permute-start | bytes 638984 | tf_op jit(solution)/shard_map/ppermute | solution.py:17
  155.6 8.0 %collective-permute-start.14 = (bf16[64,1664]{1,0:T(8,128)(2,1)S(1)}, bf16[64,1664]{1,0:T(8,128)(2,1)S(1)}, u32[]{:S(2)}, u32[]{:S(2)}) collective-permute-start(bf16[64,1664]{1,0:T(8,128)(2,1)S(1)} %collective-permute-done.13.refs_6_.refs_4_), channel_id=1, source_target_pairs={{0,64},{64,128},{128,192},{192,0},{1,65},{65,129},{129,193},{193,1... | collective-permute-start | bytes 638984 | tf_op jit(solution)/shard_map/ppermute | solution.py:17
  156.4 7.2 %collective-permute-start.15 = (bf16[64,1664]{1,0:T(8,128)(2,1)S(1)}, bf16[64,1664]{1,0:T(8,128)(2,1)S(1)}, u32[]{:S(2)}, u32[]{:S(2)}) collective-permute-start(bf16[64,1664]{1,0:T(8,128)(2,1)S(1)} %collective-permute-done.12.refs_3_.refs_1_), channel_id=1, source_target_pairs={{0,192},{64,0},{128,64},{192,128},{1,193},{65,1},{129,65},{193,129... | collective-permute-start | bytes 638984 | tf_op jit(solution)/shard_map/ppermute | solution.py:17
  173.9 16.8 %collective-permute-start.17 = (bf16[512,1664]{1,0:T(8,128)(2,1)}, bf16[512,1664]{1,0:T(8,128)(2,1)}, u32[]{:S(2)}, u32[]{:S(2)}) collective-permute-start(bf16[512,1664]{1,0:T(8,128)(2,1)} %get-tuple-element.46.refs_0_.refs_1_), channel_id=1, source_target_pairs={{0,32},{32,0},{1,33},{33,1},{2,34},{34,2},{3,35},{35,3},{4,36},{36... | collective-permute-start | bytes 5111816 | tf_op jit(solution)/shard_map/ppermute | solution.py:17
  173.9 42.6 %all-to-all-start.3 = ((bf16[16,32,2048]{2,1,0:T(8,128)(2,1)}), bf16[16,32,2048]{2,1,0:T(8,128)(2,1)}, u32[]{:S(2)}, u32[]{:S(2)}) async-start(bf16[16,32,2048]{2,1,0:T(8,128)(2,1)} %get-tuple-element.45), calls=%async_computation.3 | async-start | bytes 4194304 | tf_op jit(solution)/shard_map/all_to_all | solution.py:29
  183.1 41.9 %collective-permute-start.23 = (bf16[16,32,2048]{2,1,0:T(8,128)(2,1)}, bf16[16,32,2048]{2,1,0:T(8,128)(2,1)}, u32[]{:S(2)}, u32[]{:S(2)}) collective-permute-start(bf16[16,32,2048]{2,1,0:T(8,128)(2,1)} %copy-done.2), channel_id=1, source_target_pairs={{0,32},{32,0},{1,33},{33,1},{2,34},{34,2},{3,35},{35,3},{4,36},{36... | collective-permute-start | bytes 6291464 | tf_op jit(solution)/shard_map/ppermute | solution.py:17
  184.8 23.0 %collective-permute-start.19 = (bf16[144,832]{1,0:T(8,128)(2,1)}, bf16[144,832]{1,0:T(8,128)(2,1)S(1)}, u32[]{:S(2)}, u32[]{:S(2)}) collective-permute-start(bf16[144,832]{1,0:T(8,128)(2,1)} %shard_map.109.refs_0_), channel_id=1, source_target_pairs={{0,192},{64,0},{128,64},{192,128},{1,193},{65,1},{129,65},{193,129... | collective-permute-start | bytes 718856 | tf_op jit(solution)/shard_map/ppermute | solution.py:17
  188.3 22.7 %collective-permute-start.20 = (bf16[144,832]{1,0:T(8,128)(2,1)}, bf16[144,832]{1,0:T(8,128)(2,1)S(1)}, u32[]{:S(2)}, u32[]{:S(2)}) collective-permute-start(bf16[144,832]{1,0:T(8,128)(2,1)} %shard_map.109.refs_0_), channel_id=1, source_target_pairs={{0,128},{64,192},{128,0},{192,64},{1,129},{65,193},{129,1},{193,65... | collective-permute-start | bytes 718856 | tf_op jit(solution)/shard_map/ppermute | solution.py:17
  188.5 25.0 %collective-permute-start.21 = (bf16[144,832]{1,0:T(8,128)(2,1)}, bf16[144,832]{1,0:T(8,128)(2,1)S(1)}, u32[]{:S(2)}, u32[]{:S(2)}) collective-permute-start(bf16[144,832]{1,0:T(8,128)(2,1)} %shard_map.109.refs_0_), channel_id=1, source_target_pairs={{0,64},{64,128},{128,192},{192,0},{1,65},{65,129},{129,193},{193,1... | collective-permute-start | bytes 718856 | tf_op jit(solution)/shard_map/ppermute | solution.py:17
  216.5 8.6 %collective-permute-start.22 = (bf16[512,896]{1,0:T(8,128)(2,1)}, bf16[512,896]{1,0:T(8,128)(2,1)S(1)}, u32[]{:S(2)}, u32[]{:S(2)}) collective-permute-start(bf16[512,896]{1,0:T(8,128)(2,1)} %get-tuple-element.50.refs_1_.refs_0_), channel_id=1, source_target_pairs={{0,32},{32,0},{1,33},{33,1},{2,34},{34,2},{3,35},{35,3},{4,36},{36... | collective-permute-start | bytes 2752520 | tf_op jit(solution)/shard_map/ppermute | solution.py:17
  218.9 16.8 %all-to-all-start.4 = ((f32[8,4,2048]{2,1,0:T(4,128)}), f32[8,4,2048]{2,1,0:T(4,128)S(1)}, u32[]{:S(2)}, u32[]{:S(2)}) async-start(f32[8,4,2048]{2,1,0:T(4,128)} %shard_map.111), calls=%async_computation.4 | async-start | bytes 524288 | tf_op jit(solution)/shard_map/all_to_all | solution.py:29
  223.2 1.3 collective-permute-start.24
  (22 other events, 74.7 us)
